TPU v7x, 128 devices: a whole 4x4x4 slice. The times are simulated.
128 devices in a mesh: seq: 32 (over z, x, y_hi), head: 4 (over y_lo, core).
Axes of the slice: x: 4, y: 4 (y_hi: 2, y_lo: 2; y = y_hi * 2 + y_lo), z: 4, core: 2. Of those that a mesh axis runs over, the one named last changes fastest.
Arguments:
- video_query: bfloat16 [16384, 3072], P(('seq', 'head')), may hold values from -16 to 16
- audio_key: bfloat16 [16384, 3072], P(('seq', 'head')), may hold values from -16 to 16
- audio_value: bfloat16 [16384, 3072], P(('seq', 'head')), may hold values from -6 to 6
- grad_out: bfloat16 [16384, 3072], P(('seq', 'head')), may hold values from -6 to 6
- audio_time: int32 [16384], P(('seq', 'head')), may hold values from -1 to 19999, as said below
Outputs:
- attended: bfloat16 [16384, 3072], P(('seq', 'head'))
- grad_query: bfloat16 [16384, 3072], P(('seq', 'head'))
- grad_key: bfloat16 [16384, 3072], P(('seq', 'head'))
- grad_value: bfloat16 [16384, 3072], P(('seq', 'head'))
Inputs may be any that keep to these rules, and one draw needn't show every extreme that they name: `audio_time`: slots r * 512 to (r+1) * 512 - 1 belong to time range r: their live slots come first, with stamps from r * 625 to (r+1) * 625 - 1 in rising order, and the rest hold -1. Every range has at least 170 live slots, and in every draw some range has all 512 live.
All inputs are finite; a program needn't handle non-finite values.
Results may differ from a plain program's by a relative error of at most 0.0061.
Values may be sent and summed in bfloat16 or wider, within the bound.
No kernel may reach another device: no remote copies, remote signals or barrier semaphores. Data moves between devices by JAX's collectives and lax.ppermute only.
A program may use at most 192 MiB of HBM per device.

v0:
```python
import jax
import jax.numpy as jnp
from jax import lax
from jax.sharding import PartitionSpec as P

DH = 128
SHARD_MS = 625
RADIUS_MS = 1000


NEG_FILL = -1e30


def from_behind(value, axis, steps):
    count = lax.axis_size(axis)
    first, last = (max(0, -steps), min(count, count - steps))
    return lax.ppermute(value, axis, [(source, source + steps) for source in range(first, last)])


def copy_for_each(value, axis):
    peers = lax.axis_size(axis)
    return lax.all_to_all(
        jnp.broadcast_to(value[None], (peers, *value.shape)), axis, 0, 0, tiled=True
    )


def joined_along(pieces, dim):
    shape = list(pieces.shape[1:])
    shape[dim] *= pieces.shape[0]
    return jnp.moveaxis(pieces, 0, dim).reshape(shape)


def collect(value, axis, dim):
    pieces = copy_for_each(value, axis)
    return joined_along(pieces, dim)


def attend_block(query_rows, key_rows, value_rows, grad_rows, query_stamps, key_stamps):
    scaling = DH ** (-0.5)
    allowed = (key_stamps[None, :] >= 0) & (
        jnp.abs(query_stamps[:, None] - key_stamps[None, :]) <= RADIUS_MS
    )
    scores = (
        jnp.einsum("qhd,khd->hqk", query_rows, key_rows, preferred_element_type=jnp.float32)
        * scaling
    )
    scores = jnp.where(allowed[None], scores, NEG_FILL)
    row_max = jnp.max(scores, axis=2, keepdims=True)
    row_total = jnp.sum(jnp.exp(scores - row_max), axis=2, keepdims=True)
    log_total = row_max + jnp.log(row_total)
    weights = jnp.exp(scores - log_total)
    weights_low = weights.astype(jnp.bfloat16)
    attended_full = jnp.einsum(
        "hqk,khd->qhd", weights_low, value_rows, preferred_element_type=jnp.float32
    )
    row_dot = jnp.sum(grad_rows.astype(jnp.float32) * attended_full, axis=2)
    grad_weights = jnp.einsum(
        "qhd,khd->hqk", grad_rows, value_rows, preferred_element_type=jnp.float32
    )
    grad_scores = (weights * (grad_weights - row_dot.T[:, :, None])).astype(jnp.bfloat16)
    grad_query = (
        jnp.einsum("hqk,khd->qhd", grad_scores, key_rows, preferred_element_type=jnp.float32)
        * scaling
    )
    grad_key = (
        jnp.einsum("hqk,qhd->khd", grad_scores, query_rows, preferred_element_type=jnp.float32)
        * scaling
    )
    grad_value = jnp.einsum(
        "hqk,qhd->khd", weights_low, grad_rows, preferred_element_type=jnp.float32
    )
    return (attended_full, grad_query, grad_key, grad_value)


def neighbour_keys(stacked, offset):
    return from_behind(stacked, "seq", offset)


def neighbour_stamps(lifted, offset):
    return from_behind(lifted, "seq", offset)


def neighbour_grads(stacked, offset):
    return from_behind(stacked, "seq", offset)


def on_device(video_query, audio_key, audio_value, grad_out, audio_time):
    shard_index = lax.axis_index("seq")
    stamps_range = collect(audio_time, "head", 0)
    query_all, grad_all = (
        lax.all_to_all(video_query, "head", split_axis=1, concat_axis=0, tiled=True),
        lax.all_to_all(grad_out, "head", split_axis=1, concat_axis=0, tiled=True),
    )
    keys_here = lax.all_to_all(audio_key, "head", split_axis=1, concat_axis=0, tiled=True)
    values_here = lax.all_to_all(audio_value, "head", split_axis=1, concat_axis=0, tiled=True)
    stacked = jnp.stack([keys_here, values_here])
    lifted = stamps_range + 1
    lower_one = neighbour_keys(stacked, 1)
    lower_two = neighbour_keys(stacked, 2)
    upper_one = neighbour_keys(stacked, -1)
    upper_two = neighbour_keys(stacked, -2)
    stamp_lower_one = neighbour_stamps(lifted, 1)
    stamp_lower_two = neighbour_stamps(lifted, 2)
    stamp_upper_one = neighbour_stamps(lifted, -1)
    stamp_upper_two = neighbour_stamps(lifted, -2)
    window_rows = jnp.concatenate([lower_two, lower_one, stacked, upper_one, upper_two], axis=1)
    window_stamps = (
        jnp.concatenate(
            [stamp_lower_two, stamp_lower_one, lifted, stamp_upper_one, stamp_upper_two], axis=0
        )
        - 1
    )
    slot_count = stamps_range.shape[0]
    row_count = query_all.shape[0]
    local_width = query_all.shape[1]
    head_local = local_width // DH
    query_stamps = (
        shard_index * SHARD_MS + jnp.arange(row_count, dtype=jnp.int32) * SHARD_MS // row_count
    )
    block_rows = min(512, row_count)
    block_count = row_count // block_rows
    key_rows = window_rows[0].reshape(5 * slot_count, head_local, DH)
    value_rows = window_rows[1].reshape(5 * slot_count, head_local, DH)
    query_blocks = query_all.reshape(block_count, block_rows, head_local, DH)
    grad_blocks = grad_all.reshape(block_count, block_rows, head_local, DH)
    stamp_blocks = query_stamps.reshape(block_count, block_rows)

    def block_step(running, inputs):
        query_rows, grad_rows, stamps = inputs
        attended_full, grad_query, grad_key, grad_value = attend_block(
            query_rows, key_rows, value_rows, grad_rows, stamps, window_stamps
        )
        return ((running[0] + grad_key, running[1] + grad_value), (attended_full, grad_query))

    zero_sums = (
        jnp.zeros((5 * slot_count, head_local, DH), jnp.float32),
        jnp.zeros((5 * slot_count, head_local, DH), jnp.float32),
    )
    (key_sums, value_sums), (attended_blocks, query_grads) = lax.scan(
        block_step, zero_sums, (query_blocks, grad_blocks, stamp_blocks)
    )
    attended = attended_blocks.reshape(row_count, local_width).astype(jnp.bfloat16)
    grad_query = query_grads.reshape(row_count, local_width).astype(jnp.bfloat16)
    partial_value = jnp.stack([key_sums, value_sums]).reshape(2, 5, slot_count, local_width)
    pieces = [partial_value[:, position] for position in range(5)]
    summed = (
        pieces[2]
        + neighbour_grads(pieces[0], -2)
        + neighbour_grads(pieces[1], -1)
        + neighbour_grads(pieces[3], 1)
        + neighbour_grads(pieces[4], 2)
    )
    grads_low = summed.astype(jnp.bfloat16)
    attended_out, grad_query_out = (
        lax.all_to_all(attended, "head", split_axis=0, concat_axis=1, tiled=True),
        lax.all_to_all(grad_query, "head", split_axis=0, concat_axis=1, tiled=True),
    )
    grad_key_out, grad_value_out = (
        lax.all_to_all(grads_low[0], "head", split_axis=0, concat_axis=1, tiled=True),
        lax.all_to_all(grads_low[1], "head", split_axis=0, concat_axis=1, tiled=True),
    )
    return (attended_out, grad_query_out, grad_key_out, grad_value_out)


def solution(mesh):
    in_specs = (
        P(("seq", "head"), None),
        P(("seq", "head"), None),
        P(("seq", "head"), None),
        P(("seq", "head"), None),
        P(("seq", "head")),
    )
    out_specs = (
        P(("seq", "head"), None),
        P(("seq", "head"), None),
        P(("seq", "head"), None),
        P(("seq", "head"), None),
    )
    return jax.shard_map(
        on_device, mesh=mesh, in_specs=in_specs, out_specs=out_specs, check_vma=False
    )
```

profile of v0, /device:TPU:38, one launch (start us, length us, event | category | flops | bytes accessed | tf_op | source)
XLA Modules:
  0.0 598.0 jit_solution(6684319668614671124)
XLA Ops:
  0.6 1.3 broadcast_in_dim.40
  1.9 3.2 all-to-all-start.2
  5.2 2.3 copy.68
  7.5 1.4 all-to-all-done.2
  8.8 3.5 all-to-all-start
  12.3 2.3 copy.70
  14.6 9.3 %all-to-all-done = bf16[128,4,768]{0,2,1:T(8,128)(2,1)S(1)} async-done(((bf16[128,4,768]{0,2,1:T(8,128)(2,1)}), bf16[128,4,768]{0,2,1:T(8,128)(2,1)S(1)}, u32[]{:S(2)}, u32[]{:S(2)}) %all-to-all-start) | async-done | bytes 786464 | tf_op jit(solution)/shard_map/all_to_all | solution.py:94
  23.9 3.5 all-to-all-start.1
  27.5 3.7 collective-permute-start.4
  31.2 2.3 copy.72
  34.7 5.1 collective-permute-start.5
  39.8 3.1 collective-permute-start.6
  42.9 2.1 collective-permute-start.7
  45.1 1.5 copy.69
  46.6 1.6 stack.18
  49.2 3.5 all-to-all-start.3
  52.7 1.5 copy.71
  54.1 1.6 stack.19
  56.7 5.8 collective-permute-start
  62.6 4.2 collective-permute-start.1
  66.9 4.0 collective-permute-start.2
  71.0 1.9 collective-permute-start.3
  73.8 4.8 all-to-all-start.5
  78.5 2.2 fusion.3
  80.7 2.6 copy.73
  83.3 2.3 squeeze.29
  85.7 87.4 %all-to-all-done.5 = bf16[128,4,768]{0,2,1:T(8,128)(2,1)} async-done(((bf16[128,4,768]{0,2,1:T(8,128)(2,1)}), bf16[128,4,768]{0,2,1:T(8,128)(2,1)}, u32[]{:S(2)}, u32[]{:S(2)}) %all-to-all-start.5) | async-done | bytes 786464 | tf_op jit(solution)/shard_map/all_to_all | solution.py:92
  173.1 2.6 copy.79
  175.7 2.3 squeeze.30
  178.1 1.5 constant_dynamic-update-slice_fusion.7
  179.6 1.5 constant_dynamic-update-slice_fusion.6
  181.2 1.5 constant_dynamic-update-slice_fusion.3
  182.8 1.5 constant_dynamic-update-slice_fusion.2
  184.3 2.2 fusion.18
  186.4 13.2 %fusion.2 = (f32[6,512]{1,0:T(8,128)S(1)}, f32[6,2560,512]{2,1,0:T(8,128)}) fusion(pred[512,2560]{0,1:T(8,128)(4,1)S(1)} %fusion.3, bf16[2560,6,128]{0,2,1:T(8,128)(2,1)S(1)} %bitcast.103, bf16[512,6,128]{0,2,1:T(8,128)(2,1)S(1)} %copy-done.1), kind=kOutput, calls=%fused_computation.6 | convolution fusion | flops 2036855808 | bytes 37498880 | tf_op jit(solution)/shard_map/while/body/eval_jaxpr/qhd,khd->hqk/dot_general | solution.py:44
  199.6 13.8 %exponential_reduce_fusion = f32[6,512]{1,0:T(8,128)S(1)} fusion(f32[6,2560,512]{2,1,0:T(8,128)} %get-tuple-element.54, f32[6,512]{1,0:T(8,128)S(1)} %get-tuple-element.53, pred[512,2560]{0,1:T(8,128)(4,1)S(1)} %fusion.3), kind=kLoop, calls=%fused_computation.4 | loop fusion | flops 31454208 | bytes 32792576 | tf_op jit(solution)/shard_map/while/body/eval_jaxpr/reduce_sum | solution.py:49
  213.5 16.2 %bitcast_convert_fusion = (bf16[512,6,128]{0,2,1:T(8,128)(2,1)}, f32[6,128,512]{2,1,0:T(8,128)}) fusion(bf16[2560,6,128]{0,2,1:T(8,128)(2,1)} %bitcast.105, f32[6,2560,512]{2,1,0:T(8,128)} %get-tuple-element.54, f32[6,512]{1,0:T(8,128)S(1)} %log_add_fusion, pred[512,2560]{0,1:T(8,128)(4,1)S(1)} %fusion.3), kind=kOutput, calls=%fused_computation.22 | convolution fusion | flops 2045116416 | bytes 39071744 | tf_op jit(solution)/shard_map/while/body/eval_jaxpr/hqk,khd->qhd/dot_general | solution.py:53
  229.7 15.7 %convolution_bitcast_fusion = f32[2560,6,128]{2,0,1:T(8,128)} fusion(bf16[512,6,128]{0,2,1:T(8,128)(2,1)S(1)} %copy-done.3, f32[6,2560,512]{2,1,0:T(8,128)} %get-tuple-element.54, f32[6,512]{1,0:T(8,128)S(1)} %log_add_fusion, pred[512,2560]{0,1:T(8,128)(4,1)S(1)} %fusion.3), kind=kOutput, calls=%fused_computation.8 | convolution fusion | flops 2044723200 | bytes 41431040 | tf_op jit(solution)/shard_map/while/body/eval_jaxpr/hqk,qhd->khd/dot_general | solution.py:69
  245.4 1.7 fusion.9
  247.1 22.0 %fusion = bf16[6,512,2560]{1,2,0:T(8,128)(2,1)} fusion(f32[6,2560,512]{2,1,0:T(8,128)} %get-tuple-element.54, f32[6,512]{1,0:T(8,128)S(1)} %bitcast.118, f32[6,512]{1,0:T(8,128)S(1)} %log_add_fusion, pred[512,2560]{0,1:T(8,128)(4,1)S(1)} %fusion.3, bf16[2560,6,128]{0,2,1:T(8,128)(2,1)} %bitcast.106, bf16[512,6,128]{0,2,1:T(8,128)(2,1)S(1)} %copy-done.3), kind=kOutput, calls=%fused_computation.1 | convolution fusion | flops 2060451840 | bytes 53239808 | tf_op jit(solution)/shard_map/while/body/eval_jaxpr/qhd,khd->hqk/dot_general | solution.py:57
  269.1 7.8 %multiply_bitcast_fusion = f32[2560,6,128]{2,0,1:T(8,128)S(1)} fusion(bf16[6,512,2560]{1,2,0:T(8,128)(2,1)} %fusion, bf16[512,6,128]{0,2,1:T(8,128)(2,1)S(1)} %copy-done.1), kind=kOutput, calls=%fused_computation.7 | convolution fusion | flops 2015232000 | bytes 24379392 | tf_op jit(solution)/shard_map/while/body/eval_jaxpr/hqk,qhd->khd/dot_general | solution.py:66
  276.8 15.6 %copy.85 = f32[2560,6,128]{2,1,0:T(8,128)} copy(f32[2560,6,128]{2,0,1:T(8,128)S(1)} %multiply_bitcast_fusion) | data formatting | bytes 15728640 | tf_op jit(solution)/shard_map/while/body/eval_jaxpr/mul | solution.py:66
  292.5 10.9 %stack.21 = f32[1,5,512,768]{3,2,1,0:T(8,128)} reshape(f32[2560,6,128]{2,1,0:T(8,128)} %copy.85) | data formatting | bytes 15728640 | tf_op jit(solution)/shard_map/stack | solution.py:144
  303.3 7.2 %constant_dynamic-update-slice_fusion.10 = f32[2,5,512,768]{3,2,1,0:T(8,128)} fusion(f32[1,5,512,768]{3,2,1,0:T(8,128)} %stack.21), kind=kLoop, calls=%fused_computation.36 | loop fusion | bytes 15728640
  310.5 14.4 %copy.87 = f32[2560,6,128]{2,1,0:T(8,128)} copy(f32[2560,6,128]{2,0,1:T(8,128)} %convolution_bitcast_fusion) | data formatting | bytes 15728640 | tf_op jit(solution)/shard_map/while/body/eval_jaxpr/hqk,qhd->khd/transpose | solution.py:69
  324.9 10.8 %stack.22 = f32[1,5,512,768]{3,2,1,0:T(8,128)} reshape(f32[2560,6,128]{2,1,0:T(8,128)} %copy.87) | data formatting | bytes 15728640 | tf_op jit(solution)/shard_map/stack | solution.py:144
  335.7 7.2 %constant_dynamic-update-slice_fusion.9 = f32[2,5,512,768]{3,2,1,0:T(8,128)} fusion(f32[2,5,512,768]{3,2,1,0:T(8,128)} %constant_dynamic-update-slice_fusion.10, f32[1,5,512,768]{3,2,1,0:T(8,128)} %stack.22), kind=kLoop, calls=%fused_computation.35 | loop fusion | bytes 15728640 | tf_op jit(solution)/shard_map/stack | solution.py:144
  343.0 9.6 %slice_bitcast_fusion.3 = (f32[2,512,768]{2,1,0:T(8,128)}, f32[2,512,768]{2,1,0:T(8,128)}, f32[2,512,768]{2,1,0:T(8,128)}, f32[2,512,768]{2,1,0:T(8,128)}) fusion(f32[2,5,512,768]{3,2,1,0:T(8,128)} %constant_dynamic-update-slice_fusion.9), kind=kLoop, calls=%fused_computation.14 | loop fusion | bytes 25165824 | tf_op jit(solution)/shard_map/squeeze | solution.py:145
  352.6 1.9 collective-permute-start.11
  354.5 1.9 collective-permute-start.10
  356.4 6.3 %collective-permute-start.9 = (f32[2,512,768]{2,1,0:T(8,128)}, f32[2,512,768]{2,1,0:T(8,128)}, u32[]{:S(2)}, u32[]{:S(2)}) collective-permute-start(f32[2,512,768]{2,1,0:T(8,128)} %get-tuple-element.46), channel_id=1, source_target_pairs={{4,0},{8,4},{12,8},{16,12},{20,16},{24,20},{28,24},{32,28},{36,32}... | collective-permute-start | bytes 9437192 | tf_op jit(solution)/shard_map/ppermute | solution.py:17
  362.8 4.2 collective-permute-start.8
  368.1 3.7 all-to-all-start.4
  371.9 8.9 %fusion.10 = bf16[512,6,128]{0,2,1:T(8,128)(2,1)S(1)} fusion(bf16[2560,6,128]{0,2,1:T(8,128)(2,1)} %bitcast.104, bf16[6,512,2560]{1,2,0:T(8,128)(2,1)} %fusion), kind=kOutput, calls=%fused_computation.25 | convolution fusion | flops 2014052352 | bytes 20447232 | tf_op jit(solution)/shard_map/while/body/eval_jaxpr/hqk,khd->qhd/dot_general | solution.py:62
  381.9 169.7 %all-to-all-done.4 = bf16[4,128,768]{1,2,0:T(8,128)(2,1)S(1)} async-done(((bf16[4,128,768]{1,2,0:T(8,128)(2,1)}), bf16[4,128,768]{1,2,0:T(8,128)(2,1)S(1)}, u32[]{:S(2)}, u32[]{:S(2)}) %all-to-all-start.4) | async-done | bytes 786464 | tf_op jit(solution)/shard_map/all_to_all | solution.py:155
  551.7 3.6 all-to-all-start.6
  555.3 6.4 %fusion.8 = bf16[2,512,768]{2,1,0:T(8,128)(2,1)S(1)} fusion(f32[2,512,768]{2,1,0:T(8,128)} %collective-permute-done.11, f32[2,512,768]{2,1,0:T(8,128)} %collective-permute-done.10, f32[2,512,768]{2,1,0:T(8,128)} %collective-permute-done.9, f32[2,512,768]{2,1,0:T(8,128)} %collective-permute-done.8, f32[2,5,512,768]{3,2,1,0:T(8,128)} %constant_dynamic-update-slice_fusion.9), kind=kLoop, calls=%fused_computation.20 | loop fusion | flops 3932160 | bytes 17301504 | tf_op jit(solution)/shard_map/convert_element_type | solution.py:153
  562.7 4.4 all-to-all-done.6
  567.0 14.1 %all_to_all.140 = bf16[4,128,768]{2,1,0:T(8,128)(2,1)S(1)} all-to-all(bf16[4,128,768]{2,1,0:T(8,128)(2,1)S(1)} %bitcast.117), channel_id=1, replica_groups=mesh['seq'=32,'head'=4] {'head'}, dimensions={0} | all-to-all | bytes 1572864 | tf_op jit(solution)/shard_map/all_to_all | solution.py:159
  581.1 3.5 all-to-all-start.8
  584.6 1.2 copy.94
  587.3 1.2 copy.96
  588.5 7.8 %all-to-all-done.8 = bf16[4,128,768]{2,1,0:T(8,128)(2,1)S(1)} async-done(((bf16[4,128,768]{2,1,0:T(8,128)(2,1)}), bf16[4,128,768]{2,1,0:T(8,128)(2,1)S(1)}, u32[]{:S(2)}, u32[]{:S(2)}) %all-to-all-start.8) | async-done | bytes 786464 | tf_op jit(solution)/shard_map/all_to_all | solution.py:160
  596.6 1.2 copy.97
  (50 shorter events, 9.3 us)
Async XLA Ops:
  0.6 32.9 %copy-start.4 = (bf16[128,3072]{1,0:T(8,128)(2,1)S(1)}, bf16[128,3072]{1,0:T(8,128)(2,1)}, u32[]{:S(2)}) copy-start(bf16[128,3072]{1,0:T(8,128)(2,1)} %param.8) | copy-start | bytes 2359300
  1.9 6.9 %all-to-all-start.2 = ((s32[4,1,128]{2,1,0:T(1,128)}), s32[4,1,128]{2,1,0:T(1,128)S(1)}, u32[]{:S(2)}, u32[]{:S(2)}) async-start(s32[4,1,128]{2,1,0:T(1,128)} %broadcast_in_dim.40), calls=%async_computation.2 | async-start | bytes 4096 | tf_op jit(solution)/shard_map/all_to_all | solution.py:22
  8.8 15.1 %all-to-all-start = ((bf16[128,4,768]{0,2,1:T(8,128)(2,1)}), bf16[128,4,768]{0,2,1:T(8,128)(2,1)S(1)}, u32[]{:S(2)}, u32[]{:S(2)}) async-start(bf16[128,4,768]{0,2,1:T(8,128)(2,1)} %bitcast), calls=%async_computation | async-start | bytes 1572864 | tf_op jit(solution)/shard_map/all_to_all | solution.py:94
  23.9 25.2 %all-to-all-start.1 = ((bf16[128,4,768]{0,2,1:T(8,128)(2,1)}), bf16[128,4,768]{0,2,1:T(8,128)(2,1)S(1)}, u32[]{:S(2)}, u32[]{:S(2)}) async-start(bf16[128,4,768]{0,2,1:T(8,128)(2,1)} %bitcast.2), calls=%async_computation.1 | async-start | bytes 1572864 | tf_op jit(solution)/shard_map/all_to_all | solution.py:95
  27.5 17.6 %collective-permute-start.4 = (s32[512]{0:T(512)S(1)}, s32[512]{0:T(512)S(1)}, u32[]{:S(2)}, u32[]{:S(2)}) collective-permute-start(s32[512]{0:T(512)S(1)} %bitcast.119), channel_id=1, source_target_pairs={{0,8},{4,12},{8,16},{12,20},{16,24},{20,28},{24,32},{28,36},{32,40... | collective-permute-start | bytes 6152 | tf_op jit(solution)/shard_map/ppermute | solution.py:17
  34.7 27.9 %collective-permute-start.5 = (s32[512]{0:T(512)S(1)}, s32[512]{0:T(512)S(1)}, u32[]{:S(2)}, u32[]{:S(2)}) collective-permute-start(s32[512]{0:T(512)S(1)} %bitcast.120), channel_id=1, source_target_pairs={{0,4},{4,8},{8,12},{12,16},{16,20},{20,24},{24,28},{28,32},{32,36}... | collective-permute-start | bytes 6152 | tf_op jit(solution)/shard_map/ppermute | solution.py:17
  39.8 27.1 %collective-permute-start.6 = (s32[512]{0:T(512)S(1)}, s32[512]{0:T(512)S(1)}, u32[]{:S(2)}, u32[]{:S(2)}) collective-permute-start(s32[512]{0:T(512)S(1)} %bitcast.121), channel_id=1, source_target_pairs={{4,0},{8,4},{12,8},{16,12},{20,16},{24,20},{28,24},{32,28},{36,32}... | collective-permute-start | bytes 6152 | tf_op jit(solution)/shard_map/ppermute | solution.py:17
  42.9 23.9 %collective-permute-start.7 = (s32[512]{0:T(512)S(1)}, s32[512]{0:T(512)S(1)}, u32[]{:S(2)}, u32[]{:S(2)}) collective-permute-start(s32[512]{0:T(512)S(1)} %bitcast.122), channel_id=1, source_target_pairs={{8,0},{12,4},{16,8},{20,12},{24,16},{28,20},{32,24},{36,28},{40,32... | collective-permute-start | bytes 6152 | tf_op jit(solution)/shard_map/ppermute | solution.py:17
  49.2 23.7 %all-to-all-start.3 = ((bf16[128,4,768]{0,2,1:T(8,128)(2,1)}), bf16[128,4,768]{0,2,1:T(8,128)(2,1)S(1)}, u32[]{:S(2)}, u32[]{:S(2)}) async-start(bf16[128,4,768]{0,2,1:T(8,128)(2,1)} %bitcast.7), calls=%async_computation.3 | async-start | bytes 1572864 | tf_op jit(solution)/shard_map/all_to_all | solution.py:91
  56.7 121.3 %collective-permute-start = (bf16[2,512,768]{1,2,0:T(8,128)(2,1)}, bf16[2,512,768]{1,2,0:T(8,128)(2,1)}, u32[]{:S(2)}, u32[]{:S(2)}) collective-permute-start(bf16[2,512,768]{1,2,0:T(8,128)(2,1)} %constant_dynamic-update-slice_fusion), channel_id=1, source_target_pairs={{0,8},{4,12},{8,16},{12,20},{16,24},{20,28},{24,32},{28,36},{32,40... | collective-permute-start | bytes 4718600 | tf_op jit(solution)/shard_map/ppermute | solution.py:17
  62.6 117.0 %collective-permute-start.1 = (bf16[2,512,768]{1,2,0:T(8,128)(2,1)}, bf16[2,512,768]{1,2,0:T(8,128)(2,1)}, u32[]{:S(2)}, u32[]{:S(2)}) collective-permute-start(bf16[2,512,768]{1,2,0:T(8,128)(2,1)} %constant_dynamic-update-slice_fusion), channel_id=1, source_target_pairs={{0,4},{4,8},{8,12},{12,16},{16,20},{20,24},{24,28},{28,32},{32,36}... | collective-permute-start | bytes 4718600 | tf_op jit(solution)/shard_map/ppermute | solution.py:17
  66.9 114.3 %collective-permute-start.2 = (bf16[2,512,768]{1,2,0:T(8,128)(2,1)}, bf16[2,512,768]{1,2,0:T(8,128)(2,1)}, u32[]{:S(2)}, u32[]{:S(2)}) collective-permute-start(bf16[2,512,768]{1,2,0:T(8,128)(2,1)} %constant_dynamic-update-slice_fusion), channel_id=1, source_target_pairs={{4,0},{8,4},{12,8},{16,12},{20,16},{24,20},{28,24},{32,28},{36,32}... | collective-permute-start | bytes 4718600 | tf_op jit(solution)/shard_map/ppermute | solution.py:17
  71.0 111.8 %collective-permute-start.3 = (bf16[2,512,768]{1,2,0:T(8,128)(2,1)}, bf16[2,512,768]{1,2,0:T(8,128)(2,1)}, u32[]{:S(2)}, u32[]{:S(2)}) collective-permute-start(bf16[2,512,768]{1,2,0:T(8,128)(2,1)} %constant_dynamic-update-slice_fusion), channel_id=1, source_target_pairs={{8,0},{12,4},{16,8},{20,12},{24,16},{28,20},{32,24},{36,28},{40,32... | collective-permute-start | bytes 4718600 | tf_op jit(solution)/shard_map/ppermute | solution.py:17
  72.9 0.9 copy-start.2
  73.8 99.3 %all-to-all-start.5 = ((bf16[128,4,768]{0,2,1:T(8,128)(2,1)}), bf16[128,4,768]{0,2,1:T(8,128)(2,1)}, u32[]{:S(2)}, u32[]{:S(2)}) async-start(bf16[128,4,768]{0,2,1:T(8,128)(2,1)} %bitcast.13), calls=%async_computation.5 | async-start | bytes 1572864 | tf_op jit(solution)/shard_map/all_to_all | solution.py:92
  184.3 2.2 copy-start.1
  186.4 13.2 %copy-start = (bf16[1,2560,768]{1,2,0:T(8,128)(2,1)}, bf16[1,2560,768]{1,2,0:T(8,128)(2,1)S(1)}, u32[]{:S(2)}) copy-start(bf16[1,2560,768]{1,2,0:T(8,128)(2,1)S(1)} %get-tuple-element.49) | copy-start | bytes 11796484
  213.5 16.3 %copy-start.3 = (bf16[512,6,128]{0,2,1:T(8,128)(2,1)S(1)}, bf16[512,6,128]{0,2,1:T(8,128)(2,1)}, u32[]{:S(2)}) copy-start(bf16[512,6,128]{0,2,1:T(8,128)(2,1)} %squeeze.30) | copy-start | bytes 2359300
  343.0 24.0 %copy-start.5 = (bf16[512,6,128]{0,2,1:T(8,128)(2,1)S(1)}, bf16[512,6,128]{0,2,1:T(8,128)(2,1)}, u32[]{:S(2)}) copy-start(bf16[512,6,128]{0,2,1:T(8,128)(2,1)} %get-tuple-element.55) | copy-start | bytes 2359300
  352.6 202.7 %collective-permute-start.11 = (f32[2,512,768]{2,1,0:T(8,128)}, f32[2,512,768]{2,1,0:T(8,128)}, u32[]{:S(2)}, u32[]{:S(2)}) collective-permute-start(f32[2,512,768]{2,1,0:T(8,128)} %get-tuple-element.47), channel_id=1, source_target_pairs={{0,8},{4,12},{8,16},{12,20},{16,24},{20,28},{24,32},{28,36},{32,40... | collective-permute-start | bytes 9437192 | tf_op jit(solution)/shard_map/ppermute | solution.py:17
  354.5 200.8 %collective-permute-start.10 = (f32[2,512,768]{2,1,0:T(8,128)}, f32[2,512,768]{2,1,0:T(8,128)}, u32[]{:S(2)}, u32[]{:S(2)}) collective-permute-start(f32[2,512,768]{2,1,0:T(8,128)} %get-tuple-element.48), channel_id=1, source_target_pairs={{0,4},{4,8},{8,12},{12,16},{16,20},{20,24},{24,28},{28,32},{32,36}... | collective-permute-start | bytes 9437192 | tf_op jit(solution)/shard_map/ppermute | solution.py:17
  356.4 198.9 %collective-permute-start.9 = (f32[2,512,768]{2,1,0:T(8,128)}, f32[2,512,768]{2,1,0:T(8,128)}, u32[]{:S(2)}, u32[]{:S(2)}) collective-permute-start(f32[2,512,768]{2,1,0:T(8,128)} %get-tuple-element.46), channel_id=1, source_target_pairs={{4,0},{8,4},{12,8},{16,12},{20,16},{24,20},{28,24},{32,28},{36,32}... | collective-permute-start | bytes 9437192 | tf_op jit(solution)/shard_map/ppermute | solution.py:17
  362.8 192.6 %collective-permute-start.8 = (f32[2,512,768]{2,1,0:T(8,128)}, f32[2,512,768]{2,1,0:T(8,128)}, u32[]{:S(2)}, u32[]{:S(2)}) collective-permute-start(f32[2,512,768]{2,1,0:T(8,128)} %get-tuple-element.45), channel_id=1, source_target_pairs={{8,0},{12,4},{16,8},{20,12},{24,16},{28,20},{32,24},{36,28},{40,32... | collective-permute-start | bytes 9437192 | tf_op jit(solution)/shard_map/ppermute | solution.py:17
  368.1 183.5 %all-to-all-start.4 = ((bf16[4,128,768]{1,2,0:T(8,128)(2,1)}), bf16[4,128,768]{1,2,0:T(8,128)(2,1)S(1)}, u32[]{:S(2)}, u32[]{:S(2)}) async-start(bf16[4,128,768]{1,2,0:T(8,128)(2,1)} %copy.77), calls=%async_computation.4 | async-start | bytes 1572864 | tf_op jit(solution)/shard_map/all_to_all | solution.py:155
  551.7 15.4 %all-to-all-start.6 = ((bf16[4,128,768]{1,2,0:T(8,128)(2,1)}), bf16[4,128,768]{1,2,0:T(8,128)(2,1)S(1)}, u32[]{:S(2)}, u32[]{:S(2)}) async-start(bf16[4,128,768]{1,2,0:T(8,128)(2,1)} %copy.83), calls=%async_computation.6 | async-start | bytes 1572864 | tf_op jit(solution)/shard_map/all_to_all | solution.py:156
  581.1 15.1 %all-to-all-start.8 = ((bf16[4,128,768]{2,1,0:T(8,128)(2,1)}), bf16[4,128,768]{2,1,0:T(8,128)(2,1)S(1)}, u32[]{:S(2)}, u32[]{:S(2)}) async-start(bf16[4,128,768]{2,1,0:T(8,128)(2,1)} %bitcast.116), calls=%async_computation.8 | async-start | bytes 1572864 | tf_op jit(solution)/shard_map/all_to_all | solution.py:160
where the time goes:
time: 604 us; the launch traced here: 598 us
  waiting for transfers between devices  280 us (46%)
  local copies, waits for them, and re-layouts  121 us (20%)
  matrix products  83.7 us (14%)
  starting transfers between devices  73.8 us (12%)
  other arithmetic  24 us (4%)
  blocking collectives  14.1 us (2%)
    all_to_all x1, waiting for transfers between devices, on_device(): lax.all_to_all(attended, 'head', split_axis=0, concat_axis=1, tiled=True)  170 us
    all_to_all x1, waiting for transfers between devices, on_device(): lax.all_to_all(grad_out, 'head', split_axis=1, concat_axis=0, tiled=True)  87.4 us
    ppermute x12, starting transfers between devices, from_behind(): lax.ppermute(value, axis, [(source, source + steps) for source in range(f...  44.4 us
    another operation x3, local copies, waits for them, and re-layouts, on_device(): jnp.stack([key_sums, value_sums]).reshape(2, 5, slot_count, local_width)  28.9 us
    unnamed x31, local copies, waits for them, and re-layouts  26.4 us
    dot_general x1, matrix products, attend_block(): jnp.einsum('qhd,khd->hqk', grad_rows, value_rows, preferred_element_type=...  22 us
    dot_general x1, matrix products, attend_block(): jnp.einsum('hqk,khd->qhd', weights_low, value_rows, preferred_element_typ...  16.2 us
    dot_general x1, matrix products, attend_block(): jnp.einsum('hqk,qhd->khd', weights_low, grad_rows, preferred_element_type...  15.7 us
  transfers between devices with their start and end apart: 20, of which 6 were waited for; matrix products, arithmetic and copies ran while one was open for 9% of the time, Pallas kernels for 0%

commit v1 on v0

v1 whole, which is shorter than its diff:
```python
import functools
import math

import jax
import jax.numpy as jnp
from jax import lax
from jax.experimental import pallas as pl
from jax.experimental.pallas import tpu as pltpu
from jax.sharding import Mesh
from jax.sharding import PartitionSpec as P

DH = 128
SHARD_MS = 625
RADIUS_MS = 1000
NEG_FILL = -1e30
FAR = -1e6
SCALE = DH ** (-0.5)
LOG2E = 1.4426950408889634
GROUP = ("yh", "head")
CHUNKS = ((0,), (1,), (2,))
RANGES = 2
REACH = 2
VMEM_BYTES = 56 * 1024 * 1024


def dot(lhs, rhs, dims):
    return lax.dot_general(lhs, rhs, (dims, ((), ())), preferred_element_type=jnp.float32)


def dot_nn(lhs, rhs):
    return dot(lhs, rhs, ((1,), (0,)))


def dot_nt(lhs, rhs):
    return dot(lhs, rhs, ((1,), (1,)))


def pack_kernel(peers, heads, chunks, a_ref, b_ref, *outs):
    for out, chunk in zip(outs, chunks):
        for peer in range(peers):
            for place, head in enumerate(chunk):
                lanes = pl.ds((peer * heads + head) * DH, DH)
                out[peer, place, 0] = a_ref[:, lanes]
                out[peer, place, 1] = b_ref[:, lanes]


def pack(first, second, peers, chunks):
    rows, width = first.shape
    heads = width // DH // peers
    return pl.pallas_call(
        functools.partial(pack_kernel, peers, heads, chunks),
        out_shape=[
            jax.ShapeDtypeStruct((peers, len(chunk), 2, rows, DH), first.dtype) for chunk in chunks
        ],
        compiler_params=pltpu.CompilerParams(vmem_limit_bytes=VMEM_BYTES),
        name="pack",
    )(first, second)


def unpack_kernel(peers, heads, chunks, *refs):
    ins, (a_ref, b_ref) = refs[: len(chunks)], refs[len(chunks) :]
    for piece, chunk in zip(ins, chunks):
        for peer in range(peers):
            for place, head in enumerate(chunk):
                lanes = pl.ds((peer * heads + head) * DH, DH)
                a_ref[:, lanes] = piece[peer, place, 0]
                b_ref[:, lanes] = piece[peer, place, 1]


def unpack(pieces, chunks):
    peers, _, _, rows, _ = pieces[0].shape
    heads = sum(len(chunk) for chunk in chunks)
    shape = jax.ShapeDtypeStruct((rows, peers * heads * DH), pieces[0].dtype)
    return pl.pallas_call(
        functools.partial(unpack_kernel, peers, heads, chunks),
        out_shape=[shape, shape],
        compiler_params=pltpu.CompilerParams(vmem_limit_bytes=VMEM_BYTES),
        name="unpack",
    )(*pieces)


def attend_kernel(
    per, size, stamps_ref, qg_ref, left_ref, own_ref, right_ref,
    result_ref, to_left_ref, own_sum_ref, to_right_ref,
    keys, values, keys_t, values_t, scores, grad_weights, key_sums, value_sums, total_t, query_t,
):
    span = 2 * REACH + 1
    for side, ref in enumerate((left_ref, own_ref, right_ref)):
        for part in range(RANGES):
            place = side * RANGES + part
            rows = pl.ds(part * per, per)
            key_tile = ref[rows, 0, 0].reshape(size, DH)
            value_tile = ref[rows, 0, 1].reshape(size, DH)
            keys[place] = key_tile
            values[place] = value_tile
            keys_t[place] = key_tile.T
            values_t[place] = value_tile.T
    key_sums[...] = jnp.zeros_like(key_sums)
    value_sums[...] = jnp.zeros_like(value_sums)
    offsets = lax.broadcasted_iota(jnp.int32, (1, size), 1) * SHARD_MS // size
    for part in range(RANGES):
        rows = pl.ds(part * per, per)
        query = qg_ref[rows, 0, 0].reshape(size, DH)
        grad = qg_ref[rows, 0, 1].reshape(size, DH)
        stamp = (offsets + part * SHARD_MS).astype(jnp.float32)

        def score_step(step, top):
            place = step + part
            found = dot_nt(keys[place], query)
            near = jnp.abs(jnp.tile(stamps_ref[place], (1, size // DH)) - stamp) <= RADIUS_MS
            found = jnp.where(near, found * (SCALE * LOG2E), NEG_FILL)
            scores[step] = found
            return jnp.maximum(top, jnp.max(found.reshape(size // 8, 8, size), axis=0))

        top = lax.fori_loop(0, span, score_step, jnp.full((8, size), NEG_FILL, jnp.float32))
        top = jnp.max(top, axis=0, keepdims=True)
        total_t[...] = jnp.zeros_like(total_t)

        def weight_step(step, total):
            place = step + part
            raised = jnp.exp2(scores[step] - top)
            scores[step] = raised
            total_t[...] += dot_nn(values_t[place], raised.astype(jnp.bfloat16))
            grad_weights[step] = dot_nt(values[place], grad)
            return total + jnp.sum(raised.reshape(size // 8, 8, size), axis=0)

        total = lax.fori_loop(0, span, weight_step, jnp.zeros((8, size), jnp.float32))
        inverse = 1.0 / jnp.sum(total, axis=0, keepdims=True)
        attended_t = total_t[...] * inverse
        row_dot = jnp.sum(attended_t * grad.astype(jnp.float32).T, axis=0, keepdims=True)
        result_ref[rows, 0, 0] = attended_t.T.astype(jnp.bfloat16).reshape(per, size // per, DH)
        query_t[...] = jnp.zeros_like(query_t)

        def grad_step(step, carry):
            place = step + part
            weights = scores[step] * inverse
            slopes = (weights * (grad_weights[step] - row_dot)).astype(jnp.bfloat16)
            value_sums[place] += dot_nn(weights.astype(jnp.bfloat16), grad)
            key_sums[place] += dot_nn(slopes, query)
            query_t[...] += dot_nn(keys_t[place], slopes)
            return carry

        lax.fori_loop(0, span, grad_step, 0)
        result_ref[rows, 0, 1] = (
            (query_t[...] * SCALE).T.astype(jnp.bfloat16).reshape(per, size // per, DH)
        )
    for side, ref in enumerate((to_left_ref, own_sum_ref, to_right_ref)):
        for part in range(RANGES):
            place = side * RANGES + part
            rows = pl.ds(part * per, per)
            shape = (per, size // per, DH)
            ref[rows, 0, 0] = (key_sums[place] * SCALE).astype(ref.dtype).reshape(shape)
            ref[rows, 0, 1] = value_sums[place].astype(ref.dtype).reshape(shape)


def attend(stamps, query_grad, left, own, right):
    peers, heads, _, rows, _ = own.shape
    per = peers // RANGES
    size = per * rows
    span = 2 * REACH + 1
    places = 3 * RANGES
    piece = pl.BlockSpec((peers, 1, 2, rows, DH), lambda head: (0, head, 0, 0, 0))
    low = jax.ShapeDtypeStruct(own.shape, jnp.bfloat16)
    wide = jax.ShapeDtypeStruct(own.shape, jnp.float32)
    pairs = RANGES * span * size * size * heads
    return pl.pallas_call(
        functools.partial(attend_kernel, per, size),
        grid=(heads,),
        in_specs=[pl.BlockSpec((places, size, DH), lambda head: (0, 0, 0))] + [piece] * 4,
        out_specs=[piece] * 4,
        out_shape=[low, low, wide, low],
        scratch_shapes=[
            pltpu.VMEM((places, size, DH), jnp.bfloat16),
            pltpu.VMEM((places, size, DH), jnp.bfloat16),
            pltpu.VMEM((places, DH, size), jnp.bfloat16),
            pltpu.VMEM((places, DH, size), jnp.bfloat16),
            pltpu.VMEM((span, size, size), jnp.float32),
            pltpu.VMEM((span, size, size), jnp.float32),
            pltpu.VMEM((places, size, DH), jnp.float32),
            pltpu.VMEM((places, size, DH), jnp.float32),
            pltpu.VMEM((DH, size), jnp.float32),
            pltpu.VMEM((DH, size), jnp.float32),
        ],
        compiler_params=pltpu.CompilerParams(vmem_limit_bytes=VMEM_BYTES),
        cost_estimate=pl.CostEstimate(
            flops=pairs * DH * 12, bytes_accessed=16 * own.size, transcendentals=pairs
        ),
        name="attend",
    )(stamps, query_grad, left, own, right)


def swap(value):
    return lax.all_to_all(value, GROUP, split_axis=0, concat_axis=0, tiled=True)


def shifted(value, steps):
    count = lax.axis_size("col")
    first, last = max(0, -steps), min(count, count - steps)
    return lax.ppermute(value, "col", [(at, at + steps) for at in range(first, last)])


def on_device(video_query, audio_key, audio_value, grad_out, audio_time):
    peers = lax.axis_size(GROUP)
    key_values = pack(audio_key, audio_value, peers, CHUNKS)
    query_grads = pack(video_query, grad_out, peers, CHUNKS)
    lifted = lax.all_gather(audio_time, GROUP, axis=0, tiled=True) + 1
    window = jnp.concatenate([shifted(lifted, 1), lifted, shifted(lifted, -1)]) - 1
    base = lax.axis_index("col") * (RANGES * SHARD_MS)
    stamps = jnp.where(window >= 0, (window - base).astype(jnp.float32), FAR)
    size = lifted.shape[0] // RANGES
    stamps = jnp.broadcast_to(stamps[:, None], (stamps.shape[0], DH)).reshape(-1, size, DH)
    results, grads = [], []
    for key_value, query_grad in zip(key_values, query_grads):
        own = swap(key_value)
        left, right = shifted(own, 1), shifted(own, -1)
        result, to_left, own_sum, to_right = attend(stamps, swap(query_grad), left, own, right)
        results.append(swap(result))
        summed = (
            own_sum
            + shifted(to_left, -1).astype(jnp.float32)
            + shifted(to_right, 1).astype(jnp.float32)
        )
        grads.append(swap(summed.astype(jnp.bfloat16)))
    attended, grad_query = unpack(results, CHUNKS)
    grad_key, grad_value = unpack(grads, CHUNKS)
    return attended, grad_query, grad_key, grad_value


def solution(mesh):
    columns = mesh.shape["seq"] // RANGES
    split = Mesh(
        mesh.devices.reshape(columns, RANGES, mesh.shape["head"]), ("col", "yh", "head")
    )
    rows = P(("col", "yh", "head"), None)
    return jax.shard_map(
        on_device,
        mesh=split,
        in_specs=(rows, rows, rows, rows, P(("col", "yh", "head"))),
        out_specs=(rows, rows, rows, rows),
        check_vma=False,
    )
```

time: 604 us -> 257 us (0.43)
  the two profiles are of different devices: /device:TPU:38 before, /device:TPU:96 now
where the time goes in v1:
time: 257 us; the launch traced here: 255 us
  starting transfers between devices  90.9 us (35%)
  Pallas kernels  66.3 us (26%)
  blocking collectives  53.5 us (21%)
  waiting for transfers between devices  31.9 us (12%)
  other arithmetic  6.79 us (3%)
  local copies, waits for them, and re-layouts  4.84 us (2%)
    pallas_call x3, Pallas kernels, attend(): pl.pallas_call(functools.partial(attend_kernel, per, size), grid=(heads,)...  54.9 us
    ppermute x14, starting transfers between devices, shifted(): lax.ppermute(value, 'col', [(at, at + steps) for at in range(first, last)])  52.2 us
    all_to_all x3, blocking collectives, swap(): return lax.all_to_all(value, GROUP, split_axis=0, concat_axis=0, tiled=True)  42.7 us
    all_to_all x9, starting transfers between devices, swap(): return lax.all_to_all(value, GROUP, split_axis=0, concat_axis=0, tiled=True)  38.7 us
    ppermute x14, waiting for transfers between devices, shifted(): lax.ppermute(value, 'col', [(at, at + steps) for at in range(first, last)])  17 us
    all_to_all x9, waiting for transfers between devices, swap(): return lax.all_to_all(value, GROUP, split_axis=0, concat_axis=0, tiled=True)  14.9 us
    all_gather x1, blocking collectives, on_device(): lifted = lax.all_gather(audio_time, GROUP, axis=0, tiled=True) + 1  10.9 us
    convert_element_type x3, other arithmetic, on_device(): grads.append(swap(summed.astype(jnp.bfloat16)))  6.74 us
  transfers between devices with their start and end apart: 23, of which 7 were waited for; matrix products, arithmetic and copies ran while one was open for 3% of the time, Pallas kernels for 24%

profile of v1, /device:TPU:96, one launch (start us, length us, event | category | flops | bytes accessed | tf_op | source)
XLA Modules:
  0.0 255.3 jit_solution(8519543417144811698)
XLA Ops:
  0.6 2.8 %pack.2 = (bf16[8,1,2,128,128]{4,3,2,1,0:T(8,128)(2,1)}, bf16[8,1,2,128,128]{4,3,2,1,0:T(8,128)(2,1)}, bf16[8,1,2,128,128]{4,3,2,1,0:T(8,128)(2,1)}) custom-call(bf16[128,3072]{1,0:T(8,128)(2,1)} %a_ref.2, bf16[128,3072]{1,0:T(8,128)(2,1)} %b_ref.2), custom_call_target="tpu_custom_call" | custom-call | tf_op jit(solution)/shard_map/pack/pallas_call | solution.py:50
  3.4 15.0 %all_to_all.60.qg_ref = bf16[8,1,2,128,128]{4,3,2,1,0:T(8,128)(2,1)} all-to-all(bf16[8,1,2,128,128]{4,3,2,1,0:T(8,128)(2,1)} %get-tuple-element.26), channel_id=1, replica_groups=mesh['col'=16,'yh'=2,'head'=4] {'yh','head'}, dimensions={0} | all-to-all | bytes 1048576 | tf_op jit(solution)/shard_map/all_to_all | solution.py:193
  18.4 3.5 %all-to-all-start.3 = ((bf16[8,1,2,128,128]{4,3,2,1,0:T(8,128)(2,1)}), bf16[8,1,2,128,128]{4,3,2,1,0:T(8,128)(2,1)S(1)}, u32[]{:S(2)}, u32[]{:S(2)}) async-start(bf16[8,1,2,128,128]{4,3,2,1,0:T(8,128)(2,1)} %get-tuple-element.29), calls=%async_computation.3 | async-start | bytes 1048576 | tf_op jit(solution)/shard_map/all_to_all | solution.py:193
  21.9 2.8 %pack.3 = (bf16[8,1,2,128,128]{4,3,2,1,0:T(8,128)(2,1)}, bf16[8,1,2,128,128]{4,3,2,1,0:T(8,128)(2,1)}, bf16[8,1,2,128,128]{4,3,2,1,0:T(8,128)(2,1)}) custom-call(bf16[128,3072]{1,0:T(8,128)(2,1)} %a_ref.3, bf16[128,3072]{1,0:T(8,128)(2,1)} %b_ref.3), custom_call_target="tpu_custom_call" | custom-call | tf_op jit(solution)/shard_map/pack/pallas_call | solution.py:50
  24.6 7.5 %all-to-all-done.3.qg_ref = bf16[8,1,2,128,128]{4,3,2,1,0:T(8,128)(2,1)S(1)} async-done(((bf16[8,1,2,128,128]{4,3,2,1,0:T(8,128)(2,1)}), bf16[8,1,2,128,128]{4,3,2,1,0:T(8,128)(2,1)S(1)}, u32[]{:S(2)}, u32[]{:S(2)}) %all-to-all-start.3) | async-done | bytes 524320 | tf_op jit(solution)/shard_map/all_to_all | solution.py:193
  32.1 13.9 %all_to_all.61.own_ref = bf16[8,1,2,128,128]{4,3,2,1,0:T(8,128)(2,1)S(1)} all-to-all(bf16[8,1,2,128,128]{4,3,2,1,0:T(8,128)(2,1)} %get-tuple-element.30), channel_id=1, replica_groups=mesh['col'=16,'yh'=2,'head'=4] {'yh','head'}, dimensions={0} | all-to-all | bytes 1048576 | tf_op jit(solution)/shard_map/all_to_all | solution.py:193
  46.1 13.8 %all_to_all.62.own_ref = bf16[8,1,2,128,128]{4,3,2,1,0:T(8,128)(2,1)S(1)} all-to-all(bf16[8,1,2,128,128]{4,3,2,1,0:T(8,128)(2,1)} %get-tuple-element.33), channel_id=1, replica_groups=mesh['col'=16,'yh'=2,'head'=4] {'yh','head'}, dimensions={0} | all-to-all | bytes 1048576 | tf_op jit(solution)/shard_map/all_to_all | solution.py:193
  59.9 3.5 %all-to-all-start.6 = ((bf16[8,1,2,128,128]{4,3,2,1,0:T(8,128)(2,1)}), bf16[8,1,2,128,128]{4,3,2,1,0:T(8,128)(2,1)S(1)}, u32[]{:S(2)}, u32[]{:S(2)}) async-start(bf16[8,1,2,128,128]{4,3,2,1,0:T(8,128)(2,1)} %get-tuple-element.32), calls=%async_computation.6 | async-start | bytes 1048576 | tf_op jit(solution)/shard_map/all_to_all | solution.py:193
  63.4 4.5 %collective-permute-start.7 = (bf16[8,1,2,128,128]{4,3,2,1,0:T(8,128)(2,1)S(1)}, bf16[8,1,2,128,128]{4,3,2,1,0:T(8,128)(2,1)}, u32[]{:S(2)}, u32[]{:S(2)}) collective-permute-start(bf16[8,1,2,128,128]{4,3,2,1,0:T(8,128)(2,1)S(1)} %all_to_all.62.own_ref), channel_id=1, source_target_pairs={{8,0},{16,8},{24,16},{32,24},{40,32},{48,40},{56,48},{64,56},{72,6... | collective-permute-start | bytes 1572872 | tf_op jit(solution)/shard_map/ppermute | solution.py:199
  67.9 1.9 collective-permute-start.6
  69.8 10.9 %all-gather = s32[8,1,128]{2,1,0:T(1,128)S(1)} all-gather(s32[1,1,128]{2,1,0:T(1,128)S(1)} %bitcast.10), channel_id=1, replica_groups=mesh['col'=16,'yh'=2,'head'=4] {'yh','head'}, dimensions={0}, use_global_device_ids=true | all-gather | bytes 4608 | tf_op jit(solution)/shard_map/all_gather | solution.py:206
  80.7 6.0 %collective-permute-start.5 = (bf16[8,1,2,128,128]{4,3,2,1,0:T(8,128)(2,1)S(1)}, bf16[8,1,2,128,128]{4,3,2,1,0:T(8,128)(2,1)S(1)}, u32[]{:S(2)}, u32[]{:S(2)}) collective-permute-start(bf16[8,1,2,128,128]{4,3,2,1,0:T(8,128)(2,1)S(1)} %all_to_all.61.own_ref), channel_id=1, source_target_pairs={{8,0},{16,8},{24,16},{32,24},{40,32},{48,40},{56,48},{64,56},{72,6... | collective-permute-start | bytes 1572872 | tf_op jit(solution)/shard_map/ppermute | solution.py:199
  86.7 1.9 collective-permute-start.4
  88.7 0.0 all-to-all-done.6.qg_ref
  88.7 0.0 copy-start.14
  88.7 3.5 %all-to-all-start.1 = ((bf16[8,1,2,128,128]{4,3,2,1,0:T(8,128)(2,1)}), bf16[8,1,2,128,128]{4,3,2,1,0:T(8,128)(2,1)S(1)}, u32[]{:S(2)}, u32[]{:S(2)}) async-start(bf16[8,1,2,128,128]{4,3,2,1,0:T(8,128)(2,1)} %get-tuple-element.27), calls=%async_computation.1 | async-start | bytes 1048576 | tf_op jit(solution)/shard_map/all_to_all | solution.py:193
  92.2 6.0 %collective-permute-start.1 = (s32[1024]{0:T(1024)S(1)}, s32[1024]{0:T(1024)S(1)}, u32[]{:S(2)}, u32[]{:S(2)}) collective-permute-start(s32[1024]{0:T(1024)S(1)} %bitcast.6), channel_id=1, source_target_pairs={{8,0},{16,8},{24,16},{32,24},{40,32},{48,40},{56,48},{64,56},{72,6... | collective-permute-start | bytes 12296 | tf_op jit(solution)/shard_map/ppermute | solution.py:199
  98.3 1.3 collective-permute-done.1
  99.6 1.9 collective-permute-start
  101.5 5.9 %collective-permute-done = s32[1024]{0:T(1024)S(1)} collective-permute-done((s32[1024]{0:T(1024)S(1)}, s32[1024]{0:T(1024)S(1)}, u32[]{:S(2)}, u32[]{:S(2)}) %collective-permute-start) | collective-permute-done | bytes 4128 | tf_op jit(solution)/shard_map/ppermute | solution.py:199
  107.5 0.0 collective-permute-done.7.right_ref
  107.5 0.0 collective-permute-done.6.left_ref
  107.5 1.6 broadcast_in_dim.11.stamps_ref
  109.2 18.2 %attend.5 = (bf16[8,1,2,128,128]{4,3,2,1,0:T(8,128)(2,1)}, bf16[8,1,2,128,128]{4,3,2,1,0:T(8,128)(2,1)}, f32[8,1,2,128,128]{4,3,2,1,0:T(8,128)}, bf16[8,1,2,128,128]{4,3,2,1,0:T(8,128)(2,1)}) custom-call(f32[6,512,128]{2,1,0:T(8,128)} %broadcast_in_dim.11.stamps_ref, bf16[8,1,2,128,128]{4,3,2,1,0:T(8,128)(2,1)} %copy-done.14, ...), custom_call_target="tpu_custom_call" | custom-call | flops 4026531840 | bytes 4194304 | tf_op jit(solution)/shard_map/attend/pallas_call | solution.py:166
  127.4 0.0 all-to-all-done.1.own_ref
  127.4 4.7 %all-to-all-start.8 = ((bf16[8,1,2,128,128]{4,3,2,1,0:T(8,128)(2,1)}), bf16[8,1,2,128,128]{4,3,2,1,0:T(8,128)(2,1)S(1)}, u32[]{:S(2)}, u32[]{:S(2)}) async-start(bf16[8,1,2,128,128]{4,3,2,1,0:T(8,128)(2,1)} %get-tuple-element.34), calls=%async_computation.8 | async-start | bytes 1048576 | tf_op jit(solution)/shard_map/all_to_all | solution.py:193
  132.1 3.9 %collective-permute-start.3 = (bf16[8,1,2,128,128]{4,3,2,1,0:T(8,128)(2,1)S(1)}, bf16[8,1,2,128,128]{4,3,2,1,0:T(8,128)(2,1)}, u32[]{:S(2)}, u32[]{:S(2)}) collective-permute-start(bf16[8,1,2,128,128]{4,3,2,1,0:T(8,128)(2,1)S(1)} %all-to-all-done.1.own_ref), channel_id=1, source_target_pairs={{8,0},{16,8},{24,16},{32,24},{40,32},{48,40},{56,48},{64,56},{72,6... | collective-permute-start | bytes 1572872 | tf_op jit(solution)/shard_map/ppermute | solution.py:199
  136.1 1.9 collective-permute-start.2
  138.0 0.0 collective-permute-done.5.right_ref
  138.0 0.0 collective-permute-done.4.left_ref
  138.0 0.8 copy-done.16
  138.8 0.8 copy-done.17
  139.6 18.4 %attend.4 = (bf16[8,1,2,128,128]{4,3,2,1,0:T(8,128)(2,1)}, bf16[8,1,2,128,128]{4,3,2,1,0:T(8,128)(2,1)}, f32[8,1,2,128,128]{4,3,2,1,0:T(8,128)}, bf16[8,1,2,128,128]{4,3,2,1,0:T(8,128)(2,1)}) custom-call(f32[6,512,128]{2,1,0:T(8,128)} %broadcast_in_dim.11.stamps_ref, bf16[8,1,2,128,128]{4,3,2,1,0:T(8,128)(2,1)} %copy-done.10, ...), custom_call_target="tpu_custom_call" | custom-call | flops 4026531840 | bytes 4194304 | tf_op jit(solution)/shard_map/attend/pallas_call | solution.py:166
  158.0 0.0 all-to-all-done.8.refs_2_
  158.0 4.8 %all-to-all-start.5 = ((bf16[8,1,2,128,128]{4,3,2,1,0:T(8,128)(2,1)}), bf16[8,1,2,128,128]{4,3,2,1,0:T(8,128)(2,1)S(1)}, u32[]{:S(2)}, u32[]{:S(2)}) async-start(bf16[8,1,2,128,128]{4,3,2,1,0:T(8,128)(2,1)} %get-tuple-element.31), calls=%async_computation.5 | async-start | bytes 1048576 | tf_op jit(solution)/shard_map/all_to_all | solution.py:193
  162.8 6.0 %collective-permute-start.12 = (bf16[8,1,2,128,128]{4,3,2,1,0:T(8,128)(2,1)}, bf16[8,1,2,128,128]{4,3,2,1,0:T(8,128)(2,1)S(1)}, u32[]{:S(2)}, u32[]{:S(2)}) collective-permute-start(bf16[8,1,2,128,128]{4,3,2,1,0:T(8,128)(2,1)} %get-tuple-element.44), channel_id=1, source_target_pairs={{8,0},{16,8},{24,16},{32,24},{40,32},{48,40},{56,48},{64,56},{72,6... | collective-permute-start | bytes 1572872 | tf_op jit(solution)/shard_map/ppermute | solution.py:199
  168.8 2.1 collective-permute-start.13
  171.0 0.0 collective-permute-done.3.right_ref
  171.0 18.3 %attend.3 = (bf16[8,1,2,128,128]{4,3,2,1,0:T(8,128)(2,1)}, bf16[8,1,2,128,128]{4,3,2,1,0:T(8,128)(2,1)}, f32[8,1,2,128,128]{4,3,2,1,0:T(8,128)}, bf16[8,1,2,128,128]{4,3,2,1,0:T(8,128)(2,1)}) custom-call(f32[6,512,128]{2,1,0:T(8,128)} %broadcast_in_dim.11.stamps_ref, bf16[8,1,2,128,128]{4,3,2,1,0:T(8,128)(2,1)} %all_to_all.60.qg_ref, ...), custom_call_target="tpu_custom_call" | custom-call | flops 4026531840 | bytes 4194304 | tf_op jit(solution)/shard_map/attend/pallas_call | solution.py:166
  189.3 0.0 all-to-all-done.5.refs_1_
  189.3 4.9 %all-to-all-start.2 = ((bf16[8,1,2,128,128]{4,3,2,1,0:T(8,128)(2,1)}), bf16[8,1,2,128,128]{4,3,2,1,0:T(8,128)(2,1)S(1)}, u32[]{:S(2)}, u32[]{:S(2)}) async-start(bf16[8,1,2,128,128]{4,3,2,1,0:T(8,128)(2,1)} %get-tuple-element.28), calls=%async_computation.2 | async-start | bytes 1048576 | tf_op jit(solution)/shard_map/all_to_all | solution.py:193
  194.3 6.0 %collective-permute-start.10 = (bf16[8,1,2,128,128]{4,3,2,1,0:T(8,128)(2,1)}, bf16[8,1,2,128,128]{4,3,2,1,0:T(8,128)(2,1)}, u32[]{:S(2)}, u32[]{:S(2)}) collective-permute-start(bf16[8,1,2,128,128]{4,3,2,1,0:T(8,128)(2,1)} %get-tuple-element.41), channel_id=1, source_target_pairs={{8,0},{16,8},{24,16},{32,24},{40,32},{48,40},{56,48},{64,56},{72,6... | collective-permute-start | bytes 1572872 | tf_op jit(solution)/shard_map/ppermute | solution.py:199
  200.3 1.9 collective-permute-start.11
  202.2 0.0 copy-start.9
  202.2 0.0 collective-permute-done.13
  202.2 0.8 copy-done.9
  203.0 2.3 add_convert_fusion
  205.3 0.0 all-to-all-done.2.refs_0_
  205.3 4.8 %all-to-all-start.11 = ((bf16[8,1,2,128,128]{4,3,2,1,0:T(8,128)(2,1)}), bf16[8,1,2,128,128]{4,3,2,1,0:T(8,128)(2,1)S(1)}, u32[]{:S(2)}, u32[]{:S(2)}) async-start(bf16[8,1,2,128,128]{4,3,2,1,0:T(8,128)(2,1)} %add_convert_fusion), calls=%async_computation.11 | async-start | bytes 1048576 | tf_op jit(solution)/shard_map/all_to_all | solution.py:193
  210.1 6.0 %collective-permute-start.8 = (bf16[8,1,2,128,128]{4,3,2,1,0:T(8,128)(2,1)}, bf16[8,1,2,128,128]{4,3,2,1,0:T(8,128)(2,1)}, u32[]{:S(2)}, u32[]{:S(2)}) collective-permute-start(bf16[8,1,2,128,128]{4,3,2,1,0:T(8,128)(2,1)} %get-tuple-element.38), channel_id=1, source_target_pairs={{8,0},{16,8},{24,16},{32,24},{40,32},{48,40},{56,48},{64,56},{72,6... | collective-permute-start | bytes 1572872 | tf_op jit(solution)/shard_map/ppermute | solution.py:199
  216.2 1.9 collective-permute-start.9
  218.1 0.6 collective-permute-done.11
  218.7 2.3 add_convert_fusion.1
  220.9 0.0 all-to-all-done.11.refs_2_
  220.9 4.5 %all-to-all-start.10 = ((bf16[8,1,2,128,128]{4,3,2,1,0:T(8,128)(2,1)}), bf16[8,1,2,128,128]{4,3,2,1,0:T(8,128)(2,1)S(1)}, u32[]{:S(2)}, u32[]{:S(2)}) async-start(bf16[8,1,2,128,128]{4,3,2,1,0:T(8,128)(2,1)} %add_convert_fusion.1), calls=%async_computation.10 | async-start | bytes 1048576 | tf_op jit(solution)/shard_map/all_to_all | solution.py:193
  225.4 2.9 %collective-permute-done.8 = bf16[8,1,2,128,128]{4,3,2,1,0:T(8,128)(2,1)} collective-permute-done((bf16[8,1,2,128,128]{4,3,2,1,0:T(8,128)(2,1)}, bf16[8,1,2,128,128]{4,3,2,1,0:T(8,128)(2,1)}, u32[]{:S(2)}, u32[]{:S(2)}) %collective-permute-start.8) | collective-permute-done | bytes 524320 | tf_op jit(solution)/shard_map/ppermute | solution.py:199
  228.3 6.2 %collective-permute-done.9 = bf16[8,1,2,128,128]{4,3,2,1,0:T(8,128)(2,1)} collective-permute-done((bf16[8,1,2,128,128]{4,3,2,1,0:T(8,128)(2,1)}, bf16[8,1,2,128,128]{4,3,2,1,0:T(8,128)(2,1)}, u32[]{:S(2)}, u32[]{:S(2)}) %collective-permute-start.9) | collective-permute-done | bytes 524320 | tf_op jit(solution)/shard_map/ppermute | solution.py:199
  234.5 2.2 add_convert_fusion.2
  236.7 0.0 all-to-all-done.10.refs_1_
  236.7 4.5 %all-to-all-start.9 = ((bf16[8,1,2,128,128]{4,3,2,1,0:T(8,128)(2,1)}), bf16[8,1,2,128,128]{4,3,2,1,0:T(8,128)(2,1)S(1)}, u32[]{:S(2)}, u32[]{:S(2)}) async-start(bf16[8,1,2,128,128]{4,3,2,1,0:T(8,128)(2,1)} %add_convert_fusion.2), calls=%async_computation.9 | async-start | bytes 1048576 | tf_op jit(solution)/shard_map/all_to_all | solution.py:193
  241.2 2.9 %unpack.2 = (bf16[128,3072]{1,0:T(8,128)(2,1)}, bf16[128,3072]{1,0:T(8,128)(2,1)}) custom-call(bf16[8,1,2,128,128]{4,3,2,1,0:T(8,128)(2,1)} %copy-done.2, bf16[8,1,2,128,128]{4,3,2,1,0:T(8,128)(2,1)} %copy-done.1, bf16[8,1,2,128,128]{4,3,2,1,0:T(8,128)(2,1)} %copy-done), custom_call_target="tpu_custom_call" | custom-call | tf_op jit(solution)/shard_map/unpack/pallas_call | solution.py:74
  244.1 7.4 %all-to-all-done.9.refs_0_ = bf16[8,1,2,128,128]{4,3,2,1,0:T(8,128)(2,1)S(1)} async-done(((bf16[8,1,2,128,128]{4,3,2,1,0:T(8,128)(2,1)}), bf16[8,1,2,128,128]{4,3,2,1,0:T(8,128)(2,1)S(1)}, u32[]{:S(2)}, u32[]{:S(2)}) %all-to-all-start.9) | async-done | bytes 524320 | tf_op jit(solution)/shard_map/all_to_all | solution.py:193
  251.6 0.8 copy-done.5
  252.3 2.9 %unpack.3 = (bf16[128,3072]{1,0:T(8,128)(2,1)}, bf16[128,3072]{1,0:T(8,128)(2,1)}) custom-call(bf16[8,1,2,128,128]{4,3,2,1,0:T(8,128)(2,1)} %copy-done.5, bf16[8,1,2,128,128]{4,3,2,1,0:T(8,128)(2,1)} %copy-done.4, bf16[8,1,2,128,128]{4,3,2,1,0:T(8,128)(2,1)} %copy-done.3), custom_call_target="tpu_custom_call" | custom-call | tf_op jit(solution)/shard_map/unpack/pallas_call | solution.py:74
  (36 shorter events, 0.1 us)
Async XLA Ops:
  18.4 13.8 %all-to-all-start.3 = ((bf16[8,1,2,128,128]{4,3,2,1,0:T(8,128)(2,1)}), bf16[8,1,2,128,128]{4,3,2,1,0:T(8,128)(2,1)S(1)}, u32[]{:S(2)}, u32[]{:S(2)}) async-start(bf16[8,1,2,128,128]{4,3,2,1,0:T(8,128)(2,1)} %get-tuple-element.29), calls=%async_computation.3 | async-start | bytes 1048576 | tf_op jit(solution)/shard_map/all_to_all | solution.py:193
  32.1 27.7 %copy-start.10 = (bf16[8,1,2,128,128]{4,3,2,1,0:T(8,128)(2,1)}, bf16[8,1,2,128,128]{4,3,2,1,0:T(8,128)(2,1)S(1)}, u32[]{:S(2)}) copy-start(bf16[8,1,2,128,128]{4,3,2,1,0:T(8,128)(2,1)S(1)} %all-to-all-done.3.qg_ref) | copy-start | bytes 1572868
  32.1 37.7 %copy-start.15 = (s32[128]{0:T(128)S(1)}, s32[128]{0:T(128)}, u32[]{:S(2)}) copy-start(s32[128]{0:T(128)} %param.9) | copy-start | bytes 1540
  46.1 42.6 %copy-start.11 = (bf16[8,1,2,128,128]{4,3,2,1,0:T(8,128)(2,1)}, bf16[8,1,2,128,128]{4,3,2,1,0:T(8,128)(2,1)S(1)}, u32[]{:S(2)}) copy-start(bf16[8,1,2,128,128]{4,3,2,1,0:T(8,128)(2,1)S(1)} %all_to_all.61.own_ref) | copy-start | bytes 1572868
  59.9 49.3 %copy-start.13 = (bf16[8,1,2,128,128]{4,3,2,1,0:T(8,128)(2,1)}, bf16[8,1,2,128,128]{4,3,2,1,0:T(8,128)(2,1)S(1)}, u32[]{:S(2)}) copy-start(bf16[8,1,2,128,128]{4,3,2,1,0:T(8,128)(2,1)S(1)} %all_to_all.62.own_ref) | copy-start | bytes 1572868
  59.9 28.8 %all-to-all-start.6 = ((bf16[8,1,2,128,128]{4,3,2,1,0:T(8,128)(2,1)}), bf16[8,1,2,128,128]{4,3,2,1,0:T(8,128)(2,1)S(1)}, u32[]{:S(2)}, u32[]{:S(2)}) async-start(bf16[8,1,2,128,128]{4,3,2,1,0:T(8,128)(2,1)} %get-tuple-element.32), calls=%async_computation.6 | async-start | bytes 1048576 | tf_op jit(solution)/shard_map/all_to_all | solution.py:193
  63.4 44.1 %collective-permute-start.7 = (bf16[8,1,2,128,128]{4,3,2,1,0:T(8,128)(2,1)S(1)}, bf16[8,1,2,128,128]{4,3,2,1,0:T(8,128)(2,1)}, u32[]{:S(2)}, u32[]{:S(2)}) collective-permute-start(bf16[8,1,2,128,128]{4,3,2,1,0:T(8,128)(2,1)S(1)} %all_to_all.62.own_ref), channel_id=1, source_target_pairs={{8,0},{16,8},{24,16},{32,24},{40,32},{48,40},{56,48},{64,56},{72,6... | collective-permute-start | bytes 1572872 | tf_op jit(solution)/shard_map/ppermute | solution.py:199
  67.9 39.6 %collective-permute-start.6 = (bf16[8,1,2,128,128]{4,3,2,1,0:T(8,128)(2,1)S(1)}, bf16[8,1,2,128,128]{4,3,2,1,0:T(8,128)(2,1)}, u32[]{:S(2)}, u32[]{:S(2)}) collective-permute-start(bf16[8,1,2,128,128]{4,3,2,1,0:T(8,128)(2,1)S(1)} %all_to_all.62.own_ref), channel_id=1, source_target_pairs={{0,8},{8,16},{16,24},{24,32},{32,40},{40,48},{48,56},{56,64},{64,7... | collective-permute-start | bytes 1572872 | tf_op jit(solution)/shard_map/ppermute | solution.py:199
  80.7 57.3 %collective-permute-start.5 = (bf16[8,1,2,128,128]{4,3,2,1,0:T(8,128)(2,1)S(1)}, bf16[8,1,2,128,128]{4,3,2,1,0:T(8,128)(2,1)S(1)}, u32[]{:S(2)}, u32[]{:S(2)}) collective-permute-start(bf16[8,1,2,128,128]{4,3,2,1,0:T(8,128)(2,1)S(1)} %all_to_all.61.own_ref), channel_id=1, source_target_pairs={{8,0},{16,8},{24,16},{32,24},{40,32},{48,40},{56,48},{64,56},{72,6... | collective-permute-start | bytes 1572872 | tf_op jit(solution)/shard_map/ppermute | solution.py:199
  86.7 51.3 %collective-permute-start.4 = (bf16[8,1,2,128,128]{4,3,2,1,0:T(8,128)(2,1)S(1)}, bf16[8,1,2,128,128]{4,3,2,1,0:T(8,128)(2,1)S(1)}, u32[]{:S(2)}, u32[]{:S(2)}) collective-permute-start(bf16[8,1,2,128,128]{4,3,2,1,0:T(8,128)(2,1)S(1)} %all_to_all.61.own_ref), channel_id=1, source_target_pairs={{0,8},{8,16},{16,24},{24,32},{32,40},{40,48},{48,56},{56,64},{64,7... | collective-permute-start | bytes 1572872 | tf_op jit(solution)/shard_map/ppermute | solution.py:199
  88.7 20.5 %copy-start.14 = (bf16[8,1,2,128,128]{4,3,2,1,0:T(8,128)(2,1)}, bf16[8,1,2,128,128]{4,3,2,1,0:T(8,128)(2,1)S(1)}, u32[]{:S(2)}) copy-start(bf16[8,1,2,128,128]{4,3,2,1,0:T(8,128)(2,1)S(1)} %all-to-all-done.6.qg_ref) | copy-start | bytes 1572868
  88.7 38.7 %all-to-all-start.1 = ((bf16[8,1,2,128,128]{4,3,2,1,0:T(8,128)(2,1)}), bf16[8,1,2,128,128]{4,3,2,1,0:T(8,128)(2,1)S(1)}, u32[]{:S(2)}, u32[]{:S(2)}) async-start(bf16[8,1,2,128,128]{4,3,2,1,0:T(8,128)(2,1)} %get-tuple-element.27), calls=%async_computation.1 | async-start | bytes 1048576 | tf_op jit(solution)/shard_map/all_to_all | solution.py:193
  92.2 7.3 %collective-permute-start.1 = (s32[1024]{0:T(1024)S(1)}, s32[1024]{0:T(1024)S(1)}, u32[]{:S(2)}, u32[]{:S(2)}) collective-permute-start(s32[1024]{0:T(1024)S(1)} %bitcast.6), channel_id=1, source_target_pairs={{8,0},{16,8},{24,16},{32,24},{40,32},{48,40},{56,48},{64,56},{72,6... | collective-permute-start | bytes 12296 | tf_op jit(solution)/shard_map/ppermute | solution.py:199
  99.6 7.9 %collective-permute-start = (s32[1024]{0:T(1024)S(1)}, s32[1024]{0:T(1024)S(1)}, u32[]{:S(2)}, u32[]{:S(2)}) collective-permute-start(s32[1024]{0:T(1024)S(1)} %bitcast.7), channel_id=1, source_target_pairs={{0,8},{8,16},{16,24},{24,32},{32,40},{40,48},{48,56},{56,64},{64,7... | collective-permute-start | bytes 12296 | tf_op jit(solution)/shard_map/ppermute | solution.py:199
  127.4 30.6 %copy-start.12 = (bf16[8,1,2,128,128]{4,3,2,1,0:T(8,128)(2,1)}, bf16[8,1,2,128,128]{4,3,2,1,0:T(8,128)(2,1)S(1)}, u32[]{:S(2)}) copy-start(bf16[8,1,2,128,128]{4,3,2,1,0:T(8,128)(2,1)S(1)} %all-to-all-done.1.own_ref) | copy-start | bytes 1572868
  127.4 30.6 %all-to-all-start.8 = ((bf16[8,1,2,128,128]{4,3,2,1,0:T(8,128)(2,1)}), bf16[8,1,2,128,128]{4,3,2,1,0:T(8,128)(2,1)S(1)}, u32[]{:S(2)}, u32[]{:S(2)}) async-start(bf16[8,1,2,128,128]{4,3,2,1,0:T(8,128)(2,1)} %get-tuple-element.34), calls=%async_computation.8 | async-start | bytes 1048576 | tf_op jit(solution)/shard_map/all_to_all | solution.py:193
  132.1 38.8 %collective-permute-start.3 = (bf16[8,1,2,128,128]{4,3,2,1,0:T(8,128)(2,1)S(1)}, bf16[8,1,2,128,128]{4,3,2,1,0:T(8,128)(2,1)}, u32[]{:S(2)}, u32[]{:S(2)}) collective-permute-start(bf16[8,1,2,128,128]{4,3,2,1,0:T(8,128)(2,1)S(1)} %all-to-all-done.1.own_ref), channel_id=1, source_target_pairs={{8,0},{16,8},{24,16},{32,24},{40,32},{48,40},{56,48},{64,56},{72,6... | collective-permute-start | bytes 1572872 | tf_op jit(solution)/shard_map/ppermute | solution.py:199
  136.1 34.9 %collective-permute-start.2 = (bf16[8,1,2,128,128]{4,3,2,1,0:T(8,128)(2,1)S(1)}, bf16[8,1,2,128,128]{4,3,2,1,0:T(8,128)(2,1)}, u32[]{:S(2)}, u32[]{:S(2)}) collective-permute-start(bf16[8,1,2,128,128]{4,3,2,1,0:T(8,128)(2,1)S(1)} %all-to-all-done.1.own_ref), channel_id=1, source_target_pairs={{0,8},{8,16},{16,24},{24,32},{32,40},{40,48},{48,56},{56,64},{64,7... | collective-permute-start | bytes 1572872 | tf_op jit(solution)/shard_map/ppermute | solution.py:199
  138.0 0.8 copy-start.16
  138.8 0.8 copy-start.17
  158.0 31.3 %copy-start = (bf16[8,1,2,128,128]{4,3,2,1,0:T(8,128)(2,1)}, bf16[8,1,2,128,128]{4,3,2,1,0:T(8,128)(2,1)S(1)}, u32[]{:S(2)}) copy-start(bf16[8,1,2,128,128]{4,3,2,1,0:T(8,128)(2,1)S(1)} %all-to-all-done.8.refs_2_) | copy-start | bytes 1572868
  158.0 31.3 %all-to-all-start.5 = ((bf16[8,1,2,128,128]{4,3,2,1,0:T(8,128)(2,1)}), bf16[8,1,2,128,128]{4,3,2,1,0:T(8,128)(2,1)S(1)}, u32[]{:S(2)}, u32[]{:S(2)}) async-start(bf16[8,1,2,128,128]{4,3,2,1,0:T(8,128)(2,1)} %get-tuple-element.31), calls=%async_computation.5 | async-start | bytes 1048576 | tf_op jit(solution)/shard_map/all_to_all | solution.py:193
  162.8 39.4 %collective-permute-start.12 = (bf16[8,1,2,128,128]{4,3,2,1,0:T(8,128)(2,1)}, bf16[8,1,2,128,128]{4,3,2,1,0:T(8,128)(2,1)S(1)}, u32[]{:S(2)}, u32[]{:S(2)}) collective-permute-start(bf16[8,1,2,128,128]{4,3,2,1,0:T(8,128)(2,1)} %get-tuple-element.44), channel_id=1, source_target_pairs={{8,0},{16,8},{24,16},{32,24},{40,32},{48,40},{56,48},{64,56},{72,6... | collective-permute-start | bytes 1572872 | tf_op jit(solution)/shard_map/ppermute | solution.py:199
  168.8 33.4 %collective-permute-start.13 = (bf16[8,1,2,128,128]{4,3,2,1,0:T(8,128)(2,1)}, bf16[8,1,2,128,128]{4,3,2,1,0:T(8,128)(2,1)}, u32[]{:S(2)}, u32[]{:S(2)}) collective-permute-start(bf16[8,1,2,128,128]{4,3,2,1,0:T(8,128)(2,1)} %get-tuple-element.45), channel_id=1, source_target_pairs={{0,8},{8,16},{16,24},{24,32},{32,40},{40,48},{48,56},{56,64},{64,7... | collective-permute-start | bytes 1572872 | tf_op jit(solution)/shard_map/ppermute | solution.py:199
  189.3 13.7 %copy-start.6 = (f32[8,1,2,128,128]{4,3,2,1,0:T(8,128)S(1)}, f32[8,1,2,128,128]{4,3,2,1,0:T(8,128)}, u32[]{:S(2)}) copy-start(f32[8,1,2,128,128]{4,3,2,1,0:T(8,128)} %get-tuple-element.43) | copy-start | bytes 3145732
  189.3 16.0 %copy-start.1 = (bf16[8,1,2,128,128]{4,3,2,1,0:T(8,128)(2,1)}, bf16[8,1,2,128,128]{4,3,2,1,0:T(8,128)(2,1)S(1)}, u32[]{:S(2)}) copy-start(bf16[8,1,2,128,128]{4,3,2,1,0:T(8,128)(2,1)S(1)} %all-to-all-done.5.refs_1_) | copy-start | bytes 1572868
  189.3 16.0 %all-to-all-start.2 = ((bf16[8,1,2,128,128]{4,3,2,1,0:T(8,128)(2,1)}), bf16[8,1,2,128,128]{4,3,2,1,0:T(8,128)(2,1)S(1)}, u32[]{:S(2)}, u32[]{:S(2)}) async-start(bf16[8,1,2,128,128]{4,3,2,1,0:T(8,128)(2,1)} %get-tuple-element.28), calls=%async_computation.2 | async-start | bytes 1048576 | tf_op jit(solution)/shard_map/all_to_all | solution.py:193
  194.3 23.8 %collective-permute-start.10 = (bf16[8,1,2,128,128]{4,3,2,1,0:T(8,128)(2,1)}, bf16[8,1,2,128,128]{4,3,2,1,0:T(8,128)(2,1)}, u32[]{:S(2)}, u32[]{:S(2)}) collective-permute-start(bf16[8,1,2,128,128]{4,3,2,1,0:T(8,128)(2,1)} %get-tuple-element.41), channel_id=1, source_target_pairs={{8,0},{16,8},{24,16},{32,24},{40,32},{48,40},{56,48},{64,56},{72,6... | collective-permute-start | bytes 1572872 | tf_op jit(solution)/shard_map/ppermute | solution.py:199
  200.3 18.4 %collective-permute-start.11 = (bf16[8,1,2,128,128]{4,3,2,1,0:T(8,128)(2,1)}, bf16[8,1,2,128,128]{4,3,2,1,0:T(8,128)(2,1)}, u32[]{:S(2)}, u32[]{:S(2)}) collective-permute-start(bf16[8,1,2,128,128]{4,3,2,1,0:T(8,128)(2,1)} %get-tuple-element.42), channel_id=1, source_target_pairs={{0,8},{8,16},{16,24},{24,32},{32,40},{40,48},{48,56},{56,64},{64,7... | collective-permute-start | bytes 1572872 | tf_op jit(solution)/shard_map/ppermute | solution.py:199
  202.2 0.8 copy-start.9
  203.0 15.6 %copy-start.7 = (f32[8,1,2,128,128]{4,3,2,1,0:T(8,128)S(1)}, f32[8,1,2,128,128]{4,3,2,1,0:T(8,128)}, u32[]{:S(2)}) copy-start(f32[8,1,2,128,128]{4,3,2,1,0:T(8,128)} %get-tuple-element.40) | copy-start | bytes 3145732
  205.3 15.6 %copy-start.2 = (bf16[8,1,2,128,128]{4,3,2,1,0:T(8,128)(2,1)}, bf16[8,1,2,128,128]{4,3,2,1,0:T(8,128)(2,1)S(1)}, u32[]{:S(2)}) copy-start(bf16[8,1,2,128,128]{4,3,2,1,0:T(8,128)(2,1)S(1)} %all-to-all-done.2.refs_0_) | copy-start | bytes 1572868
  205.3 15.6 %all-to-all-start.11 = ((bf16[8,1,2,128,128]{4,3,2,1,0:T(8,128)(2,1)}), bf16[8,1,2,128,128]{4,3,2,1,0:T(8,128)(2,1)S(1)}, u32[]{:S(2)}, u32[]{:S(2)}) async-start(bf16[8,1,2,128,128]{4,3,2,1,0:T(8,128)(2,1)} %add_convert_fusion), calls=%async_computation.11 | async-start | bytes 1048576 | tf_op jit(solution)/shard_map/all_to_all | solution.py:193
  210.1 18.2 %collective-permute-start.8 = (bf16[8,1,2,128,128]{4,3,2,1,0:T(8,128)(2,1)}, bf16[8,1,2,128,128]{4,3,2,1,0:T(8,128)(2,1)}, u32[]{:S(2)}, u32[]{:S(2)}) collective-permute-start(bf16[8,1,2,128,128]{4,3,2,1,0:T(8,128)(2,1)} %get-tuple-element.38), channel_id=1, source_target_pairs={{8,0},{16,8},{24,16},{32,24},{40,32},{48,40},{56,48},{64,56},{72,6... | collective-permute-start | bytes 1572872 | tf_op jit(solution)/shard_map/ppermute | solution.py:199
  216.2 18.4 %collective-permute-start.9 = (bf16[8,1,2,128,128]{4,3,2,1,0:T(8,128)(2,1)}, bf16[8,1,2,128,128]{4,3,2,1,0:T(8,128)(2,1)}, u32[]{:S(2)}, u32[]{:S(2)}) collective-permute-start(bf16[8,1,2,128,128]{4,3,2,1,0:T(8,128)(2,1)} %get-tuple-element.39), channel_id=1, source_target_pairs={{0,8},{8,16},{16,24},{24,32},{32,40},{40,48},{48,56},{56,64},{64,7... | collective-permute-start | bytes 1572872 | tf_op jit(solution)/shard_map/ppermute | solution.py:199
  218.7 15.9 %copy-start.8 = (f32[8,1,2,128,128]{4,3,2,1,0:T(8,128)S(1)}, f32[8,1,2,128,128]{4,3,2,1,0:T(8,128)}, u32[]{:S(2)}) copy-start(f32[8,1,2,128,128]{4,3,2,1,0:T(8,128)} %get-tuple-element.37) | copy-start | bytes 3145732
  220.9 15.8 %copy-start.3 = (bf16[8,1,2,128,128]{4,3,2,1,0:T(8,128)(2,1)}, bf16[8,1,2,128,128]{4,3,2,1,0:T(8,128)(2,1)S(1)}, u32[]{:S(2)}) copy-start(bf16[8,1,2,128,128]{4,3,2,1,0:T(8,128)(2,1)S(1)} %all-to-all-done.11.refs_2_) | copy-start | bytes 1572868
  220.9 15.8 %all-to-all-start.10 = ((bf16[8,1,2,128,128]{4,3,2,1,0:T(8,128)(2,1)}), bf16[8,1,2,128,128]{4,3,2,1,0:T(8,128)(2,1)S(1)}, u32[]{:S(2)}, u32[]{:S(2)}) async-start(bf16[8,1,2,128,128]{4,3,2,1,0:T(8,128)(2,1)} %add_convert_fusion.1), calls=%async_computation.10 | async-start | bytes 1048576 | tf_op jit(solution)/shard_map/all_to_all | solution.py:193
  236.7 14.8 %copy-start.4 = (bf16[8,1,2,128,128]{4,3,2,1,0:T(8,128)(2,1)}, bf16[8,1,2,128,128]{4,3,2,1,0:T(8,128)(2,1)S(1)}, u32[]{:S(2)}) copy-start(bf16[8,1,2,128,128]{4,3,2,1,0:T(8,128)(2,1)S(1)} %all-to-all-done.10.refs_1_) | copy-start | bytes 1572868
  236.7 14.8 %all-to-all-start.9 = ((bf16[8,1,2,128,128]{4,3,2,1,0:T(8,128)(2,1)}), bf16[8,1,2,128,128]{4,3,2,1,0:T(8,128)(2,1)S(1)}, u32[]{:S(2)}, u32[]{:S(2)}) async-start(bf16[8,1,2,128,128]{4,3,2,1,0:T(8,128)(2,1)} %add_convert_fusion.2), calls=%async_computation.9 | async-start | bytes 1048576 | tf_op jit(solution)/shard_map/all_to_all | solution.py:193
  251.6 0.8 copy-start.5

commit v2 on v1

v2 whole, which is shorter than its diff:
```python
import functools
import math

import jax
import jax.numpy as jnp
from jax import lax
from jax.experimental import pallas as pl
from jax.experimental.pallas import tpu as pltpu
from jax.sharding import Mesh
from jax.sharding import PartitionSpec as P

DH = 128
SHARD_MS = 625
RADIUS_MS = 1000
NEG_FILL = -1e30
FAR = -1e6
SCALE = DH ** (-0.5)
LOG2E = 1.4426950408889634
GROUP = ("yh", "head")
CHUNKS = ((0, 1), (2,))
STAMP_ROWS = 16
STAMP_BASE = 32
RANGES = 2
UNROLL = True
REACH = 2
VMEM_BYTES = 56 * 1024 * 1024


def dot(lhs, rhs, dims):
    return lax.dot_general(lhs, rhs, (dims, ((), ())), preferred_element_type=jnp.float32)


def dot_nn(lhs, rhs):
    return dot(lhs, rhs, ((1,), (0,)))


def dot_nt(lhs, rhs):
    return dot(lhs, rhs, ((1,), (1,)))


def pack_kernel(peers, heads, plans, stamped, count, *refs):
    ins, outs = refs[:count], refs[count + stamped :]
    rows = ins[0].shape[0]
    for number, (out, plan) in enumerate(zip(outs, plans)):
        for peer in range(peers):
            for at, (which, head) in enumerate(plan):
                lanes = pl.ds((peer * heads + head) * DH, DH)
                out[peer, pl.ds(at * rows, rows)] = ins[which][:, lanes]
            if stamped and number == 0:
                out[peer, pl.ds(len(plan) * rows, STAMP_ROWS)] = refs[count][...]


def pack(arrays, plans, peers, stamp_rows=None):
    rows, width = arrays[0].shape
    stamps = [] if stamp_rows is None else [stamp_rows]
    extra = [STAMP_ROWS if stamps and number == 0 else 0 for number in range(len(plans))]
    return pl.pallas_call(
        functools.partial(
            pack_kernel, peers, width // DH // peers, plans, len(stamps), len(arrays)
        ),
        out_shape=[
            jax.ShapeDtypeStruct((peers, len(plan) * rows + more, DH), arrays[0].dtype)
            for plan, more in zip(plans, extra)
        ],
        compiler_params=pltpu.CompilerParams(vmem_limit_bytes=VMEM_BYTES),
        name="pack",
    )(*arrays, *stamps)


def place_kernel(peers, heads, chunk, offsets, *refs):
    count = len(offsets)
    pieces, outs, sems = refs[:count], refs[-2 * count - 1 : -1], refs[-1]
    rows = outs[0].shape[0]
    copies = []
    for piece, offset, pair in zip(pieces, offsets, zip(outs[::2], outs[1::2])):
        for peer in range(peers):
            for place, head in enumerate(chunk):
                lanes = pl.ds((peer * heads + head) * DH, DH)
                for which, out in enumerate(pair):
                    start = offset + (2 * place + which) * rows
                    copies.append(
                        pltpu.make_async_copy(
                            piece.at[peer, pl.ds(start, rows)],
                            out.at[:, lanes],
                            sems.at[len(copies)],
                        )
                    )
    for copy in copies:
        copy.start()
    for copy in copies:
        copy.wait()


def place(pieces, offsets, chunk, heads, rows, outs):
    peers = pieces[0].shape[0]
    shape = jax.ShapeDtypeStruct((rows, peers * heads * DH), pieces[0].dtype)
    number = 2 * len(pieces)
    anywhere = pl.BlockSpec(memory_space=pl.ANY)
    return pl.pallas_call(
        functools.partial(place_kernel, peers, heads, chunk, offsets),
        in_specs=[pl.BlockSpec(memory_space=pltpu.VMEM)] * len(pieces) + [anywhere] * len(outs),
        out_specs=[anywhere] * number,
        out_shape=[shape] * number,
        input_output_aliases={len(pieces) + at: at for at in range(len(outs))},
        scratch_shapes=[pltpu.SemaphoreType.DMA((number * peers * len(chunk),))],
        compiler_params=pltpu.CompilerParams(vmem_limit_bytes=VMEM_BYTES),
        name="place",
    )(*pieces, *outs)


def spread_stamps(codes, shift):
    size = codes.shape[1]
    place = lax.broadcasted_iota(jnp.int32, (size, size), 0)
    diagonal = place == lax.broadcasted_iota(jnp.int32, (size, size), 1)
    ones = jnp.ones((size, size), jnp.bfloat16)
    found = [
        dot_nn(jnp.where(diagonal, codes[row : row + 1].astype(jnp.float32), 0.0).astype(jnp.bfloat16), ones)
        for row in range(2)
    ]
    code = found[0] * STAMP_BASE + found[1]
    return jnp.where(code > 0.5, code + (shift - 1), FAR)


def attend_kernel(
    per, size, fresh,
    stamps_left, stamps_own, stamps_right, qg_ref, left_ref, own_ref, right_ref, *refs
):
    skip = 4 - sum(fresh)
    result_ref, to_left_ref, own_sum_ref, to_right_ref = refs[skip : skip + 4]
    (
        stamps, keys, values, keys_t, values_t,
        scores, grad_weights, key_sums, value_sums, total_t, query_t,
    ) = refs[skip + 4 :]
    rows = size // per
    span = 2 * REACH + 1

    @pl.when(pl.program_id(0) == 0)
    def _():
        for side, ref in enumerate((stamps_left, stamps_own, stamps_right)):
            for block in range(RANGES * per):
                place = side * RANGES + block // per
                spread = spread_stamps(ref[block], (place - RANGES) * SHARD_MS)
                stamps[place, pl.ds(block % per * rows, rows)] = spread

    for side, ref in enumerate((left_ref, own_ref, right_ref)):
        for part in range(RANGES):
            place = side * RANGES + part
            blocks = pl.ds(part * per, per)
            key_tile = ref[blocks, pl.ds(0, rows)].reshape(size, DH)
            value_tile = ref[blocks, pl.ds(rows, rows)].reshape(size, DH)
            keys[place] = key_tile
            values[place] = value_tile
            keys_t[place] = key_tile.T
            values_t[place] = value_tile.T
    key_sums[...] = jnp.zeros_like(key_sums)
    value_sums[...] = jnp.zeros_like(value_sums)
    total_t[...] = jnp.zeros_like(total_t)
    query_t[...] = jnp.zeros_like(query_t)
    offsets = lax.broadcasted_iota(jnp.int32, (1, size), 1) * SHARD_MS // size
    blocks = [pl.ds(part * per, per) for part in range(RANGES)]
    query = [qg_ref[block, pl.ds(0, rows)].reshape(size, DH) for block in blocks]
    grad = [qg_ref[block, pl.ds(rows, rows)].reshape(size, DH) for block in blocks]
    stamp = [(offsets + part * SHARD_MS).astype(jnp.float32) for part in range(RANGES)]
    top, inverse, row_dot = [None] * RANGES, [None] * RANGES, [None] * RANGES

    def score_step(part, step, top):
        place = step + part
        found = dot_nt(keys[place], query[part])
        near = jnp.abs(jnp.tile(stamps[place], (1, size // DH)) - stamp[part]) <= RADIUS_MS
        found = jnp.where(near, found * (SCALE * LOG2E), NEG_FILL)
        scores[part, step] = found
        return jnp.maximum(top, jnp.max(found.reshape(size // 8, 8, size), axis=0))

    def weight_step(part, step, total):
        place = step + part
        raised = jnp.exp2(scores[part, step] - top[part])
        scores[part, step] = raised
        total_t[part] += dot_nn(values_t[place], raised.astype(jnp.bfloat16))
        return total + jnp.sum(raised.reshape(size // 8, 8, size), axis=0)

    def grad_step(part, step):
        place = step + part
        weights = scores[part, step] * inverse[part]
        slopes = (weights * (dot_nt(values[place], grad[part]) - row_dot[part])).astype(jnp.bfloat16)
        value_sums[place] += dot_nn(weights.astype(jnp.bfloat16), grad[part])
        key_sums[place] += dot_nn(slopes, query[part])
        query_t[part] += dot_nn(keys_t[place], slopes)

    def finish(part, total):
        inverse[part] = 1.0 / jnp.sum(total, axis=0, keepdims=True)
        attended_t = total_t[part] * inverse[part]
        row_dot[part] = jnp.sum(
            attended_t * grad[part].astype(jnp.float32).T, axis=0, keepdims=True
        )
        shape = (per, rows, DH)
        result_ref[blocks[part], pl.ds(0, rows)] = attended_t.T.astype(jnp.bfloat16).reshape(shape)

    def finish_query(part):
        low = (query_t[part] * SCALE).T.astype(jnp.bfloat16)
        result_ref[blocks[part], pl.ds(rows, rows)] = low.reshape(per, rows, DH)

    lowest = jnp.full((8, size), NEG_FILL, jnp.float32)
    zero = jnp.zeros((8, size), jnp.float32)
    found = lax.fori_loop(0, span, lambda step, c: score_step(0, step, c), lowest, unroll=UNROLL)
    top[0] = jnp.max(found, axis=0, keepdims=True)

    def second(step, carry):
        return weight_step(0, step, carry[0]), score_step(1, step, carry[1])

    total, found = lax.fori_loop(0, span, second, (zero, lowest), unroll=UNROLL)
    top[1] = jnp.max(found, axis=0, keepdims=True)
    finish(0, total)

    def third(step, carry):
        grad_step(0, step)
        return weight_step(1, step, carry)

    total = lax.fori_loop(0, span, third, zero, unroll=UNROLL)
    finish_query(0)
    finish(1, total)

    def fourth(step, carry):
        grad_step(1, step)
        return carry

    lax.fori_loop(0, span, fourth, 0, unroll=UNROLL)
    finish_query(1)
    for side, ref in enumerate((to_left_ref, own_sum_ref, to_right_ref)):
        for part in range(RANGES):
            place = side * RANGES + part
            shape = (per, rows, DH)
            ref[blocks[part], pl.ds(0, rows)] = (key_sums[place] * SCALE).astype(ref.dtype).reshape(shape)
            ref[blocks[part], pl.ds(rows, rows)] = value_sums[place].astype(ref.dtype).reshape(shape)


def attend(heads, stamped, query_grad, sides, result, sums, sizes):
    peers = stamped[0].shape[0]
    per = peers // RANGES
    rows = (stamped[0].shape[1] - STAMP_ROWS) // (2 * len(CHUNKS[0]))
    size = per * rows
    span = 2 * REACH + 1
    places = 3 * RANGES

    def piece(first):
        start = heads[0] - first
        return pl.BlockSpec((peers, 2 * rows, DH), lambda head: (0, start + head, 0))

    stamp_block = 2 * len(CHUNKS[0]) * rows // STAMP_ROWS
    stamp_spec = pl.BlockSpec((peers, STAMP_ROWS, DH), lambda head: (0, stamp_block, 0))
    old = [result[0], *sums[0]]
    firsts = [result[1]] + [sums[1]] * 3
    kinds = [jnp.bfloat16] * 4
    counts = [sizes[0]] + [sizes[1]] * 3
    fresh = [value is None for value in old]
    operands = [*stamped, query_grad[0], *sides[0]]
    in_specs = [stamp_spec] * 3 + [piece(first) for first in (query_grad[1], *sides[1])]
    aliases = {}
    for number, value in enumerate(old):
        if value is not None:
            aliases[len(operands)] = number
            operands.append(value)
            in_specs.append(pl.BlockSpec(memory_space=pl.ANY))

    return pl.pallas_call(
        functools.partial(attend_kernel, per, size, fresh),
        grid=(len(heads),),
        in_specs=in_specs,
        out_specs=[piece(first) for first in firsts],
        out_shape=[
            jax.ShapeDtypeStruct((peers, 2 * rows * count, DH), kind)
            for count, kind in zip(counts, kinds)
        ],
        input_output_aliases=aliases,
        scratch_shapes=[
            pltpu.VMEM((places, size, DH), jnp.float32),
            pltpu.VMEM((places, size, DH), jnp.bfloat16),
            pltpu.VMEM((places, size, DH), jnp.bfloat16),
            pltpu.VMEM((places, DH, size), jnp.bfloat16),
            pltpu.VMEM((places, DH, size), jnp.bfloat16),
            pltpu.VMEM((RANGES, span, size, size), jnp.float32),
            pltpu.VMEM((RANGES, span, size, size), jnp.float32),
            pltpu.VMEM((places, size, DH), jnp.float32),
            pltpu.VMEM((places, size, DH), jnp.float32),
            pltpu.VMEM((RANGES, DH, size), jnp.float32),
            pltpu.VMEM((RANGES, DH, size), jnp.float32),
        ],
        compiler_params=pltpu.CompilerParams(vmem_limit_bytes=VMEM_BYTES),
        cost_estimate=pl.CostEstimate(
            flops=1, bytes_accessed=1, transcendentals=0
        ),
        name="attend",
    )(*operands)


def swap(value):
    return lax.all_to_all(value, GROUP, split_axis=0, concat_axis=0, tiled=True)


def shifted(value, steps):
    count = lax.axis_size("col")
    first, last = max(0, -steps), min(count, count - steps)
    return lax.ppermute(value, "col", [(at, at + steps) for at in range(first, last)])


def stamp_codes(audio_time):
    place = lax.axis_index("col") * RANGES + lax.axis_index("yh")
    code = jnp.where(audio_time >= 0, audio_time - place * SHARD_MS + 1, 0)
    pair = jnp.stack([code // STAMP_BASE, code % STAMP_BASE]).astype(jnp.bfloat16)
    return jnp.pad(pair, ((0, STAMP_ROWS - 2), (0, 0)))


def after(value, *others):
    return lax.optimization_barrier((value, others))[0]


def on_device(video_query, audio_key, audio_value, grad_out, audio_time):
    peers = lax.axis_size(GROUP)
    rows, width = video_query.shape
    heads = width // DH // peers
    early, late = CHUNKS
    key_plan = [(which, head) for head in early for which in (0, 1)]
    rest_plan = [(which, head) for head in early for which in (2, 3)]
    rest_plan += [(which, head) for head in late for which in (0, 1)]
    rest_plan += [(which, head) for head in late for which in (2, 3)]
    arrays = (audio_key, audio_value, video_query, grad_out)
    (key_pack,) = pack(arrays[:2], [key_plan], peers, stamp_codes(audio_time))
    own = swap(key_pack)
    left, right = shifted(own, 1), shifted(own, -1)
    (rest_pack,) = pack(arrays, [rest_plan], peers)
    rest = swap(after(rest_pack, own))
    late_rows = slice(2 * len(early) * rows, 2 * heads * rows)
    sent = after(rest[:, late_rows], left, right)
    late_left, late_right = shifted(sent, 1), shifted(sent, -1)

    def run(chunk, sides, firsts):
        return attend(
            chunk,
            (left, own, right),
            (rest, chunk[0] - firsts[0]),
            (sides, [chunk[0] - first for first in firsts[1:]]),
            (None, chunk[0]),
            ([None] * 3, chunk[0]),
            (len(chunk), len(chunk)),
        )

    def gather(sums, came):
        return sum(value.astype(jnp.float32) for value in (sums[1], *came)).astype(jnp.bfloat16)

    result, *sums = run(early, (left, own, right), (0, 0, 0, 0))
    to_left, to_right = after((sums[0], sums[2]), late_left, late_right)
    came = shifted(to_left, -1), shifted(to_right, 1)
    result = swap(result)
    last_result, *last_sums = run(late, (late_left, rest, late_right), (heads, 0, len(early), 0))
    to_left, to_right = after((last_sums[0], last_sums[2]), came)
    last_came = shifted(to_left, -1), shifted(to_right, 1)
    grads = swap(after(gather(sums, came), result))
    outs = place((result, grads), (0, 0), early, heads, rows, ())
    last = jnp.concatenate([last_result, gather(last_sums, last_came)], axis=1)
    last = swap(after(last, grads))
    offsets = (0, 2 * len(late) * rows)
    return tuple(place((last, last), offsets, late, heads, rows, outs))


def solution(mesh):
    columns = mesh.shape["seq"] // RANGES
    split = Mesh(
        mesh.devices.reshape(columns, RANGES, mesh.shape["head"]), ("col", "yh", "head")
    )
    rows = P(("col", "yh", "head"), None)
    return jax.shard_map(
        on_device,
        mesh=split,
        in_specs=(rows, rows, rows, rows, P(("col", "yh", "head"))),
        out_specs=(rows, rows, rows, rows),
        check_vma=False,
    )
```

time: 257 us -> 177 us (0.69)
  blocking collectives: 53.5 us -> 0 us
  starting transfers between devices: 90.9 us -> 44.5 us
  waiting for transfers between devices: 31.9 us -> 75.3 us
  Pallas kernels: 66.3 us -> 48.4 us
  local copies, waits for them, and re-layouts: 4.84 us -> 1.82 us
    all_to_all x3 -> x0, blocking collectives: 42.7 us -> none  [swap(): return lax.all_to_all(value, GROUP, split_axis=0, concat_axis=0, tiled=True)]
    all_to_all x9 -> x5, waiting for transfers between devices: 14.9 us -> 53.1 us  [swap(): return lax.all_to_all(value, GROUP, split_axis=0, concat_axis=0, tiled=True)]
    ppermute x14 -> x8, starting transfers between devices: 52.2 us -> 24.1 us  [shifted(): lax.ppermute(value, 'col', [(at, at + steps) for at in range(first, last)])]
    all_to_all x9 -> x5, starting transfers between devices: 38.7 us -> 20.5 us  [swap(): return lax.all_to_all(value, GROUP, split_axis=0, concat_axis=0, tiled=True)]
    pallas_call x7 -> x6, Pallas kernels: 66.3 us -> 48.4 us  [the longest x2 36.1 us: attend(): pl.pallas_call(functools.partial(attend_kernel, per, size, fresh), grid=(...]
    all_gather x1 -> x0, blocking collectives: 10.9 us -> none  [on_device(): lifted = lax.all_gather(audio_time, GROUP, axis=0, tiled=True) + 1]
    ppermute x14 -> x8, waiting for transfers between devices: 17 us -> 22.1 us  [shifted(): lax.ppermute(value, 'col', [(at, at + steps) for at in range(first, last)])]
    convert_element_type x3 -> x2, other arithmetic: 6.74 us -> 2.78 us  [gather(): sum((value.astype(jnp.float32) for value in (sums[1], *came)))]
  transfers between devices with their start and end apart: 23 -> 13, of which waited for: 7 -> 10; matrix products, arithmetic and copies ran while one was open for 3% -> 2% of each run, Pallas kernels for 24% -> 24%
where the time goes in v2:
time: 177 us; the launch traced here: 176 us
  waiting for transfers between devices  75.3 us (43%)
  Pallas kernels  48.4 us (27%)
  starting transfers between devices  44.5 us (25%)
  other arithmetic  5.13 us (3%)
  local copies, waits for them, and re-layouts  1.82 us (1%)
    all_to_all x5, waiting for transfers between devices, swap(): return lax.all_to_all(value, GROUP, split_axis=0, concat_axis=0, tiled=True)  53.1 us
    pallas_call x2, Pallas kernels, attend(): pl.pallas_call(functools.partial(attend_kernel, per, size, fresh), grid=(...  36.1 us
    ppermute x8, starting transfers between devices, shifted(): lax.ppermute(value, 'col', [(at, at + steps) for at in range(first, last)])  24.1 us
    ppermute x8, waiting for transfers between devices, shifted(): lax.ppermute(value, 'col', [(at, at + steps) for at in range(first, last)])  22.1 us
    all_to_all x5, starting transfers between devices, swap(): return lax.all_to_all(value, GROUP, split_axis=0, concat_axis=0, tiled=True)  20.5 us
    pallas_call x2, Pallas kernels, place(): pl.pallas_call(functools.partial(place_kernel, peers, heads, chunk, offse...  6.21 us
    pallas_call x2, Pallas kernels, pack(): pl.pallas_call(functools.partial(pack_kernel, peers, width // DH // peers...  6.11 us
  transfers between devices with their start and end apart: 13, of which 10 were waited for; matrix products, arithmetic and copies ran while one was open for 2% of the time, Pallas kernels for 24%

profile of v2, /device:TPU:96, one launch (start us, length us, event | category | flops | bytes accessed | tf_op | source)
XLA Modules:
  0.0 176.2 jit_solution(5199802106203067297)
XLA Ops:
  0.6 0.7 convert_bitcast_fusion
  1.3 0.6 fusion.2.refs_2_
  1.9 2.6 %pack.2 = bf16[8,528,128]{2,1,0:T(8,128)(2,1)} custom-call(bf16[128,3072]{1,0:T(8,128)(2,1)} %refs_0_.3, bf16[128,3072]{1,0:T(8,128)(2,1)} %refs_1_.3, bf16[16,128]{1,0:T(8,128)(2,1)} %fusion.2.refs_2_), custom_call_target="tpu_custom_call" | custom-call | tf_op jit(solution)/shard_map/pack/pallas_call | solution.py:57
  4.5 4.5 %all-to-all-start = ((bf16[8,528,128]{2,1,0:T(8,128)(2,1)}), bf16[8,528,128]{2,1,0:T(8,128)(2,1)S(1)}, u32[]{:S(2)}, u32[]{:S(2)}) async-start(bf16[8,528,128]{2,1,0:T(8,128)(2,1)} %pack.2), calls=%async_computation | async-start | bytes 2162688 | tf_op jit(solution)/shard_map/all_to_all | solution.py:296
  8.9 3.6 %pack.3 = bf16[8,1024,128]{2,1,0:T(8,128)(2,1)} custom-call(bf16[128,3072]{1,0:T(8,128)(2,1)} %refs_0_.3, bf16[128,3072]{1,0:T(8,128)(2,1)} %refs_1_.3, bf16[128,3072]{1,0:T(8,128)(2,1)} %refs_2_.1, bf16[128,3072]{1,0:T(8,128)(2,1)} %refs_3_.1), custom_call_target="tpu_custom_call" | custom-call | tf_op jit(solution)/shard_map/pack/pallas_call | solution.py:57
  12.5 12.8 %all-to-all-done.stamps_own.own_ref = bf16[8,528,128]{2,1,0:T(8,128)(2,1)S(1)} async-done(((bf16[8,528,128]{2,1,0:T(8,128)(2,1)}), bf16[8,528,128]{2,1,0:T(8,128)(2,1)S(1)}, u32[]{:S(2)}, u32[]{:S(2)}) %all-to-all-start) | async-done | bytes 1081376 | tf_op jit(solution)/shard_map/all_to_all | solution.py:296
  25.3 0.0 copy-start.1
  25.3 3.6 %all-to-all-start.1 = ((bf16[8,1024,128]{2,1,0:T(8,128)(2,1)}), bf16[8,1024,128]{2,1,0:T(8,128)(2,1)S(1)}, u32[]{:S(2)}, u32[]{:S(2)}) async-start(bf16[8,1024,128]{2,1,0:T(8,128)(2,1)} %pack.3), calls=%async_computation.1 | async-start | bytes 4194304 | tf_op jit(solution)/shard_map/all_to_all | solution.py:296
  28.9 4.5 %collective-permute-start.1 = (bf16[8,528,128]{2,1,0:T(8,128)(2,1)S(1)}, bf16[8,528,128]{2,1,0:T(8,128)(2,1)}, u32[]{:S(2)}, u32[]{:S(2)}) collective-permute-start(bf16[8,528,128]{2,1,0:T(8,128)(2,1)S(1)} %all-to-all-done.stamps_own.own_ref), channel_id=1, source_target_pairs={{8,0},{16,8},{24,16},{32,24},{40,32},{48,40},{56,48},{64,56},{72,6... | collective-permute-start | bytes 3244040 | tf_op jit(solution)/shard_map/ppermute | solution.py:302
  33.4 1.9 %collective-permute-start = (bf16[8,528,128]{2,1,0:T(8,128)(2,1)S(1)}, bf16[8,528,128]{2,1,0:T(8,128)(2,1)}, u32[]{:S(2)}, u32[]{:S(2)}) collective-permute-start(bf16[8,528,128]{2,1,0:T(8,128)(2,1)S(1)} %all-to-all-done.stamps_own.own_ref), channel_id=1, source_target_pairs={{0,8},{8,16},{16,24},{24,32},{32,40},{40,48},{48,56},{56,64},{64,7... | collective-permute-start | bytes 3244040 | tf_op jit(solution)/shard_map/ppermute | solution.py:302
  35.4 20.6 %all-to-all-done.1.qg_ref.own_ref = bf16[8,1024,128]{2,1,0:T(8,128)(2,1)S(1)} async-done(((bf16[8,1024,128]{2,1,0:T(8,128)(2,1)}), bf16[8,1024,128]{2,1,0:T(8,128)(2,1)S(1)}, u32[]{:S(2)}, u32[]{:S(2)}) %all-to-all-start.1) | async-done | bytes 2097184 | tf_op jit(solution)/shard_map/all_to_all | solution.py:296
  56.0 0.0 copy-start
  56.0 0.0 copy-done.1
  56.0 1.0 collective-permute-done.1.stamps_right.right_ref
  57.0 6.3 %collective-permute-done.stamps_left.left_ref = bf16[8,528,128]{2,1,0:T(8,128)(2,1)} collective-permute-done((bf16[8,528,128]{2,1,0:T(8,128)(2,1)S(1)}, bf16[8,528,128]{2,1,0:T(8,128)(2,1)}, u32[]{:S(2)}, u32[]{:S(2)}) %collective-permute-start) | collective-permute-done | bytes 1081376 | tf_op jit(solution)/shard_map/ppermute | solution.py:302
  63.4 1.9 %collective-permute-start.3 = (bf16[8,256,128]{2,1,0:T(8,128)(2,1)S(1)}, bf16[8,256,128]{2,1,0:T(8,128)(2,1)S(1)}, u32[]{:S(2)}, u32[]{:S(2)}) collective-permute-start(bf16[8,256,128]{2,1,0:T(8,128)(2,1)S(1)} %slice.4), channel_id=1, source_target_pairs={{8,0},{16,8},{24,16},{32,24},{40,32},{48,40},{56,48},{64,56},{72,6... | collective-permute-start | bytes 1572872 | tf_op jit(solution)/shard_map/ppermute | solution.py:302
  65.3 3.9 %collective-permute-start.2 = (bf16[8,256,128]{2,1,0:T(8,128)(2,1)S(1)}, bf16[8,256,128]{2,1,0:T(8,128)(2,1)S(1)}, u32[]{:S(2)}, u32[]{:S(2)}) collective-permute-start(bf16[8,256,128]{2,1,0:T(8,128)(2,1)S(1)} %slice.4), channel_id=1, source_target_pairs={{0,8},{8,16},{16,24},{24,32},{32,40},{40,48},{48,56},{56,64},{64,7... | collective-permute-start | bytes 1572872 | tf_op jit(solution)/shard_map/ppermute | solution.py:302
  69.2 0.0 copy-done
  69.2 23.1 %attend.3 = (bf16[8,512,128]{2,1,0:T(8,128)(2,1)}, bf16[8,512,128]{2,1,0:T(8,128)(2,1)}, bf16[8,512,128]{2,1,0:T(8,128)(2,1)}, bf16[8,512,128]{2,1,0:T(8,128)(2,1)}) custom-call(bf16[8,528,128]{2,1,0:T(8,128)(2,1)} %collective-permute-done.stamps_left.left_ref, bf16[8,528,128]{2,1,0:T(8,128)(2,1)} %copy-done.1, ...), custom_call_target="tpu_custom_call" | custom-call | flops 1 | bytes 1 | tf_op jit(solution)/shard_map/attend/pallas_call | solution.py:264
  92.4 0.0 collective-permute-done.3.right_ref
  92.4 0.0 copy-start.6
  92.4 0.0 collective-permute-done.2.left_ref
  92.4 0.0 copy-start.7
  92.4 0.8 copy-done.6
  93.2 4.0 %collective-permute-start.4 = (bf16[8,512,128]{2,1,0:T(8,128)(2,1)}, bf16[8,512,128]{2,1,0:T(8,128)(2,1)S(1)}, u32[]{:S(2)}, u32[]{:S(2)}) collective-permute-start(bf16[8,512,128]{2,1,0:T(8,128)(2,1)} %get-tuple-element.32), channel_id=1, source_target_pairs={{8,0},{16,8},{24,16},{32,24},{40,32},{48,40},{56,48},{64,56},{72,6... | collective-permute-start | bytes 3145736 | tf_op jit(solution)/shard_map/ppermute | solution.py:302
  97.2 0.0 copy-done.7
  97.2 1.9 %collective-permute-start.5 = (bf16[8,512,128]{2,1,0:T(8,128)(2,1)}, bf16[8,512,128]{2,1,0:T(8,128)(2,1)S(1)}, u32[]{:S(2)}, u32[]{:S(2)}) collective-permute-start(bf16[8,512,128]{2,1,0:T(8,128)(2,1)} %get-tuple-element.33), channel_id=1, source_target_pairs={{0,8},{8,16},{16,24},{24,32},{32,40},{40,48},{48,56},{56,64},{64,7... | collective-permute-start | bytes 3145736 | tf_op jit(solution)/shard_map/ppermute | solution.py:302
  99.2 4.5 %all-to-all-start.2 = ((bf16[8,512,128]{2,1,0:T(8,128)(2,1)}), bf16[8,512,128]{2,1,0:T(8,128)(2,1)S(1)}, u32[]{:S(2)}, u32[]{:S(2)}) async-start(bf16[8,512,128]{2,1,0:T(8,128)(2,1)} %get-tuple-element.37), calls=%async_computation.2 | async-start | bytes 2097152 | tf_op jit(solution)/shard_map/all_to_all | solution.py:296
  103.6 0.0 copy-start.5
  103.6 13.0 %attend.2 = (bf16[8,256,128]{2,1,0:T(8,128)(2,1)}, bf16[8,256,128]{2,1,0:T(8,128)(2,1)}, bf16[8,256,128]{2,1,0:T(8,128)(2,1)}, bf16[8,256,128]{2,1,0:T(8,128)(2,1)}) custom-call(bf16[8,528,128]{2,1,0:T(8,128)(2,1)} %collective-permute-done.stamps_left.left_ref, bf16[8,528,128]{2,1,0:T(8,128)(2,1)} %copy-done.1, ...), custom_call_target="tpu_custom_call" | custom-call | flops 1 | bytes 1 | tf_op jit(solution)/shard_map/attend/pallas_call | solution.py:264
  116.6 2.5 %collective-permute-done.4 = bf16[8,512,128]{2,1,0:T(8,128)(2,1)S(1)} collective-permute-done((bf16[8,512,128]{2,1,0:T(8,128)(2,1)}, bf16[8,512,128]{2,1,0:T(8,128)(2,1)S(1)}, u32[]{:S(2)}, u32[]{:S(2)}) %collective-permute-start.4) | collective-permute-done | bytes 1048608 | tf_op jit(solution)/shard_map/ppermute | solution.py:302
  119.1 6.1 %collective-permute-done.5 = bf16[8,512,128]{2,1,0:T(8,128)(2,1)S(1)} collective-permute-done((bf16[8,512,128]{2,1,0:T(8,128)(2,1)}, bf16[8,512,128]{2,1,0:T(8,128)(2,1)S(1)}, u32[]{:S(2)}, u32[]{:S(2)}) %collective-permute-start.5) | collective-permute-done | bytes 1048608 | tf_op jit(solution)/shard_map/ppermute | solution.py:302
  125.2 1.9 %collective-permute-start.6 = (bf16[8,256,128]{2,1,0:T(8,128)(2,1)}, bf16[8,256,128]{2,1,0:T(8,128)(2,1)}, u32[]{:S(2)}, u32[]{:S(2)}) collective-permute-start(bf16[8,256,128]{2,1,0:T(8,128)(2,1)} %get-tuple-element.34), channel_id=1, source_target_pairs={{8,0},{16,8},{24,16},{32,24},{40,32},{48,40},{56,48},{64,56},{72,6... | collective-permute-start | bytes 1572872 | tf_op jit(solution)/shard_map/ppermute | solution.py:302
  127.1 3.9 %collective-permute-start.7 = (bf16[8,256,128]{2,1,0:T(8,128)(2,1)}, bf16[8,256,128]{2,1,0:T(8,128)(2,1)}, u32[]{:S(2)}, u32[]{:S(2)}) collective-permute-start(bf16[8,256,128]{2,1,0:T(8,128)(2,1)} %get-tuple-element.35), channel_id=1, source_target_pairs={{0,8},{8,16},{16,24},{24,32},{32,40},{40,48},{48,56},{56,64},{64,7... | collective-permute-start | bytes 1572872 | tf_op jit(solution)/shard_map/ppermute | solution.py:302
  131.0 0.0 copy-done.5
  131.0 1.4 add_convert_fusion
  132.4 0.0 copy-start.9
  132.4 0.0 copy-start.8
  132.4 0.0 all-to-all-done.2.refs_0_
  132.4 0.0 copy-start.3
  132.4 4.4 %all-to-all-start.3 = ((bf16[8,512,128]{2,1,0:T(8,128)(2,1)}), bf16[8,512,128]{2,1,0:T(8,128)(2,1)S(1)}, u32[]{:S(2)}, u32[]{:S(2)}) async-start(bf16[8,512,128]{2,1,0:T(8,128)(2,1)} %add_convert_fusion), calls=%async_computation.3 | async-start | bytes 2097152 | tf_op jit(solution)/shard_map/all_to_all | solution.py:296
  136.8 2.2 %collective-permute-done.6 = bf16[8,256,128]{2,1,0:T(8,128)(2,1)} collective-permute-done((bf16[8,256,128]{2,1,0:T(8,128)(2,1)}, bf16[8,256,128]{2,1,0:T(8,128)(2,1)}, u32[]{:S(2)}, u32[]{:S(2)}) %collective-permute-start.6) | collective-permute-done | bytes 524320 | tf_op jit(solution)/shard_map/ppermute | solution.py:302
  139.0 4.0 %collective-permute-done.7 = bf16[8,256,128]{2,1,0:T(8,128)(2,1)} collective-permute-done((bf16[8,256,128]{2,1,0:T(8,128)(2,1)}, bf16[8,256,128]{2,1,0:T(8,128)(2,1)}, u32[]{:S(2)}, u32[]{:S(2)}) %collective-permute-start.7) | collective-permute-done | bytes 524320 | tf_op jit(solution)/shard_map/ppermute | solution.py:302
  143.0 0.0 copy-done.9
  143.0 1.4 add_convert_fusion.1
  144.4 0.0 copy-done.3
  144.4 0.0 copy-done.8
  144.4 1.1 pad_maximum_fusion
  145.5 7.3 %all-to-all-done.3.refs_1_ = bf16[8,512,128]{2,1,0:T(8,128)(2,1)S(1)} async-done(((bf16[8,512,128]{2,1,0:T(8,128)(2,1)}), bf16[8,512,128]{2,1,0:T(8,128)(2,1)S(1)}, u32[]{:S(2)}, u32[]{:S(2)}) %all-to-all-start.3) | async-done | bytes 1048608 | tf_op jit(solution)/shard_map/all_to_all | solution.py:296
  152.8 0.0 copy-start.4
  152.8 3.6 %all-to-all-start.4 = ((bf16[8,512,128]{2,1,0:T(8,128)(2,1)}), bf16[8,512,128]{2,1,0:T(8,128)(2,1)S(1)}, u32[]{:S(2)}, u32[]{:S(2)}) async-start(bf16[8,512,128]{2,1,0:T(8,128)(2,1)} %pad_maximum_fusion), calls=%async_computation.4 | async-start | bytes 2097152 | tf_op jit(solution)/shard_map/all_to_all | solution.py:296
  156.3 0.0 copy-done.4
  156.4 3.4 %place.2 = (bf16[128,3072]{1,0:T(8,128)(2,1)}, bf16[128,3072]{1,0:T(8,128)(2,1)}, bf16[128,3072]{1,0:T(8,128)(2,1)}, bf16[128,3072]{1,0:T(8,128)(2,1)}) custom-call(bf16[8,512,128]{2,1,0:T(8,128)(2,1)} %copy-done.3, bf16[8,512,128]{2,1,0:T(8,128)(2,1)} %copy-done.4), custom_call_target="tpu_custom_call" | custom-call | tf_op jit(solution)/shard_map/place/pallas_call | solution.py:99
  159.8 12.5 %all-to-all-done.4.refs_0_.refs_1_ = bf16[8,512,128]{2,1,0:T(8,128)(2,1)S(1)} async-done(((bf16[8,512,128]{2,1,0:T(8,128)(2,1)}), bf16[8,512,128]{2,1,0:T(8,128)(2,1)S(1)}, u32[]{:S(2)}, u32[]{:S(2)}) %all-to-all-start.4) | async-done | bytes 1048608 | tf_op jit(solution)/shard_map/all_to_all | solution.py:296
  172.2 0.0 copy-start.2
  172.2 1.0 copy-done.2
  173.2 2.8 %place.3 = (bf16[128,3072]{1,0:T(8,128)(2,1)}, bf16[128,3072]{1,0:T(8,128)(2,1)}, bf16[128,3072]{1,0:T(8,128)(2,1)}, bf16[128,3072]{1,0:T(8,128)(2,1)}) custom-call(bf16[8,512,128]{2,1,0:T(8,128)(2,1)} %copy-done.2, bf16[8,512,128]{2,1,0:T(8,128)(2,1)} %copy-done.2, ...), custom_call_target="tpu_custom_call", output_to_operand_aliasing={{0}: (2, {}), {1}: (3, {}), {2}: (4, {}), {3}: (5, {})} | custom-call | tf_op jit(solution)/shard_map/place/pallas_call | solution.py:99
  (2 shorter events, 0.0 us)
Async XLA Ops:
  4.5 20.8 %all-to-all-start = ((bf16[8,528,128]{2,1,0:T(8,128)(2,1)}), bf16[8,528,128]{2,1,0:T(8,128)(2,1)S(1)}, u32[]{:S(2)}, u32[]{:S(2)}) async-start(bf16[8,528,128]{2,1,0:T(8,128)(2,1)} %pack.2), calls=%async_computation | async-start | bytes 2162688 | tf_op jit(solution)/shard_map/all_to_all | solution.py:296
  25.3 30.8 %copy-start.1 = (bf16[8,528,128]{2,1,0:T(8,128)(2,1)}, bf16[8,528,128]{2,1,0:T(8,128)(2,1)S(1)}, u32[]{:S(2)}) copy-start(bf16[8,528,128]{2,1,0:T(8,128)(2,1)S(1)} %all-to-all-done.stamps_own.own_ref) | copy-start | bytes 3244036
  25.3 30.7 %all-to-all-start.1 = ((bf16[8,1024,128]{2,1,0:T(8,128)(2,1)}), bf16[8,1024,128]{2,1,0:T(8,128)(2,1)S(1)}, u32[]{:S(2)}, u32[]{:S(2)}) async-start(bf16[8,1024,128]{2,1,0:T(8,128)(2,1)} %pack.3), calls=%async_computation.1 | async-start | bytes 4194304 | tf_op jit(solution)/shard_map/all_to_all | solution.py:296
  28.9 28.2 %collective-permute-start.1 = (bf16[8,528,128]{2,1,0:T(8,128)(2,1)S(1)}, bf16[8,528,128]{2,1,0:T(8,128)(2,1)}, u32[]{:S(2)}, u32[]{:S(2)}) collective-permute-start(bf16[8,528,128]{2,1,0:T(8,128)(2,1)S(1)} %all-to-all-done.stamps_own.own_ref), channel_id=1, source_target_pairs={{8,0},{16,8},{24,16},{32,24},{40,32},{48,40},{56,48},{64,56},{72,6... | collective-permute-start | bytes 3244040 | tf_op jit(solution)/shard_map/ppermute | solution.py:302
  33.4 30.0 %collective-permute-start = (bf16[8,528,128]{2,1,0:T(8,128)(2,1)S(1)}, bf16[8,528,128]{2,1,0:T(8,128)(2,1)}, u32[]{:S(2)}, u32[]{:S(2)}) collective-permute-start(bf16[8,528,128]{2,1,0:T(8,128)(2,1)S(1)} %all-to-all-done.stamps_own.own_ref), channel_id=1, source_target_pairs={{0,8},{8,16},{16,24},{24,32},{32,40},{40,48},{48,56},{56,64},{64,7... | collective-permute-start | bytes 3244040 | tf_op jit(solution)/shard_map/ppermute | solution.py:302
  56.0 13.2 %copy-start = (bf16[8,1024,128]{2,1,0:T(8,128)(2,1)}, bf16[8,1024,128]{2,1,0:T(8,128)(2,1)S(1)}, u32[]{:S(2)}) copy-start(bf16[8,1024,128]{2,1,0:T(8,128)(2,1)S(1)} %all-to-all-done.1.qg_ref.own_ref) | copy-start | bytes 6291460
  63.4 29.0 %collective-permute-start.3 = (bf16[8,256,128]{2,1,0:T(8,128)(2,1)S(1)}, bf16[8,256,128]{2,1,0:T(8,128)(2,1)S(1)}, u32[]{:S(2)}, u32[]{:S(2)}) collective-permute-start(bf16[8,256,128]{2,1,0:T(8,128)(2,1)S(1)} %slice.4), channel_id=1, source_target_pairs={{8,0},{16,8},{24,16},{32,24},{40,32},{48,40},{56,48},{64,56},{72,6... | collective-permute-start | bytes 1572872 | tf_op jit(solution)/shard_map/ppermute | solution.py:302
  65.3 27.1 %collective-permute-start.2 = (bf16[8,256,128]{2,1,0:T(8,128)(2,1)S(1)}, bf16[8,256,128]{2,1,0:T(8,128)(2,1)S(1)}, u32[]{:S(2)}, u32[]{:S(2)}) collective-permute-start(bf16[8,256,128]{2,1,0:T(8,128)(2,1)S(1)} %slice.4), channel_id=1, source_target_pairs={{0,8},{8,16},{16,24},{24,32},{32,40},{40,48},{48,56},{56,64},{64,7... | collective-permute-start | bytes 1572872 | tf_op jit(solution)/shard_map/ppermute | solution.py:302
  92.4 0.8 copy-start.6
  92.4 4.8 %copy-start.7 = (bf16[8,256,128]{2,1,0:T(8,128)(2,1)}, bf16[8,256,128]{2,1,0:T(8,128)(2,1)S(1)}, u32[]{:S(2)}) copy-start(bf16[8,256,128]{2,1,0:T(8,128)(2,1)S(1)} %collective-permute-done.2.left_ref) | copy-start | bytes 1572868
  93.2 25.9 %collective-permute-start.4 = (bf16[8,512,128]{2,1,0:T(8,128)(2,1)}, bf16[8,512,128]{2,1,0:T(8,128)(2,1)S(1)}, u32[]{:S(2)}, u32[]{:S(2)}) collective-permute-start(bf16[8,512,128]{2,1,0:T(8,128)(2,1)} %get-tuple-element.32), channel_id=1, source_target_pairs={{8,0},{16,8},{24,16},{32,24},{40,32},{48,40},{56,48},{64,56},{72,6... | collective-permute-start | bytes 3145736 | tf_op jit(solution)/shard_map/ppermute | solution.py:302
  97.2 28.0 %collective-permute-start.5 = (bf16[8,512,128]{2,1,0:T(8,128)(2,1)}, bf16[8,512,128]{2,1,0:T(8,128)(2,1)S(1)}, u32[]{:S(2)}, u32[]{:S(2)}) collective-permute-start(bf16[8,512,128]{2,1,0:T(8,128)(2,1)} %get-tuple-element.33), channel_id=1, source_target_pairs={{0,8},{8,16},{16,24},{24,32},{32,40},{40,48},{48,56},{56,64},{64,7... | collective-permute-start | bytes 3145736 | tf_op jit(solution)/shard_map/ppermute | solution.py:302
  99.2 33.3 %all-to-all-start.2 = ((bf16[8,512,128]{2,1,0:T(8,128)(2,1)}), bf16[8,512,128]{2,1,0:T(8,128)(2,1)S(1)}, u32[]{:S(2)}, u32[]{:S(2)}) async-start(bf16[8,512,128]{2,1,0:T(8,128)(2,1)} %get-tuple-element.37), calls=%async_computation.2 | async-start | bytes 2097152 | tf_op jit(solution)/shard_map/all_to_all | solution.py:296
  103.6 27.4 %copy-start.5 = (bf16[8,512,128]{2,1,0:T(8,128)(2,1)S(1)}, bf16[8,512,128]{2,1,0:T(8,128)(2,1)}, u32[]{:S(2)}) copy-start(bf16[8,512,128]{2,1,0:T(8,128)(2,1)} %get-tuple-element.36) | copy-start | bytes 3145732
  125.2 13.8 %collective-permute-start.6 = (bf16[8,256,128]{2,1,0:T(8,128)(2,1)}, bf16[8,256,128]{2,1,0:T(8,128)(2,1)}, u32[]{:S(2)}, u32[]{:S(2)}) collective-permute-start(bf16[8,256,128]{2,1,0:T(8,128)(2,1)} %get-tuple-element.34), channel_id=1, source_target_pairs={{8,0},{16,8},{24,16},{32,24},{40,32},{48,40},{56,48},{64,56},{72,6... | collective-permute-start | bytes 1572872 | tf_op jit(solution)/shard_map/ppermute | solution.py:302
  127.1 15.9 %collective-permute-start.7 = (bf16[8,256,128]{2,1,0:T(8,128)(2,1)}, bf16[8,256,128]{2,1,0:T(8,128)(2,1)}, u32[]{:S(2)}, u32[]{:S(2)}) collective-permute-start(bf16[8,256,128]{2,1,0:T(8,128)(2,1)} %get-tuple-element.35), channel_id=1, source_target_pairs={{0,8},{8,16},{16,24},{24,32},{32,40},{40,48},{48,56},{56,64},{64,7... | collective-permute-start | bytes 1572872 | tf_op jit(solution)/shard_map/ppermute | solution.py:302
  132.4 10.6 %copy-start.9 = (bf16[8,256,128]{2,1,0:T(8,128)(2,1)S(1)}, bf16[8,256,128]{2,1,0:T(8,128)(2,1)}, u32[]{:S(2)}) copy-start(bf16[8,256,128]{2,1,0:T(8,128)(2,1)} %get-tuple-element.27) | copy-start | bytes 1572868
  132.4 12.0 %copy-start.8 = (bf16[8,256,128]{2,1,0:T(8,128)(2,1)S(1)}, bf16[8,256,128]{2,1,0:T(8,128)(2,1)}, u32[]{:S(2)}) copy-start(bf16[8,256,128]{2,1,0:T(8,128)(2,1)} %get-tuple-element.26) | copy-start | bytes 1572868
  132.4 12.0 %copy-start.3 = (bf16[8,512,128]{2,1,0:T(8,128)(2,1)}, bf16[8,512,128]{2,1,0:T(8,128)(2,1)S(1)}, u32[]{:S(2)}) copy-start(bf16[8,512,128]{2,1,0:T(8,128)(2,1)S(1)} %all-to-all-done.2.refs_0_) | copy-start | bytes 3145732
  132.4 20.3 %all-to-all-start.3 = ((bf16[8,512,128]{2,1,0:T(8,128)(2,1)}), bf16[8,512,128]{2,1,0:T(8,128)(2,1)S(1)}, u32[]{:S(2)}, u32[]{:S(2)}) async-start(bf16[8,512,128]{2,1,0:T(8,128)(2,1)} %add_convert_fusion), calls=%async_computation.3 | async-start | bytes 2097152 | tf_op jit(solution)/shard_map/all_to_all | solution.py:296
  152.8 3.6 %copy-start.4 = (bf16[8,512,128]{2,1,0:T(8,128)(2,1)}, bf16[8,512,128]{2,1,0:T(8,128)(2,1)S(1)}, u32[]{:S(2)}) copy-start(bf16[8,512,128]{2,1,0:T(8,128)(2,1)S(1)} %all-to-all-done.3.refs_1_) | copy-start | bytes 3145732
  152.8 19.4 %all-to-all-start.4 = ((bf16[8,512,128]{2,1,0:T(8,128)(2,1)}), bf16[8,512,128]{2,1,0:T(8,128)(2,1)S(1)}, u32[]{:S(2)}, u32[]{:S(2)}) async-start(bf16[8,512,128]{2,1,0:T(8,128)(2,1)} %pad_maximum_fusion), calls=%async_computation.4 | async-start | bytes 2097152 | tf_op jit(solution)/shard_map/all_to_all | solution.py:296
  172.2 1.0 copy-start.2

commit v3 on v2

--- a/solution.py
+++ b/solution.py
@@ -17,7 +17,7 @@
 SCALE = DH ** (-0.5)
 LOG2E = 1.4426950408889634
 GROUP = ("yh", "head")
-CHUNKS = ((0, 1), (2,))
+CHUNKS = ((0,), (1, 2))
 STAMP_ROWS = 16
 STAMP_BASE = 32
 RANGES = 2
@@ -46,13 +46,21 @@
             for at, (which, head) in enumerate(plan):
                 lanes = pl.ds((peer * heads + head) * DH, DH)
                 out[peer, pl.ds(at * rows, rows)] = ins[which][:, lanes]
-            if stamped and number == 0:
-                out[peer, pl.ds(len(plan) * rows, STAMP_ROWS)] = refs[count][...]
+    if stamped:
+        stamp = refs[count][...]
+        place = lax.axis_index("col") * RANGES + lax.axis_index("yh")
+        code = jnp.where(stamp >= 0, stamp - place * SHARD_MS + 1, 0)
+        row = lax.broadcasted_iota(jnp.int32, (STAMP_ROWS, rows), 0)
+        code = jnp.broadcast_to(code, (STAMP_ROWS, rows))
+        code = jnp.where(row == 0, code // STAMP_BASE, code % STAMP_BASE)
+        code = code.astype(jnp.float32).astype(jnp.bfloat16)
+        for peer in range(peers):
+            outs[0][peer, pl.ds(len(plans[0]) * rows, STAMP_ROWS)] = code
 
 
 def pack(arrays, plans, peers, stamp_rows=None):
     rows, width = arrays[0].shape
-    stamps = [] if stamp_rows is None else [stamp_rows]
+    stamps = [] if stamp_rows is None else [stamp_rows.reshape(1, rows)]
     extra = [STAMP_ROWS if stamps and number == 0 else 0 for number in range(len(plans))]
     return pl.pallas_call(
         functools.partial(
@@ -67,45 +75,42 @@
     )(*arrays, *stamps)
 
 
-def place_kernel(peers, heads, chunk, offsets, *refs):
-    count = len(offsets)
-    pieces, outs, sems = refs[:count], refs[-2 * count - 1 : -1], refs[-1]
+def place_kernel(peers, heads, chunk, offset, piece, *refs):
+    outs, sems = refs[-3:-1], refs[-1]
     rows = outs[0].shape[0]
     copies = []
-    for piece, offset, pair in zip(pieces, offsets, zip(outs[::2], outs[1::2])):
-        for peer in range(peers):
-            for place, head in enumerate(chunk):
-                lanes = pl.ds((peer * heads + head) * DH, DH)
-                for which, out in enumerate(pair):
-                    start = offset + (2 * place + which) * rows
-                    copies.append(
-                        pltpu.make_async_copy(
-                            piece.at[peer, pl.ds(start, rows)],
-                            out.at[:, lanes],
-                            sems.at[len(copies)],
-                        )
+    for peer in range(peers):
+        for place, head in enumerate(chunk):
+            lanes = pl.ds((peer * heads + head) * DH, DH)
+            for which, out in enumerate(outs):
+                start = offset + (2 * place + which) * rows
+                copies.append(
+                    pltpu.make_async_copy(
+                        piece.at[peer, pl.ds(start, rows)],
+                        out.at[:, lanes],
+                        sems.at[len(copies)],
                     )
+                )
     for copy in copies:
         copy.start()
     for copy in copies:
         copy.wait()
 
 
-def place(pieces, offsets, chunk, heads, rows, outs):
-    peers = pieces[0].shape[0]
-    shape = jax.ShapeDtypeStruct((rows, peers * heads * DH), pieces[0].dtype)
-    number = 2 * len(pieces)
+def place(piece, offset, chunk, heads, rows, outs=()):
+    peers = piece.shape[0]
+    shape = jax.ShapeDtypeStruct((rows, peers * heads * DH), piece.dtype)
     anywhere = pl.BlockSpec(memory_space=pl.ANY)
     return pl.pallas_call(
-        functools.partial(place_kernel, peers, heads, chunk, offsets),
-        in_specs=[pl.BlockSpec(memory_space=pltpu.VMEM)] * len(pieces) + [anywhere] * len(outs),
-        out_specs=[anywhere] * number,
-        out_shape=[shape] * number,
-        input_output_aliases={len(pieces) + at: at for at in range(len(outs))},
-        scratch_shapes=[pltpu.SemaphoreType.DMA((number * peers * len(chunk),))],
+        functools.partial(place_kernel, peers, heads, chunk, offset),
+        in_specs=[pl.BlockSpec(memory_space=pltpu.VMEM)] + [anywhere] * len(outs),
+        out_specs=[anywhere] * 2,
+        out_shape=[shape] * 2,
+        input_output_aliases={1 + at: at for at in range(len(outs))},
+        scratch_shapes=[pltpu.SemaphoreType.DMA((2 * peers * len(chunk),))],
         compiler_params=pltpu.CompilerParams(vmem_limit_bytes=VMEM_BYTES),
         name="place",
-    )(*pieces, *outs)
+    )(piece, *outs)
 
 
 def spread_stamps(codes, shift):
@@ -128,8 +133,8 @@
     skip = 4 - sum(fresh)
     result_ref, to_left_ref, own_sum_ref, to_right_ref = refs[skip : skip + 4]
     (
-        stamps, keys, values, keys_t, values_t,
-        scores, grad_weights, key_sums, value_sums, total_t, query_t,
+        stamps,
+        scores, key_sums, value_sums, total_t, query_t,
     ) = refs[skip + 4 :]
     rows = size // per
     span = 2 * REACH + 1
@@ -142,26 +147,27 @@
                 spread = spread_stamps(ref[block], (place - RANGES) * SHARD_MS)
                 stamps[place, pl.ds(block % per * rows, rows)] = spread
 
-    for side, ref in enumerate((left_ref, own_ref, right_ref)):
-        for part in range(RANGES):
-            place = side * RANGES + part
-            blocks = pl.ds(part * per, per)
-            key_tile = ref[blocks, pl.ds(0, rows)].reshape(size, DH)
-            value_tile = ref[blocks, pl.ds(rows, rows)].reshape(size, DH)
-            keys[place] = key_tile
-            values[place] = value_tile
-            keys_t[place] = key_tile.T
-            values_t[place] = value_tile.T
-    key_sums[...] = jnp.zeros_like(key_sums)
-    value_sums[...] = jnp.zeros_like(value_sums)
-    total_t[...] = jnp.zeros_like(total_t)
-    query_t[...] = jnp.zeros_like(query_t)
+    def slots(place, which):
+        ref = (left_ref, own_ref, right_ref)[place // RANGES]
+        found = ref[pl.ds(place % RANGES * per, per), pl.ds(which * rows, rows)]
+        return found.reshape(size, DH)
+
+    keys = [slots(place, 0) for place in range(3 * RANGES)]
+    values = [slots(place, 1) for place in range(3 * RANGES)]
     offsets = lax.broadcasted_iota(jnp.int32, (1, size), 1) * SHARD_MS // size
     blocks = [pl.ds(part * per, per) for part in range(RANGES)]
     query = [qg_ref[block, pl.ds(0, rows)].reshape(size, DH) for block in blocks]
     grad = [qg_ref[block, pl.ds(rows, rows)].reshape(size, DH) for block in blocks]
     stamp = [(offsets + part * SHARD_MS).astype(jnp.float32) for part in range(RANGES)]
     top, inverse, row_dot = [None] * RANGES, [None] * RANGES, [None] * RANGES
+
+    def add(ref, at, fresh, value):
+        ref[at] = value if fresh else ref[at] + value
+
+    def unrolled(body, carry):
+        for step in range(span):
+            carry = body(step, carry)
+        return carry
 
     def score_step(part, step, top):
         place = step + part
@@ -175,16 +181,17 @@
         place = step + part
         raised = jnp.exp2(scores[part, step] - top[part])
         scores[part, step] = raised
-        total_t[part] += dot_nn(values_t[place], raised.astype(jnp.bfloat16))
+        add(total_t, part, step == 0, dot(values[place], raised.astype(jnp.bfloat16), ((0,), (0,))))
         return total + jnp.sum(raised.reshape(size // 8, 8, size), axis=0)
 
     def grad_step(part, step):
         place = step + part
         weights = scores[part, step] * inverse[part]
         slopes = (weights * (dot_nt(values[place], grad[part]) - row_dot[part])).astype(jnp.bfloat16)
-        value_sums[place] += dot_nn(weights.astype(jnp.bfloat16), grad[part])
-        key_sums[place] += dot_nn(slopes, query[part])
-        query_t[part] += dot_nn(keys_t[place], slopes)
+        fresh = part == 0 or step == span - 1
+        add(value_sums, place, fresh, dot_nn(weights.astype(jnp.bfloat16), grad[part]))
+        add(key_sums, place, fresh, dot_nn(slopes, query[part]))
+        add(query_t, part, step == 0, dot(keys[place], slopes, ((0,), (0,))))
 
     def finish(part, total):
         inverse[part] = 1.0 / jnp.sum(total, axis=0, keepdims=True)
@@ -201,13 +208,13 @@
 
     lowest = jnp.full((8, size), NEG_FILL, jnp.float32)
     zero = jnp.zeros((8, size), jnp.float32)
-    found = lax.fori_loop(0, span, lambda step, c: score_step(0, step, c), lowest, unroll=UNROLL)
+    found = unrolled(lambda step, c: score_step(0, step, c), lowest)
     top[0] = jnp.max(found, axis=0, keepdims=True)
 
     def second(step, carry):
         return weight_step(0, step, carry[0]), score_step(1, step, carry[1])
 
-    total, found = lax.fori_loop(0, span, second, (zero, lowest), unroll=UNROLL)
+    total, found = unrolled(second, (zero, lowest))
     top[1] = jnp.max(found, axis=0, keepdims=True)
     finish(0, total)
 
@@ -215,7 +222,7 @@
         grad_step(0, step)
         return weight_step(1, step, carry)
 
-    total = lax.fori_loop(0, span, third, zero, unroll=UNROLL)
+    total = unrolled(third, zero)
     finish_query(0)
     finish(1, total)
 
@@ -223,7 +230,7 @@
         grad_step(1, step)
         return carry
 
-    lax.fori_loop(0, span, fourth, 0, unroll=UNROLL)
+    unrolled(fourth, 0)
     finish_query(1)
     for side, ref in enumerate((to_left_ref, own_sum_ref, to_right_ref)):
         for part in range(RANGES):
@@ -273,11 +280,6 @@
         input_output_aliases=aliases,
         scratch_shapes=[
             pltpu.VMEM((places, size, DH), jnp.float32),
-            pltpu.VMEM((places, size, DH), jnp.bfloat16),
-            pltpu.VMEM((places, size, DH), jnp.bfloat16),
-            pltpu.VMEM((places, DH, size), jnp.bfloat16),
-            pltpu.VMEM((places, DH, size), jnp.bfloat16),
-            pltpu.VMEM((RANGES, span, size, size), jnp.float32),
             pltpu.VMEM((RANGES, span, size, size), jnp.float32),
             pltpu.VMEM((places, size, DH), jnp.float32),
             pltpu.VMEM((places, size, DH), jnp.float32),
@@ -302,13 +304,6 @@
     return lax.ppermute(value, "col", [(at, at + steps) for at in range(first, last)])
 
 
-def stamp_codes(audio_time):
-    place = lax.axis_index("col") * RANGES + lax.axis_index("yh")
-    code = jnp.where(audio_time >= 0, audio_time - place * SHARD_MS + 1, 0)
-    pair = jnp.stack([code // STAMP_BASE, code % STAMP_BASE]).astype(jnp.bfloat16)
-    return jnp.pad(pair, ((0, STAMP_ROWS - 2), (0, 0)))
-
-
 def after(value, *others):
     return lax.optimization_barrier((value, others))[0]
 
@@ -318,47 +313,43 @@
     rows, width = video_query.shape
     heads = width // DH // peers
     early, late = CHUNKS
+    block = 2 * rows
+    arrays = (audio_key, audio_value, video_query, grad_out)
     key_plan = [(which, head) for head in early for which in (0, 1)]
-    rest_plan = [(which, head) for head in early for which in (2, 3)]
-    rest_plan += [(which, head) for head in late for which in (0, 1)]
-    rest_plan += [(which, head) for head in late for which in (2, 3)]
-    arrays = (audio_key, audio_value, video_query, grad_out)
-    (key_pack,) = pack(arrays[:2], [key_plan], peers, stamp_codes(audio_time))
+    mixed_plan = [(which, head) for head in early for which in (2, 3)]
+    mixed_plan += [(which, head) for head in late for which in (0, 1)]
+    query_plan = [(which, head) for head in late for which in (2, 3)]
+    (key_pack,) = pack(arrays[:2], [key_plan], peers, audio_time)
     own = swap(key_pack)
+    mixed_pack, query_pack = pack(arrays, [mixed_plan, query_plan], peers)
+    mixed = swap(after(mixed_pack, own))
     left, right = shifted(own, 1), shifted(own, -1)
-    (rest_pack,) = pack(arrays, [rest_plan], peers)
-    rest = swap(after(rest_pack, own))
-    late_rows = slice(2 * len(early) * rows, 2 * heads * rows)
-    sent = after(rest[:, late_rows], left, right)
+    sent = after(mixed[:, block * len(early) :], left, right)
     late_left, late_right = shifted(sent, 1), shifted(sent, -1)
-
-    def run(chunk, sides, firsts):
-        return attend(
-            chunk,
-            (left, own, right),
-            (rest, chunk[0] - firsts[0]),
-            (sides, [chunk[0] - first for first in firsts[1:]]),
-            (None, chunk[0]),
-            ([None] * 3, chunk[0]),
-            (len(chunk), len(chunk)),
-        )
+    queries = swap(after(query_pack, mixed))
 
     def gather(sums, came):
         return sum(value.astype(jnp.float32) for value in (sums[1], *came)).astype(jnp.bfloat16)
 
-    result, *sums = run(early, (left, own, right), (0, 0, 0, 0))
-    to_left, to_right = after((sums[0], sums[2]), late_left, late_right)
-    came = shifted(to_left, -1), shifted(to_right, 1)
+    stamped = (left, own, right)
+    result, *sums = attend(
+        early, stamped, (mixed, 0), (stamped, (0, 0, 0)), (None, 0), ([None] * 3, 0),
+        (heads + len(early), len(early)),
+    )
+    came = shifted(sums[0], -1), shifted(sums[2], 1)
+    first = late[0]
+    result, *late_sums = attend(
+        late, stamped, (queries, first), ((late_left, mixed, late_right), (first, 0, first)),
+        (result, 0), ([None] * 3, first), (heads + len(early), len(late)),
+    )
+    to_left, to_right = after((late_sums[0], late_sums[2]), came)
+    late_came = shifted(to_left, -1), shifted(to_right, 1)
+    result = lax.dynamic_update_slice(result, gather(sums, came), (0, block * heads, 0))
     result = swap(result)
-    last_result, *last_sums = run(late, (late_left, rest, late_right), (heads, 0, len(early), 0))
-    to_left, to_right = after((last_sums[0], last_sums[2]), came)
-    last_came = shifted(to_left, -1), shifted(to_right, 1)
-    grads = swap(after(gather(sums, came), result))
-    outs = place((result, grads), (0, 0), early, heads, rows, ())
-    last = jnp.concatenate([last_result, gather(last_sums, last_came)], axis=1)
-    last = swap(after(last, grads))
-    offsets = (0, 2 * len(late) * rows)
-    return tuple(place((last, last), offsets, late, heads, rows, outs))
+    grads = swap(gather(late_sums, late_came))
+    attended = place(result, 0, early + late, heads, rows)
+    grad = place(result, block * heads, early, heads, rows)
+    return (*attended, *place(grads, 0, late, heads, rows, grad))
 
 
 def solution(mesh):

time: 177 us -> 166 us (0.938)
  waiting for transfers between devices: 75.3 us -> 61.5 us
  starting transfers between devices: 44.5 us -> 48.8 us
  other arithmetic: 5.13 us -> 2.45 us
    all_to_all x5, waiting for transfers between devices: 53.1 us -> 32.2 us  [swap(): return lax.all_to_all(value, GROUP, split_axis=0, concat_axis=0, tiled=True)]
    ppermute x8, waiting for transfers between devices: 22.1 us -> 29.3 us  [shifted(): lax.ppermute(value, 'col', [(at, at + steps) for at in range(first, last)])]
    ppermute x8, starting transfers between devices: 24.1 us -> 28.3 us  [shifted(): lax.ppermute(value, 'col', [(at, at + steps) for at in range(first, last)])]
    pallas_call x2 -> x3, Pallas kernels: 6.21 us -> 8.09 us  [place(): pl.pallas_call(functools.partial(place_kernel, peers, heads, chunk, offse...]
  transfers between devices with their start and end apart: 13 -> 13, of which waited for: 10 -> 7; matrix products, arithmetic and copies ran while one was open for 2% -> 2% of each run, Pallas kernels for 24% -> 27%
where the time goes in v3:
time: 166 us; the launch traced here: 165 us
  waiting for transfers between devices  61.5 us (37%)
  Pallas kernels  49.4 us (30%)
  starting transfers between devices  48.8 us (29%)
  other arithmetic  2.45 us (1%)
  local copies, waits for them, and re-layouts  2.23 us (1%)
    pallas_call x2, Pallas kernels, attend(): pl.pallas_call(functools.partial(attend_kernel, per, size, fresh), grid=(...  35.2 us
    all_to_all x5, waiting for transfers between devices, swap(): return lax.all_to_all(value, GROUP, split_axis=0, concat_axis=0, tiled=True)  32.2 us
    ppermute x8, waiting for transfers between devices, shifted(): lax.ppermute(value, 'col', [(at, at + steps) for at in range(first, last)])  29.3 us
    ppermute x8, starting transfers between devices, shifted(): lax.ppermute(value, 'col', [(at, at + steps) for at in range(first, last)])  28.3 us
    all_to_all x5, starting transfers between devices, swap(): return lax.all_to_all(value, GROUP, split_axis=0, concat_axis=0, tiled=True)  20.5 us
    pallas_call x3, Pallas kernels, place(): pl.pallas_call(functools.partial(place_kernel, peers, heads, chunk, offse...  8.09 us
    pallas_call x2, Pallas kernels, pack(): pl.pallas_call(functools.partial(pack_kernel, peers, width // DH // peers...  6.13 us
  transfers between devices with their start and end apart: 13, of which 7 were waited for; matrix products, arithmetic and copies ran while one was open for 2% of the time, Pallas kernels for 27%

profile of v3, /device:TPU:96, one launch (start us, length us, event | category | flops | bytes accessed | tf_op | source)
XLA Modules:
  0.0 165.4 jit_solution(10202752598972809503)
XLA Ops:
  0.6 2.3 %pack.2 = bf16[8,272,128]{2,1,0:T(8,128)(2,1)} custom-call(bf16[128,3072]{1,0:T(8,128)(2,1)} %refs_0_.3, bf16[128,3072]{1,0:T(8,128)(2,1)} %refs_1_.3, s32[1,128]{1,0:T(1,128)} %bitcast.1), custom_call_target="tpu_custom_call" | custom-call | tf_op jit(solution)/shard_map/pack/pallas_call | solution.py:65
  2.9 4.5 %all-to-all-start = ((bf16[8,272,128]{2,1,0:T(8,128)(2,1)}), bf16[8,272,128]{2,1,0:T(8,128)(2,1)S(1)}, u32[]{:S(2)}, u32[]{:S(2)}) async-start(bf16[8,272,128]{2,1,0:T(8,128)(2,1)} %pack.2), calls=%async_computation | async-start | bytes 1114112 | tf_op jit(solution)/shard_map/all_to_all | solution.py:298
  7.4 3.8 %pack.3 = (bf16[8,768,128]{2,1,0:T(8,128)(2,1)}, bf16[8,512,128]{2,1,0:T(8,128)(2,1)}) custom-call(bf16[128,3072]{1,0:T(8,128)(2,1)} %refs_0_.3, bf16[128,3072]{1,0:T(8,128)(2,1)} %refs_1_.3, bf16[128,3072]{1,0:T(8,128)(2,1)} %refs_2_.1, bf16[128,3072]{1,0:T(8,128)(2,1)} %refs_3_.1), custom_call_target="tpu_custom_call" | custom-call | tf_op jit(solution)/shard_map/pack/pallas_call | solution.py:65
  11.2 6.9 %all-to-all-done.stamps_own.own_ref = bf16[8,272,128]{2,1,0:T(8,128)(2,1)S(1)} async-done(((bf16[8,272,128]{2,1,0:T(8,128)(2,1)}), bf16[8,272,128]{2,1,0:T(8,128)(2,1)S(1)}, u32[]{:S(2)}, u32[]{:S(2)}) %all-to-all-start) | async-done | bytes 557088 | tf_op jit(solution)/shard_map/all_to_all | solution.py:298
  18.1 0.0 copy-start.2
  18.1 3.6 %all-to-all-start.1 = ((bf16[8,768,128]{2,1,0:T(8,128)(2,1)}), bf16[8,768,128]{2,1,0:T(8,128)(2,1)S(1)}, u32[]{:S(2)}, u32[]{:S(2)}) async-start(bf16[8,768,128]{2,1,0:T(8,128)(2,1)} %get-tuple-element.27), calls=%async_computation.1 | async-start | bytes 3145728 | tf_op jit(solution)/shard_map/all_to_all | solution.py:298
  21.7 4.5 %collective-permute-start.1 = (bf16[8,272,128]{2,1,0:T(8,128)(2,1)S(1)}, bf16[8,272,128]{2,1,0:T(8,128)(2,1)S(1)}, u32[]{:S(2)}, u32[]{:S(2)}) collective-permute-start(bf16[8,272,128]{2,1,0:T(8,128)(2,1)S(1)} %all-to-all-done.stamps_own.own_ref), channel_id=1, source_target_pairs={{8,0},{16,8},{24,16},{32,24},{40,32},{48,40},{56,48},{64,56},{72,6... | collective-permute-start | bytes 1671176 | tf_op jit(solution)/shard_map/ppermute | solution.py:304
  26.2 1.9 %collective-permute-start = (bf16[8,272,128]{2,1,0:T(8,128)(2,1)S(1)}, bf16[8,272,128]{2,1,0:T(8,128)(2,1)S(1)}, u32[]{:S(2)}, u32[]{:S(2)}) collective-permute-start(bf16[8,272,128]{2,1,0:T(8,128)(2,1)S(1)} %all-to-all-done.stamps_own.own_ref), channel_id=1, source_target_pairs={{0,8},{8,16},{16,24},{24,32},{32,40},{40,48},{48,56},{56,64},{64,7... | collective-permute-start | bytes 1671176 | tf_op jit(solution)/shard_map/ppermute | solution.py:304
  28.1 15.0 %all-to-all-done.1.qg_ref.own_ref = bf16[8,768,128]{2,1,0:T(8,128)(2,1)S(1)} async-done(((bf16[8,768,128]{2,1,0:T(8,128)(2,1)}), bf16[8,768,128]{2,1,0:T(8,128)(2,1)S(1)}, u32[]{:S(2)}, u32[]{:S(2)}) %all-to-all-start.1) | async-done | bytes 1572896 | tf_op jit(solution)/shard_map/all_to_all | solution.py:298
  43.2 0.0 copy-start
  43.2 1.2 slice.4
  44.4 0.0 copy-done.2
  44.4 0.0 collective-permute-done.1.stamps_right.right_ref
  44.4 0.0 copy-start.3
  44.4 0.4 collective-permute-done.stamps_left.left_ref
  44.8 0.0 copy-start.4
  44.8 4.1 %collective-permute-start.3 = (bf16[8,512,128]{2,1,0:T(8,128)(2,1)}, bf16[8,512,128]{2,1,0:T(8,128)(2,1)}, u32[]{:S(2)}, u32[]{:S(2)}) collective-permute-start(bf16[8,512,128]{2,1,0:T(8,128)(2,1)} %slice.4), channel_id=1, source_target_pairs={{8,0},{16,8},{24,16},{32,24},{40,32},{48,40},{56,48},{64,56},{72,6... | collective-permute-start | bytes 3145736 | tf_op jit(solution)/shard_map/ppermute | solution.py:304
  48.9 1.9 %collective-permute-start.2 = (bf16[8,512,128]{2,1,0:T(8,128)(2,1)}, bf16[8,512,128]{2,1,0:T(8,128)(2,1)}, u32[]{:S(2)}, u32[]{:S(2)}) collective-permute-start(bf16[8,512,128]{2,1,0:T(8,128)(2,1)} %slice.4), channel_id=1, source_target_pairs={{0,8},{8,16},{16,24},{24,32},{32,40},{40,48},{48,56},{56,64},{64,7... | collective-permute-start | bytes 3145736 | tf_op jit(solution)/shard_map/ppermute | solution.py:304
  50.9 0.0 copy-done
  50.9 4.3 %all-to-all-start.2 = ((bf16[8,512,128]{2,1,0:T(8,128)(2,1)}), bf16[8,512,128]{2,1,0:T(8,128)(2,1)}, u32[]{:S(2)}, u32[]{:S(2)}) async-start(bf16[8,512,128]{2,1,0:T(8,128)(2,1)} %get-tuple-element.28), calls=%async_computation.2 | async-start | bytes 2097152 | tf_op jit(solution)/shard_map/all_to_all | solution.py:298
  55.2 0.0 copy-done.3
  55.2 0.0 copy-done.4
  55.2 13.0 %attend.2 = (bf16[8,1024,128]{2,1,0:T(8,128)(2,1)}, bf16[8,256,128]{2,1,0:T(8,128)(2,1)}, bf16[8,256,128]{2,1,0:T(8,128)(2,1)}, bf16[8,256,128]{2,1,0:T(8,128)(2,1)}) custom-call(bf16[8,272,128]{2,1,0:T(8,128)(2,1)} %copy-done.4, bf16[8,272,128]{2,1,0:T(8,128)(2,1)} %copy-done.2, bf16[8,272,128]{2,1,0:T(8,128)(2,1)} %copy-done.3, ...), custom_call_target="tpu_custom_call" | custom-call | flops 1 | bytes 1 | tf_op jit(solution)/shard_map/attend/pallas_call | solution.py:271
  68.2 6.0 %collective-permute-start.4 = (bf16[8,256,128]{2,1,0:T(8,128)(2,1)}, bf16[8,256,128]{2,1,0:T(8,128)(2,1)S(1)}, u32[]{:S(2)}, u32[]{:S(2)}) collective-permute-start(bf16[8,256,128]{2,1,0:T(8,128)(2,1)} %get-tuple-element.33), channel_id=1, source_target_pairs={{8,0},{16,8},{24,16},{32,24},{40,32},{48,40},{56,48},{64,56},{72,6... | collective-permute-start | bytes 1572872 | tf_op jit(solution)/shard_map/ppermute | solution.py:304
  74.2 2.1 %collective-permute-start.5 = (bf16[8,256,128]{2,1,0:T(8,128)(2,1)}, bf16[8,256,128]{2,1,0:T(8,128)(2,1)S(1)}, u32[]{:S(2)}, u32[]{:S(2)}) collective-permute-start(bf16[8,256,128]{2,1,0:T(8,128)(2,1)} %get-tuple-element.34), channel_id=1, source_target_pairs={{0,8},{8,16},{16,24},{24,32},{32,40},{40,48},{48,56},{56,64},{64,7... | collective-permute-start | bytes 1572872 | tf_op jit(solution)/shard_map/ppermute | solution.py:304
  76.3 0.0 all-to-all-done.2.qg_ref
  76.4 0.0 collective-permute-done.3.right_ref
  76.4 1.3 collective-permute-done.2.left_ref
  77.7 0.0 copy-start.7
  77.7 22.1 %attend.3 = (bf16[8,1024,128]{2,1,0:T(8,128)(2,1)}, bf16[8,512,128]{2,1,0:T(8,128)(2,1)}, bf16[8,512,128]{2,1,0:T(8,128)(2,1)}, bf16[8,512,128]{2,1,0:T(8,128)(2,1)}) custom-call(bf16[8,272,128]{2,1,0:T(8,128)(2,1)} %copy-done.4, bf16[8,272,128]{2,1,0:T(8,128)(2,1)} %copy-done.2, bf16[8,272,128]{2,1,0:T(8,128)(2,1)} %copy-done.3, ...), custom_call_target="tpu_custom_call", output_to_operand_aliasing={{0}: (7, {})} | custom-call | flops 1 | bytes 1 | tf_op jit(solution)/shard_map/attend/pallas_call | solution.py:271
  99.8 0.0 collective-permute-done.4
  99.8 0.0 collective-permute-done.5
  99.8 0.0 copy-done.7
  99.9 1.0 fusion
  100.9 0.0 copy-start.6
  100.9 3.7 %all-to-all-start.3 = ((bf16[8,1024,128]{2,1,0:T(8,128)(2,1)}), bf16[8,1024,128]{2,1,0:T(8,128)(2,1)S(1)}, u32[]{:S(2)}, u32[]{:S(2)}) async-start(bf16[8,1024,128]{2,1,0:T(8,128)(2,1)} %fusion), calls=%async_computation.3 | async-start | bytes 4194304 | tf_op jit(solution)/shard_map/all_to_all | solution.py:298
  104.6 5.8 %collective-permute-start.6 = (bf16[8,512,128]{2,1,0:T(8,128)(2,1)}, bf16[8,512,128]{2,1,0:T(8,128)(2,1)S(1)}, u32[]{:S(2)}, u32[]{:S(2)}) collective-permute-start(bf16[8,512,128]{2,1,0:T(8,128)(2,1)} %get-tuple-element.40), channel_id=1, source_target_pairs={{8,0},{16,8},{24,16},{32,24},{40,32},{48,40},{56,48},{64,56},{72,6... | collective-permute-start | bytes 3145736 | tf_op jit(solution)/shard_map/ppermute | solution.py:304
  110.4 1.9 %collective-permute-start.7 = (bf16[8,512,128]{2,1,0:T(8,128)(2,1)}, bf16[8,512,128]{2,1,0:T(8,128)(2,1)S(1)}, u32[]{:S(2)}, u32[]{:S(2)}) collective-permute-start(bf16[8,512,128]{2,1,0:T(8,128)(2,1)} %get-tuple-element.41), channel_id=1, source_target_pairs={{0,8},{8,16},{16,24},{24,32},{32,40},{40,48},{48,56},{56,64},{64,7... | collective-permute-start | bytes 3145736 | tf_op jit(solution)/shard_map/ppermute | solution.py:304
  112.4 21.5 %collective-permute-done.6 = bf16[8,512,128]{2,1,0:T(8,128)(2,1)S(1)} collective-permute-done((bf16[8,512,128]{2,1,0:T(8,128)(2,1)}, bf16[8,512,128]{2,1,0:T(8,128)(2,1)S(1)}, u32[]{:S(2)}, u32[]{:S(2)}) %collective-permute-start.6) | collective-permute-done | bytes 1048608 | tf_op jit(solution)/shard_map/ppermute | solution.py:304
  133.8 6.1 %collective-permute-done.7 = bf16[8,512,128]{2,1,0:T(8,128)(2,1)S(1)} collective-permute-done((bf16[8,512,128]{2,1,0:T(8,128)(2,1)}, bf16[8,512,128]{2,1,0:T(8,128)(2,1)S(1)}, u32[]{:S(2)}, u32[]{:S(2)}) %collective-permute-start.7) | collective-permute-done | bytes 1048608 | tf_op jit(solution)/shard_map/ppermute | solution.py:304
  139.9 0.0 copy-done.6
  139.9 1.4 add_convert_fusion
  141.3 0.0 all-to-all-done.3.piece
  141.4 0.0 copy-start.1
  141.4 4.4 %all-to-all-start.4 = ((bf16[8,512,128]{2,1,0:T(8,128)(2,1)}), bf16[8,512,128]{2,1,0:T(8,128)(2,1)S(1)}, u32[]{:S(2)}, u32[]{:S(2)}) async-start(bf16[8,512,128]{2,1,0:T(8,128)(2,1)} %add_convert_fusion), calls=%async_computation.4 | async-start | bytes 2097152 | tf_op jit(solution)/shard_map/all_to_all | solution.py:298
  145.8 0.0 copy-done.1
  145.8 2.5 %place.4 = (bf16[128,3072]{1,0:T(8,128)(2,1)}, bf16[128,3072]{1,0:T(8,128)(2,1)}) custom-call(bf16[8,1024,128]{2,1,0:T(8,128)(2,1)} %copy-done.1), custom_call_target="tpu_custom_call" | custom-call | tf_op jit(solution)/shard_map/place/pallas_call | solution.py:104
  148.3 3.1 %place.3 = (bf16[128,3072]{1,0:T(8,128)(2,1)}, bf16[128,3072]{1,0:T(8,128)(2,1)}) custom-call(bf16[8,1024,128]{2,1,0:T(8,128)(2,1)} %copy-done.1), custom_call_target="tpu_custom_call" | custom-call | tf_op jit(solution)/shard_map/place/pallas_call | solution.py:104
  151.5 10.3 %all-to-all-done.4.piece = bf16[8,512,128]{2,1,0:T(8,128)(2,1)S(1)} async-done(((bf16[8,512,128]{2,1,0:T(8,128)(2,1)}), bf16[8,512,128]{2,1,0:T(8,128)(2,1)S(1)}, u32[]{:S(2)}, u32[]{:S(2)}) %all-to-all-start.4) | async-done | bytes 1048608 | tf_op jit(solution)/shard_map/all_to_all | solution.py:298
  161.8 0.0 copy-start.5
  161.8 1.0 copy-done.5
  162.8 2.4 %place.5 = (bf16[128,3072]{1,0:T(8,128)(2,1)}, bf16[128,3072]{1,0:T(8,128)(2,1)}) custom-call(bf16[8,512,128]{2,1,0:T(8,128)(2,1)} %copy-done.5, bf16[128,3072]{1,0:T(8,128)(2,1)} %get-tuple-element.42.refs_0_, bf16[128,3072]{1,0:T(8,128)(2,1)} %get-tuple-element.43.refs_1_), custom_call_target="tpu_custom_call", output_to_operand_aliasing={{0}: (1, {}), {1}: (2, {})} | custom-call | tf_op jit(solution)/shard_map/place/pallas_call | solution.py:104
Async XLA Ops:
  2.9 15.2 %all-to-all-start = ((bf16[8,272,128]{2,1,0:T(8,128)(2,1)}), bf16[8,272,128]{2,1,0:T(8,128)(2,1)S(1)}, u32[]{:S(2)}, u32[]{:S(2)}) async-start(bf16[8,272,128]{2,1,0:T(8,128)(2,1)} %pack.2), calls=%async_computation | async-start | bytes 1114112 | tf_op jit(solution)/shard_map/all_to_all | solution.py:298
  18.1 26.3 %copy-start.2 = (bf16[8,272,128]{2,1,0:T(8,128)(2,1)}, bf16[8,272,128]{2,1,0:T(8,128)(2,1)S(1)}, u32[]{:S(2)}) copy-start(bf16[8,272,128]{2,1,0:T(8,128)(2,1)S(1)} %all-to-all-done.stamps_own.own_ref) | copy-start | bytes 1671172
  18.1 25.1 %all-to-all-start.1 = ((bf16[8,768,128]{2,1,0:T(8,128)(2,1)}), bf16[8,768,128]{2,1,0:T(8,128)(2,1)S(1)}, u32[]{:S(2)}, u32[]{:S(2)}) async-start(bf16[8,768,128]{2,1,0:T(8,128)(2,1)} %get-tuple-element.27), calls=%async_computation.1 | async-start | bytes 3145728 | tf_op jit(solution)/shard_map/all_to_all | solution.py:298
  21.7 22.7 %collective-permute-start.1 = (bf16[8,272,128]{2,1,0:T(8,128)(2,1)S(1)}, bf16[8,272,128]{2,1,0:T(8,128)(2,1)S(1)}, u32[]{:S(2)}, u32[]{:S(2)}) collective-permute-start(bf16[8,272,128]{2,1,0:T(8,128)(2,1)S(1)} %all-to-all-done.stamps_own.own_ref), channel_id=1, source_target_pairs={{8,0},{16,8},{24,16},{32,24},{40,32},{48,40},{56,48},{64,56},{72,6... | collective-permute-start | bytes 1671176 | tf_op jit(solution)/shard_map/ppermute | solution.py:304
  26.2 18.6 %collective-permute-start = (bf16[8,272,128]{2,1,0:T(8,128)(2,1)S(1)}, bf16[8,272,128]{2,1,0:T(8,128)(2,1)S(1)}, u32[]{:S(2)}, u32[]{:S(2)}) collective-permute-start(bf16[8,272,128]{2,1,0:T(8,128)(2,1)S(1)} %all-to-all-done.stamps_own.own_ref), channel_id=1, source_target_pairs={{0,8},{8,16},{16,24},{24,32},{32,40},{40,48},{48,56},{56,64},{64,7... | collective-permute-start | bytes 1671176 | tf_op jit(solution)/shard_map/ppermute | solution.py:304
  43.2 7.7 %copy-start = (bf16[8,768,128]{2,1,0:T(8,128)(2,1)}, bf16[8,768,128]{2,1,0:T(8,128)(2,1)S(1)}, u32[]{:S(2)}) copy-start(bf16[8,768,128]{2,1,0:T(8,128)(2,1)S(1)} %all-to-all-done.1.qg_ref.own_ref) | copy-start | bytes 4718596
  44.4 10.8 %copy-start.3 = (bf16[8,272,128]{2,1,0:T(8,128)(2,1)}, bf16[8,272,128]{2,1,0:T(8,128)(2,1)S(1)}, u32[]{:S(2)}) copy-start(bf16[8,272,128]{2,1,0:T(8,128)(2,1)S(1)} %collective-permute-done.1.stamps_right.right_ref) | copy-start | bytes 1671172
  44.8 10.3 %copy-start.4 = (bf16[8,272,128]{2,1,0:T(8,128)(2,1)}, bf16[8,272,128]{2,1,0:T(8,128)(2,1)S(1)}, u32[]{:S(2)}) copy-start(bf16[8,272,128]{2,1,0:T(8,128)(2,1)S(1)} %collective-permute-done.stamps_left.left_ref) | copy-start | bytes 1671172
  44.8 31.5 %collective-permute-start.3 = (bf16[8,512,128]{2,1,0:T(8,128)(2,1)}, bf16[8,512,128]{2,1,0:T(8,128)(2,1)}, u32[]{:S(2)}, u32[]{:S(2)}) collective-permute-start(bf16[8,512,128]{2,1,0:T(8,128)(2,1)} %slice.4), channel_id=1, source_target_pairs={{8,0},{16,8},{24,16},{32,24},{40,32},{48,40},{56,48},{64,56},{72,6... | collective-permute-start | bytes 3145736 | tf_op jit(solution)/shard_map/ppermute | solution.py:304
  48.9 28.7 %collective-permute-start.2 = (bf16[8,512,128]{2,1,0:T(8,128)(2,1)}, bf16[8,512,128]{2,1,0:T(8,128)(2,1)}, u32[]{:S(2)}, u32[]{:S(2)}) collective-permute-start(bf16[8,512,128]{2,1,0:T(8,128)(2,1)} %slice.4), channel_id=1, source_target_pairs={{0,8},{8,16},{16,24},{24,32},{32,40},{40,48},{48,56},{56,64},{64,7... | collective-permute-start | bytes 3145736 | tf_op jit(solution)/shard_map/ppermute | solution.py:304
  50.9 25.5 %all-to-all-start.2 = ((bf16[8,512,128]{2,1,0:T(8,128)(2,1)}), bf16[8,512,128]{2,1,0:T(8,128)(2,1)}, u32[]{:S(2)}, u32[]{:S(2)}) async-start(bf16[8,512,128]{2,1,0:T(8,128)(2,1)} %get-tuple-element.28), calls=%async_computation.2 | async-start | bytes 2097152 | tf_op jit(solution)/shard_map/all_to_all | solution.py:298
  68.2 31.6 %collective-permute-start.4 = (bf16[8,256,128]{2,1,0:T(8,128)(2,1)}, bf16[8,256,128]{2,1,0:T(8,128)(2,1)S(1)}, u32[]{:S(2)}, u32[]{:S(2)}) collective-permute-start(bf16[8,256,128]{2,1,0:T(8,128)(2,1)} %get-tuple-element.33), channel_id=1, source_target_pairs={{8,0},{16,8},{24,16},{32,24},{40,32},{48,40},{56,48},{64,56},{72,6... | collective-permute-start | bytes 1572872 | tf_op jit(solution)/shard_map/ppermute | solution.py:304
  74.2 25.6 %collective-permute-start.5 = (bf16[8,256,128]{2,1,0:T(8,128)(2,1)}, bf16[8,256,128]{2,1,0:T(8,128)(2,1)S(1)}, u32[]{:S(2)}, u32[]{:S(2)}) collective-permute-start(bf16[8,256,128]{2,1,0:T(8,128)(2,1)} %get-tuple-element.34), channel_id=1, source_target_pairs={{0,8},{8,16},{16,24},{24,32},{32,40},{40,48},{48,56},{56,64},{64,7... | collective-permute-start | bytes 1572872 | tf_op jit(solution)/shard_map/ppermute | solution.py:304
  77.7 22.2 %copy-start.7 = (bf16[8,256,128]{2,1,0:T(8,128)(2,1)S(1)}, bf16[8,256,128]{2,1,0:T(8,128)(2,1)}, u32[]{:S(2)}) copy-start(bf16[8,256,128]{2,1,0:T(8,128)(2,1)} %get-tuple-element.32) | copy-start | bytes 1572868
  100.9 39.0 %copy-start.6 = (bf16[8,512,128]{2,1,0:T(8,128)(2,1)S(1)}, bf16[8,512,128]{2,1,0:T(8,128)(2,1)}, u32[]{:S(2)}) copy-start(bf16[8,512,128]{2,1,0:T(8,128)(2,1)} %get-tuple-element.37) | copy-start | bytes 3145732
  100.9 40.4 %all-to-all-start.3 = ((bf16[8,1024,128]{2,1,0:T(8,128)(2,1)}), bf16[8,1024,128]{2,1,0:T(8,128)(2,1)S(1)}, u32[]{:S(2)}, u32[]{:S(2)}) async-start(bf16[8,1024,128]{2,1,0:T(8,128)(2,1)} %fusion), calls=%async_computation.3 | async-start | bytes 4194304 | tf_op jit(solution)/shard_map/all_to_all | solution.py:298
  104.6 29.2 %collective-permute-start.6 = (bf16[8,512,128]{2,1,0:T(8,128)(2,1)}, bf16[8,512,128]{2,1,0:T(8,128)(2,1)S(1)}, u32[]{:S(2)}, u32[]{:S(2)}) collective-permute-start(bf16[8,512,128]{2,1,0:T(8,128)(2,1)} %get-tuple-element.40), channel_id=1, source_target_pairs={{8,0},{16,8},{24,16},{32,24},{40,32},{48,40},{56,48},{64,56},{72,6... | collective-permute-start | bytes 3145736 | tf_op jit(solution)/shard_map/ppermute | solution.py:304
  110.4 29.5 %collective-permute-start.7 = (bf16[8,512,128]{2,1,0:T(8,128)(2,1)}, bf16[8,512,128]{2,1,0:T(8,128)(2,1)S(1)}, u32[]{:S(2)}, u32[]{:S(2)}) collective-permute-start(bf16[8,512,128]{2,1,0:T(8,128)(2,1)} %get-tuple-element.41), channel_id=1, source_target_pairs={{0,8},{8,16},{16,24},{24,32},{32,40},{40,48},{48,56},{56,64},{64,7... | collective-permute-start | bytes 3145736 | tf_op jit(solution)/shard_map/ppermute | solution.py:304
  141.4 4.5 %copy-start.1 = (bf16[8,1024,128]{2,1,0:T(8,128)(2,1)}, bf16[8,1024,128]{2,1,0:T(8,128)(2,1)S(1)}, u32[]{:S(2)}) copy-start(bf16[8,1024,128]{2,1,0:T(8,128)(2,1)S(1)} %all-to-all-done.3.piece) | copy-start | bytes 6291460
  141.4 20.4 %all-to-all-start.4 = ((bf16[8,512,128]{2,1,0:T(8,128)(2,1)}), bf16[8,512,128]{2,1,0:T(8,128)(2,1)S(1)}, u32[]{:S(2)}, u32[]{:S(2)}) async-start(bf16[8,512,128]{2,1,0:T(8,128)(2,1)} %add_convert_fusion), calls=%async_computation.4 | async-start | bytes 2097152 | tf_op jit(solution)/shard_map/all_to_all | solution.py:298
  161.8 1.0 copy-start.5

commit v4 on v3

--- a/solution.py
+++ b/solution.py
@@ -21,9 +21,10 @@
 STAMP_ROWS = 16
 STAMP_BASE = 32
 RANGES = 2
-UNROLL = True
+TILE = 2560
 REACH = 2
 VMEM_BYTES = 56 * 1024 * 1024
+PLACE_BYTES = 8 * 1024 * 1024
 
 
 def dot(lhs, rhs, dims):
@@ -108,7 +109,7 @@
         out_shape=[shape] * 2,
         input_output_aliases={1 + at: at for at in range(len(outs))},
         scratch_shapes=[pltpu.SemaphoreType.DMA((2 * peers * len(chunk),))],
-        compiler_params=pltpu.CompilerParams(vmem_limit_bytes=VMEM_BYTES),
+        compiler_params=pltpu.CompilerParams(vmem_limit_bytes=PLACE_BYTES),
         name="place",
     )(piece, *outs)
 
@@ -133,27 +134,28 @@
     skip = 4 - sum(fresh)
     result_ref, to_left_ref, own_sum_ref, to_right_ref = refs[skip : skip + 4]
     (
-        stamps,
+        stamps, keys, values,
         scores, key_sums, value_sums, total_t, query_t,
     ) = refs[skip + 4 :]
     rows = size // per
-    span = 2 * REACH + 1
+    span = (2 * REACH + 1) * size // TILE
 
     @pl.when(pl.program_id(0) == 0)
     def _():
         for side, ref in enumerate((stamps_left, stamps_own, stamps_right)):
             for block in range(RANGES * per):
-                place = side * RANGES + block // per
-                spread = spread_stamps(ref[block], (place - RANGES) * SHARD_MS)
-                stamps[place, pl.ds(block % per * rows, rows)] = spread
-
-    def slots(place, which):
+                place = side * RANGES * per + block
+                spread = spread_stamps(ref[block], (place // per - RANGES) * SHARD_MS)
+                stamps[pl.ds(place * rows, rows)] = spread
+
+    for place in range(3 * RANGES):
         ref = (left_ref, own_ref, right_ref)[place // RANGES]
-        found = ref[pl.ds(place % RANGES * per, per), pl.ds(which * rows, rows)]
-        return found.reshape(size, DH)
-
-    keys = [slots(place, 0) for place in range(3 * RANGES)]
-    values = [slots(place, 1) for place in range(3 * RANGES)]
+        part = pl.ds(place % RANGES * per, per)
+        keys[pl.ds(place * size, size)] = ref[part, pl.ds(0, rows)].reshape(size, DH)
+        values[pl.ds(place * size, size)] = ref[part, pl.ds(rows, rows)].reshape(size, DH)
+    tail = pl.ds((2 * REACH + 1) * size, size)
+    key_sums[tail] = jnp.zeros((size, DH), jnp.float32)
+    value_sums[tail] = jnp.zeros((size, DH), jnp.float32)
     offsets = lax.broadcasted_iota(jnp.int32, (1, size), 1) * SHARD_MS // size
     blocks = [pl.ds(part * per, per) for part in range(RANGES)]
     query = [qg_ref[block, pl.ds(0, rows)].reshape(size, DH) for block in blocks]
@@ -170,25 +172,25 @@
         return carry
 
     def score_step(part, step, top):
-        place = step + part
+        place = pl.ds(part * size + step * TILE, TILE)
         found = dot_nt(keys[place], query[part])
         near = jnp.abs(jnp.tile(stamps[place], (1, size // DH)) - stamp[part]) <= RADIUS_MS
         found = jnp.where(near, found * (SCALE * LOG2E), NEG_FILL)
         scores[part, step] = found
-        return jnp.maximum(top, jnp.max(found.reshape(size // 8, 8, size), axis=0))
+        return jnp.maximum(top, jnp.max(found.reshape(TILE // 8, 8, size), axis=0))
 
     def weight_step(part, step, total):
-        place = step + part
+        place = pl.ds(part * size + step * TILE, TILE)
         raised = jnp.exp2(scores[part, step] - top[part])
         scores[part, step] = raised
         add(total_t, part, step == 0, dot(values[place], raised.astype(jnp.bfloat16), ((0,), (0,))))
-        return total + jnp.sum(raised.reshape(size // 8, 8, size), axis=0)
+        return total + jnp.sum(raised.reshape(TILE // 8, 8, size), axis=0)
 
     def grad_step(part, step):
-        place = step + part
+        place = pl.ds(part * size + step * TILE, TILE)
         weights = scores[part, step] * inverse[part]
         slopes = (weights * (dot_nt(values[place], grad[part]) - row_dot[part])).astype(jnp.bfloat16)
-        fresh = part == 0 or step == span - 1
+        fresh = part == 0
         add(value_sums, place, fresh, dot_nn(weights.astype(jnp.bfloat16), grad[part]))
         add(key_sums, place, fresh, dot_nn(slopes, query[part]))
         add(query_t, part, step == 0, dot(keys[place], slopes, ((0,), (0,))))
@@ -234,7 +236,7 @@
     finish_query(1)
     for side, ref in enumerate((to_left_ref, own_sum_ref, to_right_ref)):
         for part in range(RANGES):
-            place = side * RANGES + part
+            place = pl.ds((side * RANGES + part) * size, size)
             shape = (per, rows, DH)
             ref[blocks[part], pl.ds(0, rows)] = (key_sums[place] * SCALE).astype(ref.dtype).reshape(shape)
             ref[blocks[part], pl.ds(rows, rows)] = value_sums[place].astype(ref.dtype).reshape(shape)
@@ -279,10 +281,12 @@
         ],
         input_output_aliases=aliases,
         scratch_shapes=[
-            pltpu.VMEM((places, size, DH), jnp.float32),
-            pltpu.VMEM((RANGES, span, size, size), jnp.float32),
-            pltpu.VMEM((places, size, DH), jnp.float32),
-            pltpu.VMEM((places, size, DH), jnp.float32),
+            pltpu.VMEM((places * size, DH), jnp.float32),
+            pltpu.VMEM((places * size, DH), jnp.bfloat16),
+            pltpu.VMEM((places * size, DH), jnp.bfloat16),
+            pltpu.VMEM((RANGES, span * size // TILE, TILE, size), jnp.float32),
+            pltpu.VMEM((places * size, DH), jnp.float32),
+            pltpu.VMEM((places * size, DH), jnp.float32),
             pltpu.VMEM((RANGES, DH, size), jnp.float32),
             pltpu.VMEM((RANGES, DH, size), jnp.float32),
         ],

time: 166 us -> 163 us (0.982)
  Pallas kernels: 49.4 us -> 44.4 us
  waiting for transfers between devices: 61.5 us -> 64.9 us
    pallas_call x3, Pallas kernels: 8.09 us -> 3.68 us  [place(): pl.pallas_call(functools.partial(place_kernel, peers, heads, chunk, offse...]
    all_to_all x5, waiting for transfers between devices: 32.2 us -> 35.4 us  [swap(): return lax.all_to_all(value, GROUP, split_axis=0, concat_axis=0, tiled=True)]
  transfers between devices with their start and end apart: 13 -> 13, of which waited for: 7 -> 7; matrix products, arithmetic and copies ran while one was open for 2% -> 2% of each run, Pallas kernels for 27% -> 25%
where the time goes in v4:
time: 163 us
  waiting for transfers between devices  64.9 us (40%)
  starting transfers between devices  48.7 us (30%)
  Pallas kernels  44.4 us (27%)
  other arithmetic  2.43 us (1%)
    all_to_all x5, waiting for transfers between devices, swap(): return lax.all_to_all(value, GROUP, split_axis=0, concat_axis=0, tiled=True)  35.4 us
    pallas_call x2, Pallas kernels, attend(): pl.pallas_call(functools.partial(attend_kernel, per, size, fresh), grid=(...  34.6 us
    ppermute x8, waiting for transfers between devices, shifted(): lax.ppermute(value, 'col', [(at, at + steps) for at in range(first, last)])  29.5 us
    ppermute x8, starting transfers between devices, shifted(): lax.ppermute(value, 'col', [(at, at + steps) for at in range(first, last)])  28.2 us
    all_to_all x5, starting transfers between devices, swap(): return lax.all_to_all(value, GROUP, split_axis=0, concat_axis=0, tiled=True)  20.5 us
    pallas_call x2, Pallas kernels, pack(): pl.pallas_call(functools.partial(pack_kernel, peers, width // DH // peers...  6.13 us
    pallas_call x3, Pallas kernels, place(): pl.pallas_call(functools.partial(place_kernel, peers, heads, chunk, offse...  3.68 us
  transfers between devices with their start and end apart: 13, of which 7 were waited for; matrix products, arithmetic and copies ran while one was open for 2% of the time, Pallas kernels for 25%

profile of v4, /device:TPU:96, one launch (start us, length us, event | category | flops | bytes accessed | tf_op | source)
XLA Modules:
  0.0 162.6 jit_solution(10931150206837256203)
XLA Ops:
  0.6 2.3 %pack.2 = bf16[8,272,128]{2,1,0:T(8,128)(2,1)} custom-call(bf16[128,3072]{1,0:T(8,128)(2,1)} %refs_0_.3, bf16[128,3072]{1,0:T(8,128)(2,1)} %refs_1_.3, s32[1,128]{1,0:T(1,128)} %bitcast.1), custom_call_target="tpu_custom_call" | custom-call | tf_op jit(solution)/shard_map/pack/pallas_call | solution.py:66
  2.9 4.5 %all-to-all-start = ((bf16[8,272,128]{2,1,0:T(8,128)(2,1)}), bf16[8,272,128]{2,1,0:T(8,128)(2,1)S(1)}, u32[]{:S(2)}, u32[]{:S(2)}) async-start(bf16[8,272,128]{2,1,0:T(8,128)(2,1)} %pack.2), calls=%async_computation | async-start | bytes 1114112 | tf_op jit(solution)/shard_map/all_to_all | solution.py:302
  7.4 3.8 %pack.3 = (bf16[8,768,128]{2,1,0:T(8,128)(2,1)}, bf16[8,512,128]{2,1,0:T(8,128)(2,1)}) custom-call(bf16[128,3072]{1,0:T(8,128)(2,1)} %refs_0_.3, bf16[128,3072]{1,0:T(8,128)(2,1)} %refs_1_.3, bf16[128,3072]{1,0:T(8,128)(2,1)} %refs_2_.1, bf16[128,3072]{1,0:T(8,128)(2,1)} %refs_3_.1), custom_call_target="tpu_custom_call" | custom-call | tf_op jit(solution)/shard_map/pack/pallas_call | solution.py:66
  11.2 6.9 %all-to-all-done.stamps_own.own_ref = bf16[8,272,128]{2,1,0:T(8,128)(2,1)S(1)} async-done(((bf16[8,272,128]{2,1,0:T(8,128)(2,1)}), bf16[8,272,128]{2,1,0:T(8,128)(2,1)S(1)}, u32[]{:S(2)}, u32[]{:S(2)}) %all-to-all-start) | async-done | bytes 557088 | tf_op jit(solution)/shard_map/all_to_all | solution.py:302
  18.1 0.0 copy-start.1
  18.1 3.6 %all-to-all-start.1 = ((bf16[8,768,128]{2,1,0:T(8,128)(2,1)}), bf16[8,768,128]{2,1,0:T(8,128)(2,1)S(1)}, u32[]{:S(2)}, u32[]{:S(2)}) async-start(bf16[8,768,128]{2,1,0:T(8,128)(2,1)} %get-tuple-element.27), calls=%async_computation.1 | async-start | bytes 3145728 | tf_op jit(solution)/shard_map/all_to_all | solution.py:302
  21.7 4.5 %collective-permute-start.1 = (bf16[8,272,128]{2,1,0:T(8,128)(2,1)S(1)}, bf16[8,272,128]{2,1,0:T(8,128)(2,1)S(1)}, u32[]{:S(2)}, u32[]{:S(2)}) collective-permute-start(bf16[8,272,128]{2,1,0:T(8,128)(2,1)S(1)} %all-to-all-done.stamps_own.own_ref), channel_id=1, source_target_pairs={{8,0},{16,8},{24,16},{32,24},{40,32},{48,40},{56,48},{64,56},{72,6... | collective-permute-start | bytes 1671176 | tf_op jit(solution)/shard_map/ppermute | solution.py:308
  26.2 1.9 %collective-permute-start = (bf16[8,272,128]{2,1,0:T(8,128)(2,1)S(1)}, bf16[8,272,128]{2,1,0:T(8,128)(2,1)S(1)}, u32[]{:S(2)}, u32[]{:S(2)}) collective-permute-start(bf16[8,272,128]{2,1,0:T(8,128)(2,1)S(1)} %all-to-all-done.stamps_own.own_ref), channel_id=1, source_target_pairs={{0,8},{8,16},{16,24},{24,32},{32,40},{40,48},{48,56},{56,64},{64,7... | collective-permute-start | bytes 1671176 | tf_op jit(solution)/shard_map/ppermute | solution.py:308
  28.1 15.0 %all-to-all-done.1.qg_ref.own_ref = bf16[8,768,128]{2,1,0:T(8,128)(2,1)S(1)} async-done(((bf16[8,768,128]{2,1,0:T(8,128)(2,1)}), bf16[8,768,128]{2,1,0:T(8,128)(2,1)S(1)}, u32[]{:S(2)}, u32[]{:S(2)}) %all-to-all-start.1) | async-done | bytes 1572896 | tf_op jit(solution)/shard_map/all_to_all | solution.py:302
  43.2 0.0 copy-start
  43.2 1.2 slice.4
  44.4 0.0 copy-done.1
  44.4 0.0 collective-permute-done.1.stamps_right.right_ref
  44.4 0.0 copy-start.2
  44.4 0.4 collective-permute-done.stamps_left.left_ref
  44.8 0.0 copy-start.3
  44.8 4.1 %collective-permute-start.3 = (bf16[8,512,128]{2,1,0:T(8,128)(2,1)}, bf16[8,512,128]{2,1,0:T(8,128)(2,1)}, u32[]{:S(2)}, u32[]{:S(2)}) collective-permute-start(bf16[8,512,128]{2,1,0:T(8,128)(2,1)} %slice.4), channel_id=1, source_target_pairs={{8,0},{16,8},{24,16},{32,24},{40,32},{48,40},{56,48},{64,56},{72,6... | collective-permute-start | bytes 3145736 | tf_op jit(solution)/shard_map/ppermute | solution.py:308
  48.9 1.9 %collective-permute-start.2 = (bf16[8,512,128]{2,1,0:T(8,128)(2,1)}, bf16[8,512,128]{2,1,0:T(8,128)(2,1)}, u32[]{:S(2)}, u32[]{:S(2)}) collective-permute-start(bf16[8,512,128]{2,1,0:T(8,128)(2,1)} %slice.4), channel_id=1, source_target_pairs={{0,8},{8,16},{16,24},{24,32},{32,40},{40,48},{48,56},{56,64},{64,7... | collective-permute-start | bytes 3145736 | tf_op jit(solution)/shard_map/ppermute | solution.py:308
  50.9 0.0 copy-done
  50.9 4.3 %all-to-all-start.2 = ((bf16[8,512,128]{2,1,0:T(8,128)(2,1)}), bf16[8,512,128]{2,1,0:T(8,128)(2,1)}, u32[]{:S(2)}, u32[]{:S(2)}) async-start(bf16[8,512,128]{2,1,0:T(8,128)(2,1)} %get-tuple-element.28), calls=%async_computation.2 | async-start | bytes 2097152 | tf_op jit(solution)/shard_map/all_to_all | solution.py:302
  55.2 0.0 copy-done.2
  55.2 0.0 copy-done.3
  55.2 12.9 %attend.2 = (bf16[8,1024,128]{2,1,0:T(8,128)(2,1)}, bf16[8,256,128]{2,1,0:T(8,128)(2,1)}, bf16[8,256,128]{2,1,0:T(8,128)(2,1)}, bf16[8,256,128]{2,1,0:T(8,128)(2,1)}) custom-call(bf16[8,272,128]{2,1,0:T(8,128)(2,1)} %copy-done.3, bf16[8,272,128]{2,1,0:T(8,128)(2,1)} %copy-done.1, bf16[8,272,128]{2,1,0:T(8,128)(2,1)} %copy-done.2, ...), custom_call_target="tpu_custom_call" | custom-call | flops 1 | bytes 1 | tf_op jit(solution)/shard_map/attend/pallas_call | solution.py:273
  68.1 6.0 %collective-permute-start.4 = (bf16[8,256,128]{2,1,0:T(8,128)(2,1)}, bf16[8,256,128]{2,1,0:T(8,128)(2,1)S(1)}, u32[]{:S(2)}, u32[]{:S(2)}) collective-permute-start(bf16[8,256,128]{2,1,0:T(8,128)(2,1)} %get-tuple-element.33), channel_id=1, source_target_pairs={{8,0},{16,8},{24,16},{32,24},{40,32},{48,40},{56,48},{64,56},{72,6... | collective-permute-start | bytes 1572872 | tf_op jit(solution)/shard_map/ppermute | solution.py:308
  74.1 2.1 %collective-permute-start.5 = (bf16[8,256,128]{2,1,0:T(8,128)(2,1)}, bf16[8,256,128]{2,1,0:T(8,128)(2,1)S(1)}, u32[]{:S(2)}, u32[]{:S(2)}) collective-permute-start(bf16[8,256,128]{2,1,0:T(8,128)(2,1)} %get-tuple-element.34), channel_id=1, source_target_pairs={{0,8},{8,16},{16,24},{24,32},{32,40},{40,48},{48,56},{56,64},{64,7... | collective-permute-start | bytes 1572872 | tf_op jit(solution)/shard_map/ppermute | solution.py:308
  76.2 0.0 all-to-all-done.2.qg_ref
  76.2 0.0 collective-permute-done.3.right_ref
  76.2 1.5 collective-permute-done.2.left_ref
  77.7 0.0 copy-start.5
  77.7 21.7 %attend.3 = (bf16[8,1024,128]{2,1,0:T(8,128)(2,1)}, bf16[8,512,128]{2,1,0:T(8,128)(2,1)}, bf16[8,512,128]{2,1,0:T(8,128)(2,1)}, bf16[8,512,128]{2,1,0:T(8,128)(2,1)}) custom-call(bf16[8,272,128]{2,1,0:T(8,128)(2,1)} %copy-done.3, bf16[8,272,128]{2,1,0:T(8,128)(2,1)} %copy-done.1, bf16[8,272,128]{2,1,0:T(8,128)(2,1)} %copy-done.2, ...), custom_call_target="tpu_custom_call", output_to_operand_aliasing={{0}: (7, {})} | custom-call | flops 1 | bytes 1 | tf_op jit(solution)/shard_map/attend/pallas_call | solution.py:273
  99.4 0.0 collective-permute-done.4
  99.4 0.0 collective-permute-done.5
  99.4 0.0 copy-done.5
  99.4 1.0 fusion
  100.5 0.0 copy-start.4
  100.5 3.7 %all-to-all-start.3 = ((bf16[8,1024,128]{2,1,0:T(8,128)(2,1)}), bf16[8,1024,128]{2,1,0:T(8,128)(2,1)S(1)}, u32[]{:S(2)}, u32[]{:S(2)}) async-start(bf16[8,1024,128]{2,1,0:T(8,128)(2,1)} %fusion), calls=%async_computation.3 | async-start | bytes 4194304 | tf_op jit(solution)/shard_map/all_to_all | solution.py:302
  104.2 5.7 %collective-permute-start.6 = (bf16[8,512,128]{2,1,0:T(8,128)(2,1)}, bf16[8,512,128]{2,1,0:T(8,128)(2,1)S(1)}, u32[]{:S(2)}, u32[]{:S(2)}) collective-permute-start(bf16[8,512,128]{2,1,0:T(8,128)(2,1)} %get-tuple-element.40), channel_id=1, source_target_pairs={{8,0},{16,8},{24,16},{32,24},{40,32},{48,40},{56,48},{64,56},{72,6... | collective-permute-start | bytes 3145736 | tf_op jit(solution)/shard_map/ppermute | solution.py:308
  109.9 1.9 %collective-permute-start.7 = (bf16[8,512,128]{2,1,0:T(8,128)(2,1)}, bf16[8,512,128]{2,1,0:T(8,128)(2,1)S(1)}, u32[]{:S(2)}, u32[]{:S(2)}) collective-permute-start(bf16[8,512,128]{2,1,0:T(8,128)(2,1)} %get-tuple-element.41), channel_id=1, source_target_pairs={{0,8},{8,16},{16,24},{24,32},{32,40},{40,48},{48,56},{56,64},{64,7... | collective-permute-start | bytes 3145736 | tf_op jit(solution)/shard_map/ppermute | solution.py:308
  111.8 21.5 %collective-permute-done.6 = bf16[8,512,128]{2,1,0:T(8,128)(2,1)S(1)} collective-permute-done((bf16[8,512,128]{2,1,0:T(8,128)(2,1)}, bf16[8,512,128]{2,1,0:T(8,128)(2,1)S(1)}, u32[]{:S(2)}, u32[]{:S(2)}) %collective-permute-start.6) | collective-permute-done | bytes 1048608 | tf_op jit(solution)/shard_map/ppermute | solution.py:308
  133.3 6.1 %collective-permute-done.7 = bf16[8,512,128]{2,1,0:T(8,128)(2,1)S(1)} collective-permute-done((bf16[8,512,128]{2,1,0:T(8,128)(2,1)}, bf16[8,512,128]{2,1,0:T(8,128)(2,1)S(1)}, u32[]{:S(2)}, u32[]{:S(2)}) %collective-permute-start.7) | collective-permute-done | bytes 1048608 | tf_op jit(solution)/shard_map/ppermute | solution.py:308
  139.4 0.0 copy-done.4
  139.4 1.4 add_convert_fusion
  140.8 0.0 all-to-all-done.3.piece
  140.8 4.4 %all-to-all-start.4 = ((bf16[8,512,128]{2,1,0:T(8,128)(2,1)}), bf16[8,512,128]{2,1,0:T(8,128)(2,1)S(1)}, u32[]{:S(2)}, u32[]{:S(2)}) async-start(bf16[8,512,128]{2,1,0:T(8,128)(2,1)} %add_convert_fusion), calls=%async_computation.4 | async-start | bytes 2097152 | tf_op jit(solution)/shard_map/all_to_all | solution.py:302
  145.3 0.9 place.4
  146.2 1.5 place.3
  147.7 13.5 %all-to-all-done.4.piece = bf16[8,512,128]{2,1,0:T(8,128)(2,1)S(1)} async-done(((bf16[8,512,128]{2,1,0:T(8,128)(2,1)}), bf16[8,512,128]{2,1,0:T(8,128)(2,1)S(1)}, u32[]{:S(2)}, u32[]{:S(2)}) %all-to-all-start.4) | async-done | bytes 1048608 | tf_op jit(solution)/shard_map/all_to_all | solution.py:302
  161.2 1.2 place.5
Async XLA Ops:
  2.9 15.2 %all-to-all-start = ((bf16[8,272,128]{2,1,0:T(8,128)(2,1)}), bf16[8,272,128]{2,1,0:T(8,128)(2,1)S(1)}, u32[]{:S(2)}, u32[]{:S(2)}) async-start(bf16[8,272,128]{2,1,0:T(8,128)(2,1)} %pack.2), calls=%async_computation | async-start | bytes 1114112 | tf_op jit(solution)/shard_map/all_to_all | solution.py:302
  18.1 26.3 %copy-start.1 = (bf16[8,272,128]{2,1,0:T(8,128)(2,1)}, bf16[8,272,128]{2,1,0:T(8,128)(2,1)S(1)}, u32[]{:S(2)}) copy-start(bf16[8,272,128]{2,1,0:T(8,128)(2,1)S(1)} %all-to-all-done.stamps_own.own_ref) | copy-start | bytes 1671172
  18.1 25.1 %all-to-all-start.1 = ((bf16[8,768,128]{2,1,0:T(8,128)(2,1)}), bf16[8,768,128]{2,1,0:T(8,128)(2,1)S(1)}, u32[]{:S(2)}, u32[]{:S(2)}) async-start(bf16[8,768,128]{2,1,0:T(8,128)(2,1)} %get-tuple-element.27), calls=%async_computation.1 | async-start | bytes 3145728 | tf_op jit(solution)/shard_map/all_to_all | solution.py:302
  21.7 22.7 %collective-permute-start.1 = (bf16[8,272,128]{2,1,0:T(8,128)(2,1)S(1)}, bf16[8,272,128]{2,1,0:T(8,128)(2,1)S(1)}, u32[]{:S(2)}, u32[]{:S(2)}) collective-permute-start(bf16[8,272,128]{2,1,0:T(8,128)(2,1)S(1)} %all-to-all-done.stamps_own.own_ref), channel_id=1, source_target_pairs={{8,0},{16,8},{24,16},{32,24},{40,32},{48,40},{56,48},{64,56},{72,6... | collective-permute-start | bytes 1671176 | tf_op jit(solution)/shard_map/ppermute | solution.py:308
  26.2 18.6 %collective-permute-start = (bf16[8,272,128]{2,1,0:T(8,128)(2,1)S(1)}, bf16[8,272,128]{2,1,0:T(8,128)(2,1)S(1)}, u32[]{:S(2)}, u32[]{:S(2)}) collective-permute-start(bf16[8,272,128]{2,1,0:T(8,128)(2,1)S(1)} %all-to-all-done.stamps_own.own_ref), channel_id=1, source_target_pairs={{0,8},{8,16},{16,24},{24,32},{32,40},{40,48},{48,56},{56,64},{64,7... | collective-permute-start | bytes 1671176 | tf_op jit(solution)/shard_map/ppermute | solution.py:308
  43.2 7.7 %copy-start = (bf16[8,768,128]{2,1,0:T(8,128)(2,1)}, bf16[8,768,128]{2,1,0:T(8,128)(2,1)S(1)}, u32[]{:S(2)}) copy-start(bf16[8,768,128]{2,1,0:T(8,128)(2,1)S(1)} %all-to-all-done.1.qg_ref.own_ref) | copy-start | bytes 4718596
  44.4 10.8 %copy-start.2 = (bf16[8,272,128]{2,1,0:T(8,128)(2,1)}, bf16[8,272,128]{2,1,0:T(8,128)(2,1)S(1)}, u32[]{:S(2)}) copy-start(bf16[8,272,128]{2,1,0:T(8,128)(2,1)S(1)} %collective-permute-done.1.stamps_right.right_ref) | copy-start | bytes 1671172
  44.8 10.3 %copy-start.3 = (bf16[8,272,128]{2,1,0:T(8,128)(2,1)}, bf16[8,272,128]{2,1,0:T(8,128)(2,1)S(1)}, u32[]{:S(2)}) copy-start(bf16[8,272,128]{2,1,0:T(8,128)(2,1)S(1)} %collective-permute-done.stamps_left.left_ref) | copy-start | bytes 1671172
  44.8 31.4 %collective-permute-start.3 = (bf16[8,512,128]{2,1,0:T(8,128)(2,1)}, bf16[8,512,128]{2,1,0:T(8,128)(2,1)}, u32[]{:S(2)}, u32[]{:S(2)}) collective-permute-start(bf16[8,512,128]{2,1,0:T(8,128)(2,1)} %slice.4), channel_id=1, source_target_pairs={{8,0},{16,8},{24,16},{32,24},{40,32},{48,40},{56,48},{64,56},{72,6... | collective-permute-start | bytes 3145736 | tf_op jit(solution)/shard_map/ppermute | solution.py:308
  48.9 28.7 %collective-permute-start.2 = (bf16[8,512,128]{2,1,0:T(8,128)(2,1)}, bf16[8,512,128]{2,1,0:T(8,128)(2,1)}, u32[]{:S(2)}, u32[]{:S(2)}) collective-permute-start(bf16[8,512,128]{2,1,0:T(8,128)(2,1)} %slice.4), channel_id=1, source_target_pairs={{0,8},{8,16},{16,24},{24,32},{32,40},{40,48},{48,56},{56,64},{64,7... | collective-permute-start | bytes 3145736 | tf_op jit(solution)/shard_map/ppermute | solution.py:308
  50.9 25.3 %all-to-all-start.2 = ((bf16[8,512,128]{2,1,0:T(8,128)(2,1)}), bf16[8,512,128]{2,1,0:T(8,128)(2,1)}, u32[]{:S(2)}, u32[]{:S(2)}) async-start(bf16[8,512,128]{2,1,0:T(8,128)(2,1)} %get-tuple-element.28), calls=%async_computation.2 | async-start | bytes 2097152 | tf_op jit(solution)/shard_map/all_to_all | solution.py:302
  68.1 31.3 %collective-permute-start.4 = (bf16[8,256,128]{2,1,0:T(8,128)(2,1)}, bf16[8,256,128]{2,1,0:T(8,128)(2,1)S(1)}, u32[]{:S(2)}, u32[]{:S(2)}) collective-permute-start(bf16[8,256,128]{2,1,0:T(8,128)(2,1)} %get-tuple-element.33), channel_id=1, source_target_pairs={{8,0},{16,8},{24,16},{32,24},{40,32},{48,40},{56,48},{64,56},{72,6... | collective-permute-start | bytes 1572872 | tf_op jit(solution)/shard_map/ppermute | solution.py:308
  74.1 25.3 %collective-permute-start.5 = (bf16[8,256,128]{2,1,0:T(8,128)(2,1)}, bf16[8,256,128]{2,1,0:T(8,128)(2,1)S(1)}, u32[]{:S(2)}, u32[]{:S(2)}) collective-permute-start(bf16[8,256,128]{2,1,0:T(8,128)(2,1)} %get-tuple-element.34), channel_id=1, source_target_pairs={{0,8},{8,16},{16,24},{24,32},{32,40},{40,48},{48,56},{56,64},{64,7... | collective-permute-start | bytes 1572872 | tf_op jit(solution)/shard_map/ppermute | solution.py:308
  77.7 21.8 %copy-start.5 = (bf16[8,256,128]{2,1,0:T(8,128)(2,1)S(1)}, bf16[8,256,128]{2,1,0:T(8,128)(2,1)}, u32[]{:S(2)}) copy-start(bf16[8,256,128]{2,1,0:T(8,128)(2,1)} %get-tuple-element.32) | copy-start | bytes 1572868
  100.5 38.9 %copy-start.4 = (bf16[8,512,128]{2,1,0:T(8,128)(2,1)S(1)}, bf16[8,512,128]{2,1,0:T(8,128)(2,1)}, u32[]{:S(2)}) copy-start(bf16[8,512,128]{2,1,0:T(8,128)(2,1)} %get-tuple-element.37) | copy-start | bytes 3145732
  100.5 40.3 %all-to-all-start.3 = ((bf16[8,1024,128]{2,1,0:T(8,128)(2,1)}), bf16[8,1024,128]{2,1,0:T(8,128)(2,1)S(1)}, u32[]{:S(2)}, u32[]{:S(2)}) async-start(bf16[8,1024,128]{2,1,0:T(8,128)(2,1)} %fusion), calls=%async_computation.3 | async-start | bytes 4194304 | tf_op jit(solution)/shard_map/all_to_all | solution.py:302
  104.2 29.1 %collective-permute-start.6 = (bf16[8,512,128]{2,1,0:T(8,128)(2,1)}, bf16[8,512,128]{2,1,0:T(8,128)(2,1)S(1)}, u32[]{:S(2)}, u32[]{:S(2)}) collective-permute-start(bf16[8,512,128]{2,1,0:T(8,128)(2,1)} %get-tuple-element.40), channel_id=1, source_target_pairs={{8,0},{16,8},{24,16},{32,24},{40,32},{48,40},{56,48},{64,56},{72,6... | collective-permute-start | bytes 3145736 | tf_op jit(solution)/shard_map/ppermute | solution.py:308
  109.9 29.5 %collective-permute-start.7 = (bf16[8,512,128]{2,1,0:T(8,128)(2,1)}, bf16[8,512,128]{2,1,0:T(8,128)(2,1)S(1)}, u32[]{:S(2)}, u32[]{:S(2)}) collective-permute-start(bf16[8,512,128]{2,1,0:T(8,128)(2,1)} %get-tuple-element.41), channel_id=1, source_target_pairs={{0,8},{8,16},{16,24},{24,32},{32,40},{40,48},{48,56},{56,64},{64,7... | collective-permute-start | bytes 3145736 | tf_op jit(solution)/shard_map/ppermute | solution.py:308
  140.8 20.4 %all-to-all-start.4 = ((bf16[8,512,128]{2,1,0:T(8,128)(2,1)}), bf16[8,512,128]{2,1,0:T(8,128)(2,1)S(1)}, u32[]{:S(2)}, u32[]{:S(2)}) async-start(bf16[8,512,128]{2,1,0:T(8,128)(2,1)} %add_convert_fusion), calls=%async_computation.4 | async-start | bytes 2097152 | tf_op jit(solution)/shard_map/all_to_all | solution.py:302

commit v5 on v4

--- a/solution.py
+++ b/solution.py
@@ -25,6 +25,7 @@
 REACH = 2
 VMEM_BYTES = 56 * 1024 * 1024
 PLACE_BYTES = 8 * 1024 * 1024
+PACK_BYTES = 12 * 1024 * 1024
 
 
 def dot(lhs, rhs, dims):
@@ -71,7 +72,7 @@
             jax.ShapeDtypeStruct((peers, len(plan) * rows + more, DH), arrays[0].dtype)
             for plan, more in zip(plans, extra)
         ],
-        compiler_params=pltpu.CompilerParams(vmem_limit_bytes=VMEM_BYTES),
+        compiler_params=pltpu.CompilerParams(vmem_limit_bytes=PACK_BYTES),
         name="pack",
     )(*arrays, *stamps)
 

time: 163 us -> 165 us (1.012)
  Pallas kernels: 44.4 us -> 41.2 us
  local copies, waits for them, and re-layouts: 1.24 us -> 4.15 us
  waiting for transfers between devices: 64.9 us -> 67 us
    pallas_call x2, Pallas kernels: 6.13 us -> 2.9 us  [pack(): pl.pallas_call(functools.partial(pack_kernel, peers, width // DH // peers...]
    unnamed x12 -> x24, local copies, waits for them, and re-layouts: 0.02 us -> 2.95 us
    all_to_all x5, waiting for transfers between devices: 35.4 us -> 37.3 us  [swap(): return lax.all_to_all(value, GROUP, split_axis=0, concat_axis=0, tiled=True)]
  transfers between devices with their start and end apart: 13 -> 13, of which waited for: 7 -> 7; matrix products, arithmetic and copies ran while one was open for 2% -> 2% of each run, Pallas kernels for 25% -> 24%
where the time goes in v5:
time: 165 us; the launch traced here: 164 us
  waiting for transfers between devices  67 us (41%)
  starting transfers between devices  48.6 us (29%)
  Pallas kernels  41.2 us (25%)
  local copies, waits for them, and re-layouts  4.15 us (3%)
  other arithmetic  2.42 us (1%)
    all_to_all x5, waiting for transfers between devices, swap(): return lax.all_to_all(value, GROUP, split_axis=0, concat_axis=0, tiled=True)  37.3 us
    pallas_call x2, Pallas kernels, attend(): pl.pallas_call(functools.partial(attend_kernel, per, size, fresh), grid=(...  34.7 us
    ppermute x8, waiting for transfers between devices, shifted(): lax.ppermute(value, 'col', [(at, at + steps) for at in range(first, last)])  29.7 us
    ppermute x8, starting transfers between devices, shifted(): lax.ppermute(value, 'col', [(at, at + steps) for at in range(first, last)])  27.7 us
    all_to_all x5, starting transfers between devices, swap(): return lax.all_to_all(value, GROUP, split_axis=0, concat_axis=0, tiled=True)  20.8 us
    pallas_call x3, Pallas kernels, place(): pl.pallas_call(functools.partial(place_kernel, peers, heads, chunk, offse...  3.68 us
  transfers between devices with their start and end apart: 13, of which 7 were waited for; matrix products, arithmetic and copies ran while one was open for 2% of the time, Pallas kernels for 24%

profile of v5, /device:TPU:96, one launch (start us, length us, event | category | flops | bytes accessed | tf_op | source)
XLA Modules:
  0.0 164.4 jit_solution(18201449407141597551)
XLA Ops:
  0.6 0.0 copy-start
  0.6 1.1 copy-done
  1.8 0.0 copy-start.2
  1.8 1.1 copy-done.2
  2.9 0.0 copy-start.6
  2.9 0.7 copy-done.6
  3.6 0.0 copy-start.1
  3.6 0.0 copy-start.3
  3.6 0.0 copy-start.4
  3.6 0.0 copy-start.5
  3.6 0.9 pack.2
  4.5 4.6 %all-to-all-start = ((bf16[8,272,128]{2,1,0:T(8,128)(2,1)}), bf16[8,272,128]{2,1,0:T(8,128)(2,1)}, u32[]{:S(2)}, u32[]{:S(2)}) async-start(bf16[8,272,128]{2,1,0:T(8,128)(2,1)} %pack.2), calls=%async_computation | async-start | bytes 1114112 | tf_op jit(solution)/shard_map/all_to_all | solution.py:303
  9.1 0.0 copy-done.1
  9.1 0.0 copy-done.3
  9.1 0.0 copy-done.4
  9.1 0.0 copy-done.5
  9.1 2.0 %pack.3 = (bf16[8,768,128]{2,1,0:T(8,128)(2,1)}, bf16[8,512,128]{2,1,0:T(8,128)(2,1)}) custom-call(bf16[128,3072]{1,0:T(8,128)(2,1)S(1)} %copy-done.1, bf16[128,3072]{1,0:T(8,128)(2,1)S(1)} %copy-done.3, bf16[128,3072]{1,0:T(8,128)(2,1)S(1)} %copy-done.4, bf16[128,3072]{1,0:T(8,128)(2,1)S(1)} %copy-done.5), custom_call_target="tpu_custom_call" | custom-call | tf_op jit(solution)/shard_map/pack/pallas_call | solution.py:67
  11.1 8.8 %all-to-all-done.stamps_own.own_ref = bf16[8,272,128]{2,1,0:T(8,128)(2,1)} async-done(((bf16[8,272,128]{2,1,0:T(8,128)(2,1)}), bf16[8,272,128]{2,1,0:T(8,128)(2,1)}, u32[]{:S(2)}, u32[]{:S(2)}) %all-to-all-start) | async-done | bytes 557088 | tf_op jit(solution)/shard_map/all_to_all | solution.py:303
  19.9 3.6 %all-to-all-start.1 = ((bf16[8,768,128]{2,1,0:T(8,128)(2,1)}), bf16[8,768,128]{2,1,0:T(8,128)(2,1)S(1)}, u32[]{:S(2)}, u32[]{:S(2)}) async-start(bf16[8,768,128]{2,1,0:T(8,128)(2,1)} %get-tuple-element.27), calls=%async_computation.1 | async-start | bytes 3145728 | tf_op jit(solution)/shard_map/all_to_all | solution.py:303
  23.5 4.5 %collective-permute-start.1 = (bf16[8,272,128]{2,1,0:T(8,128)(2,1)}, bf16[8,272,128]{2,1,0:T(8,128)(2,1)S(1)}, u32[]{:S(2)}, u32[]{:S(2)}) collective-permute-start(bf16[8,272,128]{2,1,0:T(8,128)(2,1)} %all-to-all-done.stamps_own.own_ref), channel_id=1, source_target_pairs={{8,0},{16,8},{24,16},{32,24},{40,32},{48,40},{56,48},{64,56},{72,6... | collective-permute-start | bytes 1671176 | tf_op jit(solution)/shard_map/ppermute | solution.py:309
  28.0 1.9 %collective-permute-start = (bf16[8,272,128]{2,1,0:T(8,128)(2,1)}, bf16[8,272,128]{2,1,0:T(8,128)(2,1)S(1)}, u32[]{:S(2)}, u32[]{:S(2)}) collective-permute-start(bf16[8,272,128]{2,1,0:T(8,128)(2,1)} %all-to-all-done.stamps_own.own_ref), channel_id=1, source_target_pairs={{0,8},{8,16},{16,24},{24,32},{32,40},{40,48},{48,56},{56,64},{64,7... | collective-permute-start | bytes 1671176 | tf_op jit(solution)/shard_map/ppermute | solution.py:309
  30.0 15.0 %all-to-all-done.1.qg_ref.own_ref = bf16[8,768,128]{2,1,0:T(8,128)(2,1)S(1)} async-done(((bf16[8,768,128]{2,1,0:T(8,128)(2,1)}), bf16[8,768,128]{2,1,0:T(8,128)(2,1)S(1)}, u32[]{:S(2)}, u32[]{:S(2)}) %all-to-all-start.1) | async-done | bytes 1572896 | tf_op jit(solution)/shard_map/all_to_all | solution.py:303
  45.0 0.0 copy-start.7
  45.0 1.2 slice.4
  46.2 0.0 collective-permute-done.1.stamps_right.right_ref
  46.2 0.0 copy-start.8
  46.2 0.7 collective-permute-done.stamps_left.left_ref
  46.9 0.0 copy-start.9
  46.9 3.9 %collective-permute-start.3 = (bf16[8,512,128]{2,1,0:T(8,128)(2,1)}, bf16[8,512,128]{2,1,0:T(8,128)(2,1)}, u32[]{:S(2)}, u32[]{:S(2)}) collective-permute-start(bf16[8,512,128]{2,1,0:T(8,128)(2,1)} %slice.4), channel_id=1, source_target_pairs={{8,0},{16,8},{24,16},{32,24},{40,32},{48,40},{56,48},{64,56},{72,6... | collective-permute-start | bytes 3145736 | tf_op jit(solution)/shard_map/ppermute | solution.py:309
  50.7 2.0 %collective-permute-start.2 = (bf16[8,512,128]{2,1,0:T(8,128)(2,1)}, bf16[8,512,128]{2,1,0:T(8,128)(2,1)}, u32[]{:S(2)}, u32[]{:S(2)}) collective-permute-start(bf16[8,512,128]{2,1,0:T(8,128)(2,1)} %slice.4), channel_id=1, source_target_pairs={{0,8},{8,16},{16,24},{24,32},{32,40},{40,48},{48,56},{56,64},{64,7... | collective-permute-start | bytes 3145736 | tf_op jit(solution)/shard_map/ppermute | solution.py:309
  52.7 0.0 copy-done.7
  52.7 4.5 %all-to-all-start.2 = ((bf16[8,512,128]{2,1,0:T(8,128)(2,1)}), bf16[8,512,128]{2,1,0:T(8,128)(2,1)}, u32[]{:S(2)}, u32[]{:S(2)}) async-start(bf16[8,512,128]{2,1,0:T(8,128)(2,1)} %get-tuple-element.28), calls=%async_computation.2 | async-start | bytes 2097152 | tf_op jit(solution)/shard_map/all_to_all | solution.py:303
  57.2 0.0 copy-done.8
  57.2 0.0 copy-done.9
  57.2 12.9 %attend.2 = (bf16[8,1024,128]{2,1,0:T(8,128)(2,1)}, bf16[8,256,128]{2,1,0:T(8,128)(2,1)}, bf16[8,256,128]{2,1,0:T(8,128)(2,1)}, bf16[8,256,128]{2,1,0:T(8,128)(2,1)}) custom-call(bf16[8,272,128]{2,1,0:T(8,128)(2,1)} %copy-done.9, bf16[8,272,128]{2,1,0:T(8,128)(2,1)} %all-to-all-done.stamps_own.own_ref, bf16[8,272,128]{2,1,0:T(8,128)(2,1)} %copy-done.8, ...), custom_call_target="tpu_custom_call" | custom-call | flops 1 | bytes 1 | tf_op jit(solution)/shard_map/attend/pallas_call | solution.py:274
  70.1 5.8 %collective-permute-start.4 = (bf16[8,256,128]{2,1,0:T(8,128)(2,1)}, bf16[8,256,128]{2,1,0:T(8,128)(2,1)S(1)}, u32[]{:S(2)}, u32[]{:S(2)}) collective-permute-start(bf16[8,256,128]{2,1,0:T(8,128)(2,1)} %get-tuple-element.33), channel_id=1, source_target_pairs={{8,0},{16,8},{24,16},{32,24},{40,32},{48,40},{56,48},{64,56},{72,6... | collective-permute-start | bytes 1572872 | tf_op jit(solution)/shard_map/ppermute | solution.py:309
  75.9 2.1 %collective-permute-start.5 = (bf16[8,256,128]{2,1,0:T(8,128)(2,1)}, bf16[8,256,128]{2,1,0:T(8,128)(2,1)S(1)}, u32[]{:S(2)}, u32[]{:S(2)}) collective-permute-start(bf16[8,256,128]{2,1,0:T(8,128)(2,1)} %get-tuple-element.34), channel_id=1, source_target_pairs={{0,8},{8,16},{16,24},{24,32},{32,40},{40,48},{48,56},{56,64},{64,7... | collective-permute-start | bytes 1572872 | tf_op jit(solution)/shard_map/ppermute | solution.py:309
  78.0 0.0 all-to-all-done.2.qg_ref
  78.0 0.0 collective-permute-done.3.right_ref
  78.0 1.5 collective-permute-done.2.left_ref
  79.5 0.0 copy-start.11
  79.5 21.8 %attend.3 = (bf16[8,1024,128]{2,1,0:T(8,128)(2,1)}, bf16[8,512,128]{2,1,0:T(8,128)(2,1)}, bf16[8,512,128]{2,1,0:T(8,128)(2,1)}, bf16[8,512,128]{2,1,0:T(8,128)(2,1)}) custom-call(bf16[8,272,128]{2,1,0:T(8,128)(2,1)} %copy-done.9, bf16[8,272,128]{2,1,0:T(8,128)(2,1)} %all-to-all-done.stamps_own.own_ref, ...), custom_call_target="tpu_custom_call", output_to_operand_aliasing={{0}: (7, {})} | custom-call | flops 1 | bytes 1 | tf_op jit(solution)/shard_map/attend/pallas_call | solution.py:274
  101.3 0.0 collective-permute-done.4
  101.3 0.0 collective-permute-done.5
  101.3 0.0 copy-done.11
  101.3 1.0 fusion
  102.3 0.0 copy-start.10
  102.3 3.7 %all-to-all-start.3 = ((bf16[8,1024,128]{2,1,0:T(8,128)(2,1)}), bf16[8,1024,128]{2,1,0:T(8,128)(2,1)S(1)}, u32[]{:S(2)}, u32[]{:S(2)}) async-start(bf16[8,1024,128]{2,1,0:T(8,128)(2,1)} %fusion), calls=%async_computation.3 | async-start | bytes 4194304 | tf_op jit(solution)/shard_map/all_to_all | solution.py:303
  106.0 5.6 %collective-permute-start.6 = (bf16[8,512,128]{2,1,0:T(8,128)(2,1)}, bf16[8,512,128]{2,1,0:T(8,128)(2,1)S(1)}, u32[]{:S(2)}, u32[]{:S(2)}) collective-permute-start(bf16[8,512,128]{2,1,0:T(8,128)(2,1)} %get-tuple-element.40), channel_id=1, source_target_pairs={{8,0},{16,8},{24,16},{32,24},{40,32},{48,40},{56,48},{64,56},{72,6... | collective-permute-start | bytes 3145736 | tf_op jit(solution)/shard_map/ppermute | solution.py:309
  111.7 1.9 %collective-permute-start.7 = (bf16[8,512,128]{2,1,0:T(8,128)(2,1)}, bf16[8,512,128]{2,1,0:T(8,128)(2,1)S(1)}, u32[]{:S(2)}, u32[]{:S(2)}) collective-permute-start(bf16[8,512,128]{2,1,0:T(8,128)(2,1)} %get-tuple-element.41), channel_id=1, source_target_pairs={{0,8},{8,16},{16,24},{24,32},{32,40},{40,48},{48,56},{56,64},{64,7... | collective-permute-start | bytes 3145736 | tf_op jit(solution)/shard_map/ppermute | solution.py:309
  113.6 21.5 %collective-permute-done.6 = bf16[8,512,128]{2,1,0:T(8,128)(2,1)S(1)} collective-permute-done((bf16[8,512,128]{2,1,0:T(8,128)(2,1)}, bf16[8,512,128]{2,1,0:T(8,128)(2,1)S(1)}, u32[]{:S(2)}, u32[]{:S(2)}) %collective-permute-start.6) | collective-permute-done | bytes 1048608 | tf_op jit(solution)/shard_map/ppermute | solution.py:309
  135.1 6.1 %collective-permute-done.7 = bf16[8,512,128]{2,1,0:T(8,128)(2,1)S(1)} collective-permute-done((bf16[8,512,128]{2,1,0:T(8,128)(2,1)}, bf16[8,512,128]{2,1,0:T(8,128)(2,1)S(1)}, u32[]{:S(2)}, u32[]{:S(2)}) %collective-permute-start.7) | collective-permute-done | bytes 1048608 | tf_op jit(solution)/shard_map/ppermute | solution.py:309
  141.2 0.0 copy-done.10
  141.2 1.4 add_convert_fusion
  142.6 0.0 all-to-all-done.3.piece
  142.6 4.4 %all-to-all-start.4 = ((bf16[8,512,128]{2,1,0:T(8,128)(2,1)}), bf16[8,512,128]{2,1,0:T(8,128)(2,1)S(1)}, u32[]{:S(2)}, u32[]{:S(2)}) async-start(bf16[8,512,128]{2,1,0:T(8,128)(2,1)} %add_convert_fusion), calls=%async_computation.4 | async-start | bytes 2097152 | tf_op jit(solution)/shard_map/all_to_all | solution.py:303
  147.0 0.9 place.4
  148.0 1.5 place.3
  149.5 13.5 %all-to-all-done.4.piece = bf16[8,512,128]{2,1,0:T(8,128)(2,1)S(1)} async-done(((bf16[8,512,128]{2,1,0:T(8,128)(2,1)}), bf16[8,512,128]{2,1,0:T(8,128)(2,1)S(1)}, u32[]{:S(2)}, u32[]{:S(2)}) %all-to-all-start.4) | async-done | bytes 1048608 | tf_op jit(solution)/shard_map/all_to_all | solution.py:303
  163.0 1.2 place.5
Async XLA Ops:
  0.6 1.1 copy-start
  1.8 1.1 copy-start.2
  2.9 0.7 copy-start.6
  3.6 5.5 %copy-start.1 = (bf16[128,3072]{1,0:T(8,128)(2,1)S(1)}, bf16[128,3072]{1,0:T(8,128)(2,1)}, u32[]{:S(2)}) copy-start(bf16[128,3072]{1,0:T(8,128)(2,1)} %refs_0_.3) | copy-start | bytes 2359300
  3.6 5.5 %copy-start.3 = (bf16[128,3072]{1,0:T(8,128)(2,1)S(1)}, bf16[128,3072]{1,0:T(8,128)(2,1)}, u32[]{:S(2)}) copy-start(bf16[128,3072]{1,0:T(8,128)(2,1)} %refs_1_.3) | copy-start | bytes 2359300
  3.6 5.6 %copy-start.4 = (bf16[128,3072]{1,0:T(8,128)(2,1)S(1)}, bf16[128,3072]{1,0:T(8,128)(2,1)}, u32[]{:S(2)}) copy-start(bf16[128,3072]{1,0:T(8,128)(2,1)} %refs_2_.1) | copy-start | bytes 2359300
  3.6 5.6 %copy-start.5 = (bf16[128,3072]{1,0:T(8,128)(2,1)S(1)}, bf16[128,3072]{1,0:T(8,128)(2,1)}, u32[]{:S(2)}) copy-start(bf16[128,3072]{1,0:T(8,128)(2,1)} %refs_3_.1) | copy-start | bytes 2359300
  4.5 15.4 %all-to-all-start = ((bf16[8,272,128]{2,1,0:T(8,128)(2,1)}), bf16[8,272,128]{2,1,0:T(8,128)(2,1)}, u32[]{:S(2)}, u32[]{:S(2)}) async-start(bf16[8,272,128]{2,1,0:T(8,128)(2,1)} %pack.2), calls=%async_computation | async-start | bytes 1114112 | tf_op jit(solution)/shard_map/all_to_all | solution.py:303
  19.9 25.1 %all-to-all-start.1 = ((bf16[8,768,128]{2,1,0:T(8,128)(2,1)}), bf16[8,768,128]{2,1,0:T(8,128)(2,1)S(1)}, u32[]{:S(2)}, u32[]{:S(2)}) async-start(bf16[8,768,128]{2,1,0:T(8,128)(2,1)} %get-tuple-element.27), calls=%async_computation.1 | async-start | bytes 3145728 | tf_op jit(solution)/shard_map/all_to_all | solution.py:303
  23.5 22.7 %collective-permute-start.1 = (bf16[8,272,128]{2,1,0:T(8,128)(2,1)}, bf16[8,272,128]{2,1,0:T(8,128)(2,1)S(1)}, u32[]{:S(2)}, u32[]{:S(2)}) collective-permute-start(bf16[8,272,128]{2,1,0:T(8,128)(2,1)} %all-to-all-done.stamps_own.own_ref), channel_id=1, source_target_pairs={{8,0},{16,8},{24,16},{32,24},{40,32},{48,40},{56,48},{64,56},{72,6... | collective-permute-start | bytes 1671176 | tf_op jit(solution)/shard_map/ppermute | solution.py:309
  28.0 18.8 %collective-permute-start = (bf16[8,272,128]{2,1,0:T(8,128)(2,1)}, bf16[8,272,128]{2,1,0:T(8,128)(2,1)S(1)}, u32[]{:S(2)}, u32[]{:S(2)}) collective-permute-start(bf16[8,272,128]{2,1,0:T(8,128)(2,1)} %all-to-all-done.stamps_own.own_ref), channel_id=1, source_target_pairs={{0,8},{8,16},{16,24},{24,32},{32,40},{40,48},{48,56},{56,64},{64,7... | collective-permute-start | bytes 1671176 | tf_op jit(solution)/shard_map/ppermute | solution.py:309
  45.0 7.7 %copy-start.7 = (bf16[8,768,128]{2,1,0:T(8,128)(2,1)}, bf16[8,768,128]{2,1,0:T(8,128)(2,1)S(1)}, u32[]{:S(2)}) copy-start(bf16[8,768,128]{2,1,0:T(8,128)(2,1)S(1)} %all-to-all-done.1.qg_ref.own_ref) | copy-start | bytes 4718596
  46.2 11.0 %copy-start.8 = (bf16[8,272,128]{2,1,0:T(8,128)(2,1)}, bf16[8,272,128]{2,1,0:T(8,128)(2,1)S(1)}, u32[]{:S(2)}) copy-start(bf16[8,272,128]{2,1,0:T(8,128)(2,1)S(1)} %collective-permute-done.1.stamps_right.right_ref) | copy-start | bytes 1671172
  46.9 10.3 %copy-start.9 = (bf16[8,272,128]{2,1,0:T(8,128)(2,1)}, bf16[8,272,128]{2,1,0:T(8,128)(2,1)S(1)}, u32[]{:S(2)}) copy-start(bf16[8,272,128]{2,1,0:T(8,128)(2,1)S(1)} %collective-permute-done.stamps_left.left_ref) | copy-start | bytes 1671172
  46.9 31.1 %collective-permute-start.3 = (bf16[8,512,128]{2,1,0:T(8,128)(2,1)}, bf16[8,512,128]{2,1,0:T(8,128)(2,1)}, u32[]{:S(2)}, u32[]{:S(2)}) collective-permute-start(bf16[8,512,128]{2,1,0:T(8,128)(2,1)} %slice.4), channel_id=1, source_target_pairs={{8,0},{16,8},{24,16},{32,24},{40,32},{48,40},{56,48},{64,56},{72,6... | collective-permute-start | bytes 3145736 | tf_op jit(solution)/shard_map/ppermute | solution.py:309
  50.7 28.7 %collective-permute-start.2 = (bf16[8,512,128]{2,1,0:T(8,128)(2,1)}, bf16[8,512,128]{2,1,0:T(8,128)(2,1)}, u32[]{:S(2)}, u32[]{:S(2)}) collective-permute-start(bf16[8,512,128]{2,1,0:T(8,128)(2,1)} %slice.4), channel_id=1, source_target_pairs={{0,8},{8,16},{16,24},{24,32},{32,40},{40,48},{48,56},{56,64},{64,7... | collective-permute-start | bytes 3145736 | tf_op jit(solution)/shard_map/ppermute | solution.py:309
  52.7 25.3 %all-to-all-start.2 = ((bf16[8,512,128]{2,1,0:T(8,128)(2,1)}), bf16[8,512,128]{2,1,0:T(8,128)(2,1)}, u32[]{:S(2)}, u32[]{:S(2)}) async-start(bf16[8,512,128]{2,1,0:T(8,128)(2,1)} %get-tuple-element.28), calls=%async_computation.2 | async-start | bytes 2097152 | tf_op jit(solution)/shard_map/all_to_all | solution.py:303
  70.1 31.2 %collective-permute-start.4 = (bf16[8,256,128]{2,1,0:T(8,128)(2,1)}, bf16[8,256,128]{2,1,0:T(8,128)(2,1)S(1)}, u32[]{:S(2)}, u32[]{:S(2)}) collective-permute-start(bf16[8,256,128]{2,1,0:T(8,128)(2,1)} %get-tuple-element.33), channel_id=1, source_target_pairs={{8,0},{16,8},{24,16},{32,24},{40,32},{48,40},{56,48},{64,56},{72,6... | collective-permute-start | bytes 1572872 | tf_op jit(solution)/shard_map/ppermute | solution.py:309
  75.9 25.4 %collective-permute-start.5 = (bf16[8,256,128]{2,1,0:T(8,128)(2,1)}, bf16[8,256,128]{2,1,0:T(8,128)(2,1)S(1)}, u32[]{:S(2)}, u32[]{:S(2)}) collective-permute-start(bf16[8,256,128]{2,1,0:T(8,128)(2,1)} %get-tuple-element.34), channel_id=1, source_target_pairs={{0,8},{8,16},{16,24},{24,32},{32,40},{40,48},{48,56},{56,64},{64,7... | collective-permute-start | bytes 1572872 | tf_op jit(solution)/shard_map/ppermute | solution.py:309
  79.5 21.8 %copy-start.11 = (bf16[8,256,128]{2,1,0:T(8,128)(2,1)S(1)}, bf16[8,256,128]{2,1,0:T(8,128)(2,1)}, u32[]{:S(2)}) copy-start(bf16[8,256,128]{2,1,0:T(8,128)(2,1)} %get-tuple-element.32) | copy-start | bytes 1572868
  102.3 38.9 %copy-start.10 = (bf16[8,512,128]{2,1,0:T(8,128)(2,1)S(1)}, bf16[8,512,128]{2,1,0:T(8,128)(2,1)}, u32[]{:S(2)}) copy-start(bf16[8,512,128]{2,1,0:T(8,128)(2,1)} %get-tuple-element.37) | copy-start | bytes 3145732
  102.3 40.3 %all-to-all-start.3 = ((bf16[8,1024,128]{2,1,0:T(8,128)(2,1)}), bf16[8,1024,128]{2,1,0:T(8,128)(2,1)S(1)}, u32[]{:S(2)}, u32[]{:S(2)}) async-start(bf16[8,1024,128]{2,1,0:T(8,128)(2,1)} %fusion), calls=%async_computation.3 | async-start | bytes 4194304 | tf_op jit(solution)/shard_map/all_to_all | solution.py:303
  106.0 29.0 %collective-permute-start.6 = (bf16[8,512,128]{2,1,0:T(8,128)(2,1)}, bf16[8,512,128]{2,1,0:T(8,128)(2,1)S(1)}, u32[]{:S(2)}, u32[]{:S(2)}) collective-permute-start(bf16[8,512,128]{2,1,0:T(8,128)(2,1)} %get-tuple-element.40), channel_id=1, source_target_pairs={{8,0},{16,8},{24,16},{32,24},{40,32},{48,40},{56,48},{64,56},{72,6... | collective-permute-start | bytes 3145736 | tf_op jit(solution)/shard_map/ppermute | solution.py:309
  111.7 29.5 %collective-permute-start.7 = (bf16[8,512,128]{2,1,0:T(8,128)(2,1)}, bf16[8,512,128]{2,1,0:T(8,128)(2,1)S(1)}, u32[]{:S(2)}, u32[]{:S(2)}) collective-permute-start(bf16[8,512,128]{2,1,0:T(8,128)(2,1)} %get-tuple-element.41), channel_id=1, source_target_pairs={{0,8},{8,16},{16,24},{24,32},{32,40},{40,48},{48,56},{56,64},{64,7... | collective-permute-start | bytes 3145736 | tf_op jit(solution)/shard_map/ppermute | solution.py:309
  142.6 20.4 %all-to-all-start.4 = ((bf16[8,512,128]{2,1,0:T(8,128)(2,1)}), bf16[8,512,128]{2,1,0:T(8,128)(2,1)S(1)}, u32[]{:S(2)}, u32[]{:S(2)}) async-start(bf16[8,512,128]{2,1,0:T(8,128)(2,1)} %add_convert_fusion), calls=%async_computation.4 | async-start | bytes 2097152 | tf_op jit(solution)/shard_map/all_to_all | solution.py:303
